TPU v7x, 256 devices: a whole 4x4x8 slice. The times are simulated.
256 devices in a mesh: tm: 8 (over y, z_lo), space: 32 (over z_hi, x, core).
Axes of the slice: x: 4, y: 4, z: 8 (z_hi: 4, z_lo: 2; z = z_hi * 2 + z_lo), core: 2. Of those that a mesh axis runs over, the one named last changes fastest.
Arguments:
- latents: float32 [256, 16, 128], P('space', 'tm'), may hold values from -16 to 16
- timestep: int32 [1], replicated, may hold values from 0 to 979
- alpha_table: float32 [1000], replicated, may hold values from 0.02 to 1, as said below
- norm_gain: float32 [2, 4096], replicated, may hold values from 0.1 to 1.9
- head_gain: float32 [4, 128], replicated, may hold values from 0.1 to 1.9
- embed_weight: bfloat16 [128, 4096], replicated, may hold values from -4 to 4
- space_project: bfloat16 [3, 4096, 4096], P(None, None, 'space'), may hold values from -0.09375 to 0.09375
- space_output: bfloat16 [4096, 4096], P('space'), may hold values from -0.375 to 0.375
- time_project: bfloat16 [3, 4096, 4096], P(None, None, 'space'), may hold values from -0.09375 to 0.09375
- time_output: bfloat16 [4096, 4096], P('space'), may hold values from -0.375 to 0.375
- noise_weight: bfloat16 [4096, 128], replicated, may hold values from -0.09375 to 0.09375
Outputs:
- predicted_noise: float32 [256, 16, 128], P('space', 'tm')
- latents_next: float32 [256, 16, 128], P('space', 'tm')
Inputs may be any that keep to these rules, and one draw needn't show every extreme that they name: `alpha_table`: strictly falling from each entry to the next.
All inputs are finite; a program needn't handle non-finite values.
Results may differ from a plain program's by a relative error of at most 0.024.
Values may be sent and summed in bfloat16 or wider, within the bound.
No kernel may reach another device: no remote copies, remote signals or barrier semaphores. Data moves between devices by JAX's collectives and lax.ppermute only.
A program may use at most 64 MiB of HBM per device.

v0:
```python
import math

import jax
import jax.numpy as jnp
from jax import lax
from jax.sharding import PartitionSpec as P

STRIDE = 20


epsilon = 1e-06


def time_embedding(step_now, model_width):
    half_width = model_width // 2
    positions = jnp.arange(half_width, dtype=jnp.float32)
    frequency = jnp.exp(positions * (-math.log(10000.0) / half_width))
    angles = step_now.astype(jnp.float32) * frequency
    return jnp.concatenate([jnp.sin(angles), jnp.cos(angles)])


def norm_rows(values, gain_row):
    mean_square = jnp.mean(values * values, axis=-1, keepdims=True)
    return values * gain_row / jnp.sqrt(mean_square + epsilon)


def head_norm(values, gain_row, head_size):
    row_count = values.shape[0]
    reshaped = values.reshape(row_count, -1, head_size)
    return norm_rows(reshaped, gain_row).reshape(row_count, -1)


def project_rows(hidden, gain_row, weights, query_gain, key_gain, head_size):
    normed = norm_rows(hidden.astype(jnp.float32), gain_row).astype(jnp.bfloat16)
    query_proj = jnp.dot(normed, weights[0], preferred_element_type=jnp.float32)
    key_proj = jnp.dot(normed, weights[1], preferred_element_type=jnp.float32)
    value_proj = jnp.dot(normed, weights[2], preferred_element_type=jnp.float32)
    query_rows = head_norm(query_proj, query_gain, head_size).astype(jnp.bfloat16)
    key_rows = head_norm(key_proj, key_gain, head_size).astype(jnp.bfloat16)
    return (query_rows, key_rows, value_proj.astype(jnp.bfloat16))


def softmax_rows(scores):
    exp_scores = jnp.exp(scores)
    return exp_scores / jnp.sum(exp_scores, axis=-1, keepdims=True)


def attend_space(query_rows, key_rows, value_rows):
    head_size = query_rows.shape[-1]
    scores = jnp.einsum(
        "pfhd,qfhd->fhpq", query_rows, key_rows, preferred_element_type=jnp.float32
    ) / math.sqrt(head_size)
    weights = softmax_rows(scores).astype(jnp.bfloat16)
    return jnp.einsum(
        "fhpq,qfhd->pfhd", weights, value_rows, preferred_element_type=jnp.float32
    ).astype(jnp.bfloat16)


def attend_time(pieces):
    query_rows, key_rows, value_rows = pieces
    head_size = query_rows.shape[-1]
    scores = jnp.einsum(
        "pfhd,pghd->phfg", query_rows, key_rows, preferred_element_type=jnp.float32
    ) / math.sqrt(head_size)
    weights = softmax_rows(scores).astype(jnp.bfloat16)
    return jnp.einsum(
        "phfg,pghd->pfhd", weights, value_rows, preferred_element_type=jnp.float32
    ).astype(jnp.bfloat16)


def embed_rows(latent_in, embed_weight, embedding):
    patch_count, frame_count, channels = latent_in.shape
    flat_rows = latent_in.reshape(patch_count * frame_count, channels)
    mixed = jnp.dot(flat_rows, embed_weight, preferred_element_type=jnp.float32) + embedding
    return mixed.astype(jnp.bfloat16).reshape(patch_count, frame_count, -1)


def output_term(attended, weights):
    return jnp.dot(attended, weights, preferred_element_type=jnp.float32)


def body(
    latents,
    timestep,
    alpha_table,
    norm_gain,
    head_gain,
    embed_weight,
    space_project,
    space_output,
    time_project,
    time_output,
    noise_weight,
):
    patch_local, frame_local, channels = latents.shape
    model_width = embed_weight.shape[1]
    inner_width = space_output.shape[0]
    head_size = head_gain.shape[1]
    local_heads = inner_width // head_size
    step_now = timestep[0]
    positions = jnp.arange(alpha_table.shape[0], dtype=jnp.int32)
    alpha_now = jnp.sum(jnp.where(positions == step_now, alpha_table, 0.0))
    alpha_next = jnp.sum(jnp.where(positions == step_now + STRIDE, alpha_table, 0.0))
    embedding = time_embedding(step_now, model_width)
    latent_in = latents.astype(jnp.bfloat16)
    own_first = embed_rows(latent_in, embed_weight, embedding)
    all_first = lax.all_gather(own_first, "space", axis=0, tiled=True)
    patch_total = all_first.shape[0]
    shape_heads = (patch_total, frame_local, local_heads, head_size)
    query_rows, key_rows, value_rows = project_rows(
        all_first.reshape(-1, model_width),
        norm_gain[0],
        space_project,
        head_gain[0],
        head_gain[1],
        head_size,
    )
    attended = attend_space(
        query_rows.reshape(shape_heads),
        key_rows.reshape(shape_heads),
        value_rows.reshape(shape_heads),
    )
    own_rows = patch_local * frame_local
    spatial_out = lax.psum_scatter(
        output_term(attended.reshape(-1, inner_width), space_output).astype(jnp.bfloat16),
        "space",
        scatter_dimension=0,
        tiled=True,
    ).astype(jnp.float32)
    second = (own_first.reshape(own_rows, model_width).astype(jnp.float32) + spatial_out).astype(
        jnp.bfloat16
    )
    all_second = lax.all_gather(
        second.reshape(patch_local, frame_local, model_width), "space", axis=0, tiled=True
    )
    query_rows, key_rows, value_rows = project_rows(
        all_second.reshape(-1, model_width),
        norm_gain[1],
        time_project,
        head_gain[2],
        head_gain[3],
        head_size,
    )
    regrouped = attend_time(
        (
            lax.all_to_all(
                query_rows.reshape(shape_heads), "tm", split_axis=0, concat_axis=1, tiled=True
            ),
            lax.all_to_all(
                key_rows.reshape(shape_heads), "tm", split_axis=0, concat_axis=1, tiled=True
            ),
            lax.all_to_all(
                value_rows.reshape(shape_heads), "tm", split_axis=0, concat_axis=1, tiled=True
            ),
        )
    )
    attended_time = lax.all_to_all(
        regrouped, "tm", split_axis=1, concat_axis=0, tiled=True
    ).reshape(-1, inner_width)
    temporal_out = lax.psum_scatter(
        output_term(attended_time, time_output).astype(jnp.bfloat16),
        "space",
        scatter_dimension=0,
        tiled=True,
    ).astype(jnp.float32)
    third = (second.astype(jnp.float32) + temporal_out).astype(jnp.bfloat16)
    predicted_noise = jnp.dot(third, noise_weight, preferred_element_type=jnp.float32).reshape(
        patch_local, frame_local, channels
    )
    latents_next = (
        jnp.sqrt(alpha_next)
        * (latents - jnp.sqrt(1.0 - alpha_now) * predicted_noise)
        / jnp.sqrt(alpha_now)
        + jnp.sqrt(1.0 - alpha_next) * predicted_noise
    )
    return (predicted_noise, latents_next)


def solution(mesh):
    placed = (
        P("space", "tm", None),
        P(),
        P(),
        P(),
        P(),
        P(),
        P(None, None, "space"),
        P("space", None),
        P(None, None, "space"),
        P("space", None),
        P(),
    )
    return jax.shard_map(
        body,
        mesh=mesh,
        in_specs=placed,
        out_specs=(P("space", "tm", None), P("space", "tm", None)),
        check_vma=False,
    )
```

profile of v0, /device:TPU:8, one launch (start us, length us, event | category | flops | bytes accessed | tf_op | source)
XLA Modules:
  0.0 449.8 jit_solution(1207640740079779086)
XLA Ops:
  7.2 0.0 copy-start
  7.2 0.0 all-gather.3.cloned.1.call-start
  8.0 0.1 fusion.34
  8.0 0.7 convert_element_type.137
  8.7 1.5 fusion.6
  10.2 0.8 reshape.285
  11.0 0.0 all-gather.3.cloned.1.call-update
  11.0 0.0 reduce-scatter.3.cloned.1.call-start
  11.0 0.8 slice_bitcast_fusion
  11.9 0.9 fusion.40
  12.7 61.6 %all-gather.3.cloned.1.call-done = bf16[256,2,4096]{2,1,0:T(2,128)(2,1)} async-done(((bf16[8,2,4096]{2,1,0:T(2,128)(2,1)}), bf16[256,2,4096]{2,1,0:T(2,128)(2,1)}) %all-gather.3.cloned.1.call-update) | async-done | bytes 4194320 | tf_op jit(solution)/shard_map/all_gather | solution.py:107
  74.3 6.6 %fusion.2 = f32[256,2]{1,0:T(8,128)S(1)} fusion(bf16[256,2,4096]{2,1,0:T(2,128)(2,1)} %all-gather.3.cloned.1.call-done), kind=kLoop, calls=%fused_computation.6 | loop fusion | flops 6290944 | bytes 4196352 | tf_op jit(solution)/shard_map/reduce_sum | solution.py:23
  81.0 10.2 %fusion.1 = bf16[256,2,4096]{2,1,0:T(2,128)(2,1)} fusion(bf16[256,2,4096]{2,1,0:T(2,128)(2,1)} %all-gather.3.cloned.1.call-done, f32[256,2]{1,0:T(8,128)S(1)} %add_sqrt_fusion.1, f32[4096]{0:T(1024)S(1)} %bitcast.112), kind=kLoop, calls=%fused_computation.5 | loop fusion | flops 8388608 | bytes 8407040 | tf_op jit(solution)/shard_map/convert_element_type | solution.py:34
  91.2 7.2 %convert_element_type.143 = bf16[512,4096]{1,0:T(8,128)(2,1)} reshape(bf16[256,2,4096]{2,1,0:T(2,128)(2,1)} %fusion.1) | data formatting | bytes 8388608 | tf_op jit(solution)/shard_map/convert_element_type | solution.py:34
  98.4 4.0 multiply_reduce_fusion.3
  102.3 0.0 copy-done.2
  102.3 2.6 multiply_reduce_fusion.2
  104.9 2.5 convolution_convert_fusion.4
  107.4 0.1 divide_convert_fusion.5
  107.6 0.1 divide_convert_fusion.4
  107.7 0.2 fusion.7
  108.0 0.3 fusion.9
  108.2 0.1 copy.67
  108.4 0.0 copy-done
  108.4 3.2 convolution_convert_fusion.1
  111.5 0.0 reduce-scatter.3.cloned.1.call-update
  111.6 0.0 all-gather.5.cloned.1.call-start
  111.6 97.5 %reduce-scatter.3.cloned.1.call-done = bf16[16,4096]{1,0:T(8,128)(2,1)} async-done(((bf16[512,4096]{1,0:T(8,128)(2,1)}), bf16[16,4096]{1,0:T(8,128)(2,1)}) %reduce-scatter.3.cloned.1.call-update) | async-done | bytes 131088 | tf_op jit(solution)/shard_map/reduce_scatter | solution.py:124
  209.1 0.9 add_convert_fusion.1
  210.1 0.7 reshape.288
  210.8 0.0 all-gather.5.cloned.1.call-update
  210.8 58.7 %all-gather.5.cloned.1.call-done = bf16[256,2,4096]{2,1,0:T(2,128)(2,1)} async-done(((bf16[8,2,4096]{2,1,0:T(2,128)(2,1)}), bf16[256,2,4096]{2,1,0:T(2,128)(2,1)}) %all-gather.5.cloned.1.call-update) | async-done | bytes 4194320 | tf_op jit(solution)/shard_map/all_gather | solution.py:133
  269.5 6.6 %fusion.5 = f32[256,2]{1,0:T(8,128)S(1)} fusion(bf16[256,2,4096]{2,1,0:T(2,128)(2,1)} %all-gather.5.cloned.1.call-done), kind=kLoop, calls=%fused_computation.9 | loop fusion | flops 6290944 | bytes 4196352 | tf_op jit(solution)/shard_map/reduce_sum | solution.py:23
  276.1 10.2 %fusion.4 = bf16[256,2,4096]{2,1,0:T(2,128)(2,1)} fusion(bf16[256,2,4096]{2,1,0:T(2,128)(2,1)} %all-gather.5.cloned.1.call-done, f32[256,2]{1,0:T(8,128)S(1)} %add_sqrt_fusion, f32[4096]{0:T(1024)S(1)} %bitcast.111), kind=kLoop, calls=%fused_computation.8 | loop fusion | flops 8388608 | bytes 8407040 | tf_op jit(solution)/shard_map/convert_element_type | solution.py:34
  286.3 7.2 %convert_element_type.159 = bf16[512,4096]{1,0:T(8,128)(2,1)} reshape(bf16[256,2,4096]{2,1,0:T(2,128)(2,1)} %fusion.4) | data formatting | bytes 8388608 | tf_op jit(solution)/shard_map/convert_element_type | solution.py:34
  293.6 4.0 multiply_reduce_fusion
  297.5 2.6 multiply_reduce_fusion.1
  300.1 0.8 divide_convert_fusion.2
  300.9 4.8 %all-to-all-start.2 = ((bf16[256,2,1,128]{3,1,2,0:T(2,128)(2,1)}), bf16[256,2,1,128]{3,1,2,0:T(2,128)(2,1)S(1)}, u32[]{:S(2)}, u32[]{:S(2)}) async-start(bf16[256,2,1,128]{3,1,2,0:T(2,128)(2,1)} %bitcast.31), calls=%async_computation.3 | async-start | bytes 262144 | tf_op jit(solution)/shard_map/all_to_all | solution.py:149
  305.7 0.8 divide_convert_fusion.3
  306.5 4.3 all-to-all-done.2
  310.8 4.9 %all-to-all-start.1 = ((bf16[256,2,1,128]{3,1,2,0:T(2,128)(2,1)}), bf16[256,2,1,128]{3,1,2,0:T(2,128)(2,1)S(1)}, u32[]{:S(2)}, u32[]{:S(2)}) async-start(bf16[256,2,1,128]{3,1,2,0:T(2,128)(2,1)} %bitcast.24), calls=%async_computation.2 | async-start | bytes 262144 | tf_op jit(solution)/shard_map/all_to_all | solution.py:146
  315.7 4.5 convolution_convert_fusion.2
  320.2 0.6 all-to-all-done.1
  320.8 5.1 %all-to-all-start = ((bf16[256,2,1,128]{3,1,2,0:T(2,128)(2,1)}), bf16[256,2,1,128]{3,1,2,0:T(2,128)(2,1)S(1)}, u32[]{:S(2)}, u32[]{:S(2)}) async-start(bf16[256,2,1,128]{3,1,2,0:T(2,128)(2,1)} %bitcast.17), calls=%async_computation.1 | async-start | bytes 262144 | tf_op jit(solution)/shard_map/all_to_all | solution.py:152
  325.9 0.1 copy.75
  326.0 0.1 copy.73
  326.1 4.9 %all-to-all-done = bf16[256,2,1,128]{3,1,2,0:T(2,128)(2,1)S(1)} async-done(((bf16[256,2,1,128]{3,1,2,0:T(2,128)(2,1)}), bf16[256,2,1,128]{3,1,2,0:T(2,128)(2,1)S(1)}, u32[]{:S(2)}, u32[]{:S(2)}) %all-to-all-start) | async-done | bytes 131104 | tf_op jit(solution)/shard_map/all_to_all | solution.py:152
  331.0 0.1 copy.71
  331.1 0.2 fusion.8
  331.3 0.3 fusion.10
  331.6 9.1 %all_to_all.60 = bf16[32,16,1,128]{3,0,2,1:T(8,128)(2,1)S(1)} all-to-all(bf16[32,16,1,128]{3,0,2,1:T(8,128)(2,1)S(1)} %copy.77), channel_id=1, replica_groups=mesh['tm'=8,'space'=32] {'tm'}, dimensions={1} | all-to-all | bytes 262144 | tf_op jit(solution)/shard_map/all_to_all | solution.py:157
  340.7 0.1 copy.78
  340.8 0.0 copy-done.3
  340.8 0.0 copy-start.7
  340.8 0.0 copy-start.4
  340.8 3.2 convolution_convert_fusion
  344.0 0.0 reduce-scatter.5.cloned.1.call-update
  344.1 0.6 select_reduce_fusion
  347.4 94.1 %reduce-scatter.5.cloned.1.call-done = bf16[16,4096]{1,0:T(8,128)(2,1)} async-done(((bf16[512,4096]{1,0:T(8,128)(2,1)}), bf16[16,4096]{1,0:T(8,128)(2,1)}) %reduce-scatter.5.cloned.1.call-update) | async-done | bytes 131088 | tf_op jit(solution)/shard_map/reduce_scatter | solution.py:160
  441.5 0.0 copy-done.4
  441.5 1.1 fusion.28
  442.6 0.0 copy-done.6
  442.6 0.6 divide_add_fusion
  (17 shorter events, 0.2 us)
Async XLA Ops:
  7.2 101.2 %copy-start = (bf16[128,4096]{1,0:T(8,128)(2,1)S(1)}, bf16[128,4096]{1,0:T(8,128)(2,1)}, u32[]{:S(2)}) copy-start(bf16[128,4096]{1,0:T(8,128)(2,1)} %param.18) | copy-start | bytes 3145732
  7.2 67.2 %all-gather.3.cloned.1.call-start = ((), (), s32[]{:S(2)}) async-start(), calls=%async_computation.6 | async-start | bytes 4325376 | tf_op jit(solution)/shard_map/all_gather | solution.py:107
  11.0 198.1 %reduce-scatter.3.cloned.1.call-start = ((), (), s32[]{:S(2)}) async-start(), calls=%async_computation.7 | async-start | bytes 4325376 | tf_op jit(solution)/shard_map/reduce_scatter | solution.py:124
  98.4 4.0 copy-start.2
  111.6 158.0 %all-gather.5.cloned.1.call-start = ((), (), s32[]{:S(2)}) async-start(), calls=%async_computation.8 | async-start | bytes 4325376 | tf_op jit(solution)/shard_map/all_gather | solution.py:133
  293.6 4.0 copy-start.1
  300.9 9.9 %all-to-all-start.2 = ((bf16[256,2,1,128]{3,1,2,0:T(2,128)(2,1)}), bf16[256,2,1,128]{3,1,2,0:T(2,128)(2,1)S(1)}, u32[]{:S(2)}, u32[]{:S(2)}) async-start(bf16[256,2,1,128]{3,1,2,0:T(2,128)(2,1)} %bitcast.31), calls=%async_computation.3 | async-start | bytes 262144 | tf_op jit(solution)/shard_map/all_to_all | solution.py:149
  310.8 10.0 %all-to-all-start.1 = ((bf16[256,2,1,128]{3,1,2,0:T(2,128)(2,1)}), bf16[256,2,1,128]{3,1,2,0:T(2,128)(2,1)S(1)}, u32[]{:S(2)}, u32[]{:S(2)}) async-start(bf16[256,2,1,128]{3,1,2,0:T(2,128)(2,1)} %bitcast.24), calls=%async_computation.2 | async-start | bytes 262144 | tf_op jit(solution)/shard_map/all_to_all | solution.py:146
  315.7 25.1 %copy-start.3 = (bf16[128,4096]{1,0:T(8,128)(2,1)S(1)}, bf16[128,4096]{1,0:T(8,128)(2,1)}, u32[]{:S(2)}) copy-start(bf16[128,4096]{1,0:T(8,128)(2,1)} %param.20) | copy-start | bytes 3145732
  320.8 10.2 %all-to-all-start = ((bf16[256,2,1,128]{3,1,2,0:T(2,128)(2,1)}), bf16[256,2,1,128]{3,1,2,0:T(2,128)(2,1)S(1)}, u32[]{:S(2)}, u32[]{:S(2)}) async-start(bf16[256,2,1,128]{3,1,2,0:T(2,128)(2,1)} %bitcast.17), calls=%async_computation.1 | async-start | bytes 262144 | tf_op jit(solution)/shard_map/all_to_all | solution.py:152
  325.9 115.6 %reduce-scatter.5.cloned.1.call-start = ((), (), s32[]{:S(2)}) async-start(), calls=%async_computation.9 | async-start | bytes 4325376 | tf_op jit(solution)/shard_map/reduce_scatter | solution.py:160
  340.8 3.2 copy-start.7
  340.8 100.7 %copy-start.4 = (bf16[4096,128]{1,0:T(8,128)(2,1)S(1)}, bf16[4096,128]{1,0:T(8,128)(2,1)}, u32[]{:S(2)}) copy-start(bf16[4096,128]{1,0:T(8,128)(2,1)} %param.21) | copy-start | bytes 3145732
  344.0 98.6 %copy-start.6 = (f32[8,2,128]{2,1,0:T(2,128)S(1)}, f32[8,2,128]{2,1,0:T(2,128)}, u32[]{:S(2)}) copy-start(f32[8,2,128]{2,1,0:T(2,128)} %param.11) | copy-start | bytes 24580
  442.6 0.6 copy-start.5
Sparse Core Ops, SparseCore 0:
  11.1 63.1 all-gather.2
  111.7 97.3 reduce-scatter.2
  212.0 57.4 all-gather.4
  344.2 97.2 reduce-scatter.4
where the time goes:
time: 451 us; the launch traced here: 450 us
  waiting for transfers between devices  322 us (71%)
  other arithmetic  38.5 us (9%)
  matrix products  29.9 us (7%)
  local copies, waits for them, and re-layouts  18.2 us (4%)
  between operations  17.4 us (4%)
  starting transfers between devices  15 us (3%)
  blocking collectives  9.11 us (2%)
    reduce_scatter x1, waiting for transfers between devices, body(): lax.psum_scatter(output_term(attended.reshape(-1, inner_width), space_out...  97.5 us
    reduce_scatter x1, waiting for transfers between devices, body(): lax.psum_scatter(output_term(attended_time, time_output).astype(jnp.bfloa...  94.1 us
    all_gather x1, waiting for transfers between devices, body(): all_first = lax.all_gather(own_first, 'space', axis=0, tiled=True)  61.6 us
    all_gather x1, waiting for transfers between devices, body(): lax.all_gather(second.reshape(patch_local, frame_local, model_width), 'sp...  58.7 us
    convert_element_type x2, other arithmetic, project_rows(): norm_rows(hidden.astype(jnp.float32), gain_row).astype(jnp.bfloat16)  20.4 us
    convert_element_type x2, local copies, waits for them, and re-layouts, project_rows(): norm_rows(hidden.astype(jnp.float32), gain_row).astype(jnp.bfloat16)  14.4 us
    reduce_sum x2, other arithmetic, norm_rows(): mean_square = jnp.mean(values * values, axis=-1, keepdims=True)  13.1 us
    all_to_all x1, blocking collectives, body(): lax.all_to_all(regrouped, 'tm', split_axis=1, concat_axis=0, tiled=True)  9.11 us
  transfers between devices with their start and end apart: 7, of which 7 were waited for; matrix products, arithmetic and copies ran while one was open for 2% of the time, Pallas kernels for 0%

commit v1 on v0

v1 whole, which is shorter than its diff:
```python
import math

import jax
import jax.numpy as jnp
from jax import lax
from jax.experimental import pallas as pl
from jax.experimental.pallas import tpu as pltpu
from jax.sharding import Mesh, PartitionSpec as P

STRIDE = 20
EPS = 1e-06
NX = 4
HD = 128
BF = jnp.bfloat16
F32 = jnp.float32


def shift(value, axis, step):
    size = lax.axis_size(axis)
    return lax.ppermute(value, axis, [(i, (i + step) % size) for i in range(size)])


def time_embedding(step_now, model_width):
    half_width = model_width // 2
    positions = jnp.arange(half_width, dtype=F32)
    frequency = jnp.exp(positions * (-math.log(10000.0) / half_width))
    angles = step_now.astype(F32) * frequency
    return jnp.concatenate([jnp.sin(angles), jnp.cos(angles)])


def head_norm(values, gain):
    mean_square = jnp.mean(values * values, axis=-1, keepdims=True)
    return (values * gain * lax.rsqrt(mean_square + EPS)).astype(BF)


def weigh(scores, mask=None):
    e = jnp.exp(scores * (1.0 / math.sqrt(HD)))
    if mask is not None:
        e = jnp.where(mask, e, 0.0)
    return (e / jnp.sum(e, axis=-1, keepdims=True)).astype(BF)


def dot_t(a, b):
    return lax.dot_general(a, b, (((1,), (1,)), ((), ())), preferred_element_type=F32)


def dot(a, b):
    return jnp.dot(a, b, preferred_element_type=F32)


def space_kernel(lat_ref, embed_ref, temb_ref, fold_ref, gain_ref, out_ref):
    lat = lat_ref[...]
    width = embed_ref.shape[1]
    chunk = 512
    total = jnp.zeros((lat.shape[0], 128), F32)
    for start in range(0, width, chunk):
        first = dot(lat, embed_ref[:, start : start + chunk]) + temb_ref[:, start : start + chunk]
        first = first.astype(BF).astype(F32)
        square = first * first
        for lane in range(0, chunk, 128):
            total = total + square[:, lane : lane + 128]
    mean_square = jnp.sum(total, axis=-1, keepdims=True) * (1.0 / width)
    scale = lax.rsqrt(mean_square + EPS)
    bias = fold_ref[128:129, :].astype(F32) + fold_ref[129:130, :].astype(F32)
    proj = (dot(lat, fold_ref[:128, :]) + bias) * scale
    for head in range(2):
        base = head * 3 * HD
        query = head_norm(proj[:, base : base + HD], gain_ref[0:1, :])
        key = head_norm(proj[:, base + HD : base + 2 * HD], gain_ref[1:2, :])
        value = proj[:, base + 2 * HD : base + 3 * HD].astype(BF)
        weights = weigh(dot_t(query, key))
        out_ref[:, head * HD : (head + 1) * HD] = dot(weights, value).astype(BF)
    out_ref[:, 2 * HD :] = lat


def rolled(block, step):
    if step == 0:
        return block
    parts = []
    for z in range(NX):
        for x in range(NX):
            start = (z * NX + (x - step) % NX) * 16
            parts.append(block[start : start + 16, :])
    return jnp.concatenate(parts, axis=0)


def output_kernel(core_ref, a0, a1, a2, a3, own_ref, other_ref, out_ref, lhs_own, lhs_other):
    @pl.when(pl.program_id(0) == 0)
    def _():
        core = core_ref[0]
        for step, ref in enumerate((a0, a1, a2, a3)):
            own = ref[:, pl.ds(pl.multiple_of(core * HD, HD), HD)]
            other = ref[:, pl.ds(pl.multiple_of((1 - core) * HD, HD), HD)]
            lhs_own[:, step * HD : (step + 1) * HD] = rolled(own, step)
            lhs_other[:, step * HD : (step + 1) * HD] = rolled(other, step)

    width = own_ref.shape[2]
    own = own_ref[...].reshape(NX * HD, width)
    other = other_ref[...].reshape(NX * HD, width)
    out_ref[...] = (dot(lhs_own[...], own) + dot(lhs_other[...], other)).astype(BF)


def time_kernel(
    place_ref, x0, x1, x2, x3, gain_ref, own_ref, other_ref, head_gain_ref, att_ref, fold_ref, out_ref, proj, total
):
    step = pl.program_id(0)

    @pl.when(step == 0)
    def _():
        proj[...] = jnp.zeros_like(proj)
        total[...] = jnp.zeros_like(total)

    for k, ref in enumerate((x0, x1, x2, x3)):

        @pl.when(step == k)
        def _(k=k, ref=ref):
            rows = rolled(ref[...], k).astype(F32)
            square = rows * rows
            part = total[...]
            for lane in range(0, rows.shape[1], 128):
                part = part + square[:, lane : lane + 128]
            total[...] = part
            gained = (rows * gain_ref[0]).astype(BF)
            for part_index in range(3):
                for side, w_ref in enumerate((own_ref, other_ref)):
                    col = (side * 3 + part_index) * HD
                    proj[:, col : col + HD] += dot(gained, w_ref[part_index])

    @pl.when(step == NX - 1)
    def _():
        width = NX * x0.shape[1]
        mean_square = jnp.sum(total[...], axis=-1, keepdims=True) * (1.0 / width)
        scale = lax.rsqrt(mean_square + EPS)
        count = x0.shape[0]
        row_patch = lax.broadcasted_iota(jnp.int32, (count, count), 0) >> 4
        col_patch = lax.broadcasted_iota(jnp.int32, (count, count), 1) >> 4
        mask = row_patch == col_patch
        noise = dot(att_ref[...], fold_ref[: 2 * HD, :])
        for side in range(2):
            base = side * 3 * HD
            query = head_norm(proj[:, base : base + HD] * scale, head_gain_ref[2:3, :])
            key = head_norm(proj[:, base + HD : base + 2 * HD] * scale, head_gain_ref[3:4, :])
            value = (proj[:, base + 2 * HD : base + 3 * HD] * scale).astype(BF)
            weights = weigh(dot_t(query, key), mask)
            attended = dot(weights, value).astype(BF)
            start = (2 + side) * HD
            noise = noise + dot(attended, fold_ref[start : start + HD, :])
        out_ref[...] = noise


def body(
    latents,
    timestep,
    alpha_table,
    norm_gain,
    head_gain,
    embed_weight,
    space_project,
    space_output,
    time_project,
    time_output,
    noise_weight,
):
    width = embed_weight.shape[1]
    block = width // NX
    core = lax.axis_index("c")
    place = lax.axis_index("x")
    step_now = timestep[0]
    positions = jnp.arange(alpha_table.shape[0], dtype=jnp.int32)
    alpha_now = jnp.sum(jnp.where(positions == step_now, alpha_table, 0.0))
    alpha_next = jnp.sum(jnp.where(positions == step_now + STRIDE, alpha_table, 0.0))
    temb = time_embedding(step_now, width)[None, :]

    def in_order(own, other):
        first = jnp.where(core == 0, own, other)
        second = jnp.where(core == 0, other, own)
        return jnp.stack([first, second])

    lat_bf = latents.astype(BF)
    mine = jnp.where(core == 0, lat_bf[:, 0], lat_bf[:, 1])
    theirs = jnp.where(core == 0, lat_bf[:, 1], lat_bf[:, 0])
    piece = in_order(mine, shift(theirs, "c", 1)).transpose(1, 0, 2).reshape(16, HD)
    piece = jnp.stack([piece] + [shift(piece, "x", -d) for d in range(1, NX)])
    piece = jnp.stack([piece] + [shift(piece, "zh", -d) for d in range(1, NX)])
    lat_rows = piece.reshape(16, 16, HD).transpose(1, 0, 2).reshape(256, HD)

    scaled = temb * norm_gain[0:1]
    high = scaled.astype(BF)
    low = (scaled - high.astype(F32)).astype(BF)
    lhs = jnp.concatenate(
        [(embed_weight.astype(F32) * norm_gain[0:1]).astype(BF), high, low, jnp.zeros((14, width), BF)]
    )
    fold = jnp.concatenate([dot(lhs, space_project[i]) for i in range(3)], axis=1)
    bias = fold[128:129] + fold[129:130]
    bias_high = bias.astype(BF)
    bias_low = (bias - bias_high.astype(F32)).astype(BF)
    fold = jnp.concatenate([fold[:128].astype(BF), bias_high, bias_low, jnp.zeros((14, 3 * HD), BF)])
    fold = in_order(fold, shift(fold, "c", 1)).transpose(1, 0, 2).reshape(144, 6 * HD)

    time_other = shift(time_project, "c", 1)
    pieces = [
        lax.dynamic_slice(space_output, (0, ((place - d) % NX) * block), (HD, block)) for d in range(NX)
    ]
    out_own = jnp.stack([pieces[0]] + [shift(pieces[d], "x", -d) for d in range(1, NX)])
    out_other = shift(out_own, "c", 1)
    noise_fold = jnp.concatenate(
        [dot(space_output, noise_weight).astype(BF), dot(time_output, noise_weight).astype(BF)]
    )
    noise_other = shift(noise_fold, "c", 1)
    noise_fold = jnp.concatenate(
        [in_order(noise_fold[:HD], noise_other[:HD]).reshape(2 * HD, HD), noise_fold[HD:], noise_other[HD:]]
    )

    attended = pl.pallas_call(
        space_kernel,
        out_shape=jax.ShapeDtypeStruct((256, 3 * HD), BF),
        compiler_params=pltpu.CompilerParams(vmem_limit_bytes=32 * 1024 * 1024),
        name="space_attention",
    )(lat_rows, embed_weight, temb, fold, head_gain)

    regrouped = lax.all_to_all(attended, ("y", "zl", "c"), split_axis=0, concat_axis=0, tiled=True)
    regrouped = regrouped.reshape(16, 16, 3 * HD).transpose(1, 0, 2).reshape(256, 3 * HD)
    att = regrouped[:, : 2 * HD]
    lat_block = regrouped[:64, 2 * HD :]
    att_all = [att] + [shift(att, "x", -d) for d in range(1, NX)]

    tiles = 4
    tile = block // tiles
    partial = pl.pallas_call(
        output_kernel,
        out_shape=jax.ShapeDtypeStruct((256, block), BF),
        grid_spec=pltpu.PrefetchScalarGridSpec(
            num_scalar_prefetch=1,
            grid=(tiles,),
            in_specs=[pl.BlockSpec((256, 2 * HD), lambda i, s: (0, 0))] * NX
            + [pl.BlockSpec((NX, HD, tile), lambda i, s: (0, 0, i))] * 2,
            out_specs=pl.BlockSpec((256, tile), lambda i, s: (0, i)),
            scratch_shapes=[pltpu.VMEM((256, NX * HD), BF)] * 2,
        ),
        compiler_params=pltpu.CompilerParams(vmem_limit_bytes=32 * 1024 * 1024),
        name="space_output",
    )(core.reshape(1).astype(jnp.int32), *att_all, out_own, out_other)

    own_cols = lax.dynamic_slice(embed_weight, (0, place * block), (HD, block))
    own_temb = lax.dynamic_slice(temb, (0, place * block), (1, block))
    first_block = (dot(lat_block, own_cols) + own_temb).astype(BF).astype(F32)
    spatial_out = partial[:64].astype(F32)
    for d in range(1, NX):
        spatial_out = spatial_out + shift(partial[64 * d : 64 * (d + 1)], "zh", d).astype(F32)
    second = (first_block + spatial_out).astype(BF)
    second = jnp.concatenate([second] + [shift(second, "zh", -d) for d in range(1, NX)])
    second_all = [second] + [shift(second, "x", -d) for d in range(1, NX)]

    weight_spec = pl.BlockSpec((3, block, HD), lambda i, s: (0, (s[0] + i) % NX, 0))
    partial = pl.pallas_call(
        time_kernel,
        out_shape=jax.ShapeDtypeStruct((256, HD), F32),
        grid_spec=pltpu.PrefetchScalarGridSpec(
            num_scalar_prefetch=1,
            grid=(NX,),
            in_specs=[pl.BlockSpec((256, block), lambda i, s: (0, 0))] * NX
            + [
                pl.BlockSpec((1, 1, block), lambda i, s: ((s[0] + i) % NX, 0, 0)),
                weight_spec,
                weight_spec,
                pl.BlockSpec((4, HD), lambda i, s: (0, 0)),
                pl.BlockSpec((256, 2 * HD), lambda i, s: (0, 0)),
                pl.BlockSpec((4 * HD, HD), lambda i, s: (0, 0)),
            ],
            out_specs=pl.BlockSpec((256, HD), lambda i, s: (0, 0)),
            scratch_shapes=[pltpu.VMEM((256, 6 * HD), F32), pltpu.VMEM((256, HD), F32)],
        ),
        compiler_params=pltpu.CompilerParams(vmem_limit_bytes=40 * 1024 * 1024),
        name="time_attention",
    )(
        place.reshape(1).astype(jnp.int32),
        *second_all,
        norm_gain[1].reshape(NX, 1, block),
        time_project,
        time_other,
        head_gain,
        att,
        noise_fold,
    )

    noise = partial[:64]
    for d in range(1, NX):
        noise = noise + shift(partial[64 * d : 64 * (d + 1)], "zh", d)
    total = noise[:16]
    for d in range(1, NX):
        total = total + shift(noise[16 * d : 16 * (d + 1)], "x", d)
    total = lax.all_to_all(total, ("y", "zl"), split_axis=0, concat_axis=0, tiled=True)

    own_first = (dot(lat_bf.reshape(16, HD), embed_weight) + temb).astype(BF)
    predicted_noise = (total + dot(own_first, noise_weight)).reshape(latents.shape)
    latents_next = (
        jnp.sqrt(alpha_next)
        * (latents - jnp.sqrt(1.0 - alpha_now) * predicted_noise)
        / jnp.sqrt(alpha_now)
        + jnp.sqrt(1.0 - alpha_next) * predicted_noise
    )
    return (predicted_noise, latents_next)


def solution(mesh):
    fine = Mesh(mesh.devices.reshape(4, 2, 4, 4, 2), ("y", "zl", "zh", "x", "c"))
    space = ("zh", "x", "c")
    rows = P(space, ("y", "zl"), None)
    placed = (
        rows,
        P(),
        P(),
        P(),
        P(),
        P(),
        P(None, None, space),
        P(space, None),
        P(None, None, space),
        P(space, None),
        P(),
    )
    return jax.shard_map(
        body,
        mesh=fine,
        in_specs=placed,
        out_specs=(rows, rows),
        check_vma=False,
    )
```

time: 451 us -> 168 us (0.37)
  waiting for transfers between devices: 322 us -> 55.9 us
  starting transfers between devices: 15 us -> 70.4 us
  other arithmetic: 38.5 us -> 5.92 us
  matrix products: 29.9 us -> 5.71 us
  local copies, waits for them, and re-layouts: 18.2 us -> 3.55 us
  between operations: 17.4 us -> 4.57 us
  Pallas kernels: 0 us -> 11.4 us
    reduce_scatter x2 -> x0, waiting for transfers between devices: 192 us -> none  [the longest x1 97.5 us: body(): lax.psum_scatter(output_term(attended.reshape(-1, inner_width), space_out...]
    all_gather x2 -> x0, waiting for transfers between devices: 120 us -> none  [the longest x1 61.6 us: body(): all_first = lax.all_gather(own_first, 'space', axis=0, tiled=True)]
    ppermute x0 -> x32, starting transfers between devices: none -> 59.2 us  [shift(): lax.ppermute(value, axis, [(i, (i + step) % size) for i in range(size)])]
    ppermute x0 -> x32, waiting for transfers between devices: none -> 54.5 us  [shift(): lax.ppermute(value, axis, [(i, (i + step) % size) for i in range(size)])]
    dot_general x14 -> x7, matrix products: 29.9 us -> 5.71 us  [dot(): return jnp.dot(a, b, preferred_element_type=F32)]
    convert_element_type x8 -> x5, other arithmetic: 23.9 us -> 1.77 us  [the longest x1 1.48 us: body(): high = scaled.astype(BF)]
    convert_element_type x4 -> x1, local copies, waits for them, and re-layouts: 14.6 us -> 0.01 us  [body(): lat_bf = latents.astype(BF)]
    reduce_sum x2 -> x0, other arithmetic: 13.1 us -> none  [norm_rows(): mean_square = jnp.mean(values * values, axis=-1, keepdims=True)]
  transfers between devices with their start and end apart: 7 -> 33, of which waited for: 7 -> 22; matrix products, arithmetic and copies ran while one was open for 2% -> 8% of each run, Pallas kernels for 0% -> 3%
where the time goes in v1:
time: 168 us; the launch traced here: 167 us
  starting transfers between devices  70.4 us (42%)
  waiting for transfers between devices  55.9 us (33%)
  Pallas kernels  11.4 us (7%)
  blocking collectives  10 us (6%)
  other arithmetic  5.92 us (4%)
  matrix products  5.71 us (3%)
  between operations  4.57 us (3%)
  local copies, waits for them, and re-layouts  3.55 us (2%)
    ppermute x32, starting transfers between devices, shift(): lax.ppermute(value, axis, [(i, (i + step) % size) for i in range(size)])  59.2 us
    ppermute x32, waiting for transfers between devices, shift(): lax.ppermute(value, axis, [(i, (i + step) % size) for i in range(size)])  54.5 us
    all_to_all x1, starting transfers between devices, body(): lax.all_to_all(total, ('y', 'zl'), split_axis=0, concat_axis=0, tiled=True)  11.2 us
    all_to_all x1, blocking collectives, body(): lax.all_to_all(attended, ('y', 'zl', 'c'), split_axis=0, concat_axis=0, t...  10 us
    pallas_call x1, Pallas kernels, body(): pl.pallas_call(time_kernel, out_shape=jax.ShapeDtypeStruct((256, HD), F32...  6.81 us
    dot_general x7, matrix products, dot(): return jnp.dot(a, b, preferred_element_type=F32)  5.71 us
  transfers between devices with their start and end apart: 33, of which 22 were waited for; matrix products, arithmetic and copies ran while one was open for 8% of the time, Pallas kernels for 3%

profile of v1, /device:TPU:8, one launch (start us, length us, event | category | flops | bytes accessed | tf_op | source)
XLA Modules:
  0.0 167.5 jit_solution(17497242573584346445)
XLA Ops:
  0.7 0.8 copy.46
  1.7 2.1 %dynamic-slice_bitcast_fusion = (bf16[1,128,1024]{2,1,0:T(8,128)(2,1)S(1)}, bf16[128,1024]{1,0:T(8,128)(2,1)}, bf16[128,1024]{1,0:T(8,128)(2,1)}, bf16[128,1024]{1,0:T(8,128)(2,1)}) fusion(bf16[128,4096]{1,0:T(8,128)(2,1)} %param.18, s32[]{:T(128)S(6)} %select_n.107, s32[]{:T(128)S(6)} %select_n.111, s32[]{:T(128)S(6)} %select_n.109, s32[]{:T(128)S(6)} %select_n.113), kind=kLoop, calls=%fused_computation.22 | loop fusion | bytes 2097168 | tf_op jit(solution)/shard_map/stack | solution.py:204
  3.8 3.0 %collective-permute-start.12 = (bf16[128,1024]{1,0:T(8,128)(2,1)}, bf16[128,1024]{1,0:T(8,128)(2,1)}, u32[]{:S(2)}, u32[]{:S(2)}) collective-permute-start(bf16[128,1024]{1,0:T(8,128)(2,1)} %get-tuple-element.7), channel_id=1, source_target_pairs={{0,4},{2,6},{4,0},{6,2},{1,5},{3,7},{5,1},{7,3},{8,12},{10,14},{12... | collective-permute-start | bytes 786440 | tf_op jit(solution)/shard_map/ppermute | solution.py:20
  6.8 1.1 collective-permute-start.11
  8.8 1.5 multiply_convert_fusion.1
  10.5 1.9 %fusion.6 = f32[144,128]{1,0:T(8,128)S(1)} fusion(bf16[3,4096,128]{2,1,0:T(8,128)(2,1)} %param.17, bf16[1,4096]{1,0:T(2,128)(2,1)S(1)} %get-tuple-element.22, bf16[1,4096]{1,0:T(2,128)(2,1)S(1)} %get-tuple-element.21, bf16[128,4096]{1,0:T(8,128)(2,1)S(1)} %multiply_convert_fusion, bf16[144]{0:T(256)(128)(2,1)S(1)} %pad.27.clone), kind=kOutput, calls=%fused_computation.13 | convolution fusion | flops 155713536 | bytes 2187552 | tf_op jit(solution)/shard_map/dot_general | solution.py:48
  12.7 0.5 fusion.4
  13.2 0.5 fusion.8
  13.8 1.0 collective-permute-start.3
  14.8 0.7 collective-permute-start.2
  15.5 2.5 %collective-permute-start.1 = (bf16[16,128]{1,0:T(8,128)(2,1)S(1)}, bf16[16,128]{1,0:T(8,128)(2,1)S(1)}, u32[]{:S(2)}, u32[]{:S(2)}) collective-permute-start(bf16[16,128]{1,0:T(8,128)(2,1)S(1)} %bitcast.102), channel_id=1, source_target_pairs={{0,6},{2,0},{4,2},{6,4},{1,7},{3,1},{5,3},{7,5},{8,14},{10,8},{12,... | collective-permute-start | bytes 12296 | tf_op jit(solution)/shard_map/ppermute | solution.py:20
  18.1 0.7 collective-permute-done.3
  18.7 1.2 collective-permute-done.2
  20.1 7.2 %collective-permute-start.5 = (bf16[4,16,128]{2,1,0:T(8,128)(2,1)S(1)}, bf16[4,16,128]{2,1,0:T(8,128)(2,1)S(1)}, u32[]{:S(2)}, u32[]{:S(2)}) collective-permute-start(bf16[4,16,128]{2,1,0:T(8,128)(2,1)S(1)} %get-tuple-element.29), channel_id=1, source_target_pairs={{0,16},{8,24},{16,0},{24,8},{1,17},{9,25},{17,1},{25,9},{2,18},{10... | collective-permute-start | bytes 49160 | tf_op jit(solution)/shard_map/ppermute | solution.py:20
  27.3 1.7 %collective-permute-done.5 = bf16[4,16,128]{2,1,0:T(8,128)(2,1)S(1)} collective-permute-done((bf16[4,16,128]{2,1,0:T(8,128)(2,1)S(1)}, bf16[4,16,128]{2,1,0:T(8,128)(2,1)S(1)}, u32[]{:S(2)}, u32[]{:S(2)}) %collective-permute-start.5) | collective-permute-done | bytes 16416 | tf_op jit(solution)/shard_map/ppermute | solution.py:20
  29.0 2.9 %collective-permute-done.4 = bf16[4,16,128]{2,1,0:T(8,128)(2,1)S(1)} collective-permute-done((bf16[4,16,128]{2,1,0:T(8,128)(2,1)S(1)}, bf16[4,16,128]{2,1,0:T(8,128)(2,1)S(1)}, u32[]{:S(2)}, u32[]{:S(2)}) %collective-permute-start.4) | collective-permute-done | bytes 16416 | tf_op jit(solution)/shard_map/ppermute | solution.py:20
  31.9 2.7 %collective-permute-start.6 = (bf16[4,16,128]{2,1,0:T(8,128)(2,1)S(1)}, bf16[4,16,128]{2,1,0:T(8,128)(2,1)S(1)}, u32[]{:S(2)}, u32[]{:S(2)}) collective-permute-start(bf16[4,16,128]{2,1,0:T(8,128)(2,1)S(1)} %get-tuple-element.29), channel_id=1, source_target_pairs={{0,8},{8,16},{16,24},{24,0},{1,9},{9,17},{17,25},{25,1},{2,10},{10... | collective-permute-start | bytes 49160 | tf_op jit(solution)/shard_map/ppermute | solution.py:20
  34.7 3.2 %collective-permute-done.6 = bf16[4,16,128]{2,1,0:T(8,128)(2,1)S(1)} collective-permute-done((bf16[4,16,128]{2,1,0:T(8,128)(2,1)S(1)}, bf16[4,16,128]{2,1,0:T(8,128)(2,1)S(1)}, u32[]{:S(2)}, u32[]{:S(2)}) %collective-permute-start.6) | collective-permute-done | bytes 16416 | tf_op jit(solution)/shard_map/ppermute | solution.py:20
  38.0 1.2 pad_maximum_fusion.own_ref
  39.2 0.8 collective-permute-start.14
  40.2 1.4 space_attention.1
  41.6 10.0 %all_to_all.21 = bf16[16,16,384]{2,1,0:T(8,128)(2,1)S(1)} all-to-all(bf16[16,16,384]{2,1,0:T(8,128)(2,1)S(1)} %bitcast.83), channel_id=1, replica_groups=mesh['y'=4,'zl'=2,'zh'=4,'x'=4,'c'=2] {'y','zl','c'}, dimensions={0} | all-to-all | bytes 393216 | tf_op jit(solution)/shard_map/all_to_all | solution.py:221
  51.7 1.6 collective-permute-start.10
  53.3 2.7 %collective-permute-start.9 = (bf16[256,256]{1,0:T(8,128)(2,1)S(1)}, bf16[256,256]{1,0:T(8,128)(2,1)S(1)}, u32[]{:S(2)}, u32[]{:S(2)}) collective-permute-start(bf16[256,256]{1,0:T(8,128)(2,1)S(1)} %slice.112.a0.att_ref), channel_id=1, source_target_pairs={{0,4},{2,6},{4,0},{6,2},{1,5},{3,7},{5,1},{7,3},{8,12},{10,14},{12... | collective-permute-start | bytes 393224 | tf_op jit(solution)/shard_map/ppermute | solution.py:20
  56.0 0.5 collective-permute-start.8
  56.6 1.1 convolution_convert_fusion.1
  57.6 0.7 fusion.22
  58.3 0.8 collective-permute-done.10.a3
  59.1 3.8 %collective-permute-done.9.a2 = bf16[256,256]{1,0:T(8,128)(2,1)S(1)} collective-permute-done((bf16[256,256]{1,0:T(8,128)(2,1)S(1)}, bf16[256,256]{1,0:T(8,128)(2,1)S(1)}, u32[]{:S(2)}, u32[]{:S(2)}) %collective-permute-start.9) | collective-permute-done | bytes 131104 | tf_op jit(solution)/shard_map/ppermute | solution.py:20
  63.0 3.2 %space_output.1 = bf16[256,1024]{1,0:T(8,128)(2,1)S(1)} custom-call(s32[1]{0:T(128)} %bitcast.30.core_ref, bf16[256,256]{1,0:T(8,128)(2,1)S(1)} %slice.112.a0.att_ref, bf16[256,256]{1,0:T(8,128)(2,1)} %collective-permute-done.8.a1, bf16[256,256]{1,0:T(8,128)(2,1)S(1)} %collective-permute-done.9.a2, bf16[256,256]{1,0:T(8,128)(2,1)S(1)} %collective-permute-done.10.a3, ...), custom_call_target="tpu_custom_call" | custom-call | tf_op jit(solution)/shard_map/space_output/pallas_call | solution.py:229
  66.3 1.5 collective-permute-start.15
  67.9 2.7 %collective-permute-start.17 = (bf16[64,1024]{1,0:T(8,128)(2,1)S(1)}, bf16[64,1024]{1,0:T(8,128)(2,1)S(1)}, u32[]{:S(2)}, u32[]{:S(2)}) collective-permute-start(bf16[64,1024]{1,0:T(8,128)(2,1)S(1)} %get-tuple-element.11), channel_id=1, source_target_pairs={{0,24},{8,0},{16,8},{24,16},{1,25},{9,1},{17,9},{25,17},{2,26},{10... | collective-permute-start | bytes 393224 | tf_op jit(solution)/shard_map/ppermute | solution.py:20
  70.5 3.2 %collective-permute-start.16 = (bf16[64,1024]{1,0:T(8,128)(2,1)S(1)}, bf16[64,1024]{1,0:T(8,128)(2,1)S(1)}, u32[]{:S(2)}, u32[]{:S(2)}) collective-permute-start(bf16[64,1024]{1,0:T(8,128)(2,1)S(1)} %get-tuple-element.12), channel_id=1, source_target_pairs={{0,16},{8,24},{16,0},{24,8},{1,17},{9,25},{17,1},{25,9},{2,18},{10... | collective-permute-start | bytes 393224 | tf_op jit(solution)/shard_map/ppermute | solution.py:20
  73.7 0.9 fusion.2
  74.6 1.7 %collective-permute-done.15 = bf16[64,1024]{1,0:T(8,128)(2,1)S(1)} collective-permute-done((bf16[64,1024]{1,0:T(8,128)(2,1)S(1)}, bf16[64,1024]{1,0:T(8,128)(2,1)S(1)}, u32[]{:S(2)}, u32[]{:S(2)}) %collective-permute-start.15) | collective-permute-done | bytes 131104 | tf_op jit(solution)/shard_map/ppermute | solution.py:20
  76.3 2.9 %collective-permute-done.17 = bf16[64,1024]{1,0:T(8,128)(2,1)S(1)} collective-permute-done((bf16[64,1024]{1,0:T(8,128)(2,1)S(1)}, bf16[64,1024]{1,0:T(8,128)(2,1)S(1)}, u32[]{:S(2)}, u32[]{:S(2)}) %collective-permute-start.17) | collective-permute-done | bytes 131104 | tf_op jit(solution)/shard_map/ppermute | solution.py:20
  79.2 2.1 %collective-permute-done.16 = bf16[64,1024]{1,0:T(8,128)(2,1)S(1)} collective-permute-done((bf16[64,1024]{1,0:T(8,128)(2,1)S(1)}, bf16[64,1024]{1,0:T(8,128)(2,1)S(1)}, u32[]{:S(2)}, u32[]{:S(2)}) %collective-permute-start.16) | collective-permute-done | bytes 131104 | tf_op jit(solution)/shard_map/ppermute | solution.py:20
  81.4 1.9 %collective-permute-start.20 = (bf16[64,1024]{1,0:T(8,128)(2,1)S(1)}, bf16[64,1024]{1,0:T(8,128)(2,1)S(1)}, u32[]{:S(2)}, u32[]{:S(2)}) collective-permute-start(bf16[64,1024]{1,0:T(8,128)(2,1)S(1)} %add_convert_fusion), channel_id=1, source_target_pairs={{0,8},{8,16},{16,24},{24,0},{1,9},{9,17},{17,25},{25,1},{2,10},{10... | collective-permute-start | bytes 393224 | tf_op jit(solution)/shard_map/ppermute | solution.py:20
  83.3 3.3 %collective-permute-start.19 = (bf16[64,1024]{1,0:T(8,128)(2,1)S(1)}, bf16[64,1024]{1,0:T(8,128)(2,1)S(1)}, u32[]{:S(2)}, u32[]{:S(2)}) collective-permute-start(bf16[64,1024]{1,0:T(8,128)(2,1)S(1)} %add_convert_fusion), channel_id=1, source_target_pairs={{0,16},{8,24},{16,0},{24,8},{1,17},{9,25},{17,1},{25,9},{2,18},{10... | collective-permute-start | bytes 393224 | tf_op jit(solution)/shard_map/ppermute | solution.py:20
  86.6 2.4 %collective-permute-start.18 = (bf16[64,1024]{1,0:T(8,128)(2,1)S(1)}, bf16[64,1024]{1,0:T(8,128)(2,1)S(1)}, u32[]{:S(2)}, u32[]{:S(2)}) collective-permute-start(bf16[64,1024]{1,0:T(8,128)(2,1)S(1)} %add_convert_fusion), channel_id=1, source_target_pairs={{0,24},{8,0},{16,8},{24,16},{1,25},{9,1},{17,9},{25,17},{2,26},{10... | collective-permute-start | bytes 393224 | tf_op jit(solution)/shard_map/ppermute | solution.py:20
  89.0 0.4 convolution_convert_fusion
  89.5 4.9 %collective-permute-done.20 = bf16[64,1024]{1,0:T(8,128)(2,1)S(1)} collective-permute-done((bf16[64,1024]{1,0:T(8,128)(2,1)S(1)}, bf16[64,1024]{1,0:T(8,128)(2,1)S(1)}, u32[]{:S(2)}, u32[]{:S(2)}) %collective-permute-start.20) | collective-permute-done | bytes 131104 | tf_op jit(solution)/shard_map/ppermute | solution.py:20
  94.4 6.4 %collective-permute-done.18 = bf16[64,1024]{1,0:T(8,128)(2,1)S(1)} collective-permute-done((bf16[64,1024]{1,0:T(8,128)(2,1)S(1)}, bf16[64,1024]{1,0:T(8,128)(2,1)S(1)}, u32[]{:S(2)}, u32[]{:S(2)}) %collective-permute-start.18) | collective-permute-done | bytes 131104 | tf_op jit(solution)/shard_map/ppermute | solution.py:20
  100.9 0.7 collective-permute-start.23
  101.6 2.7 %collective-permute-start.22 = (bf16[256,1024]{1,0:T(8,128)(2,1)S(1)}, bf16[256,1024]{1,0:T(8,128)(2,1)S(1)}, u32[]{:S(2)}, u32[]{:S(2)}) collective-permute-start(bf16[256,1024]{1,0:T(8,128)(2,1)S(1)} %pad_maximum_fusion.1.x0), channel_id=1, source_target_pairs={{0,4},{2,6},{4,0},{6,2},{1,5},{3,7},{5,1},{7,3},{8,12},{10,14},{12... | collective-permute-start | bytes 1572872 | tf_op jit(solution)/shard_map/ppermute | solution.py:20
  104.3 1.3 collective-permute-start.21
  106.0 1.2 collective-permute-done.25
  107.3 6.3 %collective-permute-done.23.x3 = bf16[256,1024]{1,0:T(8,128)(2,1)S(1)} collective-permute-done((bf16[256,1024]{1,0:T(8,128)(2,1)S(1)}, bf16[256,1024]{1,0:T(8,128)(2,1)S(1)}, u32[]{:S(2)}, u32[]{:S(2)}) %collective-permute-start.23) | collective-permute-done | bytes 524320 | tf_op jit(solution)/shard_map/ppermute | solution.py:20
  113.5 5.6 %collective-permute-done.22.x2 = bf16[256,1024]{1,0:T(8,128)(2,1)S(1)} collective-permute-done((bf16[256,1024]{1,0:T(8,128)(2,1)S(1)}, bf16[256,1024]{1,0:T(8,128)(2,1)S(1)}, u32[]{:S(2)}, u32[]{:S(2)}) %collective-permute-start.22) | collective-permute-done | bytes 524320 | tf_op jit(solution)/shard_map/ppermute | solution.py:20
  119.2 6.8 %time_attention.1 = f32[256,128]{1,0:T(8,128)S(1)} custom-call(s32[1]{0:T(128)} %bitcast.place_ref, bf16[256,1024]{1,0:T(8,128)(2,1)S(1)} %pad_maximum_fusion.1.x0, bf16[256,1024]{1,0:T(8,128)(2,1)S(1)} %collective-permute-done.21.x1, bf16[256,1024]{1,0:T(8,128)(2,1)S(1)} %collective-permute-done.22.x2, bf16[256,1024]{1,0:T(8,128)(2,1)S(1)} %collective-permute-done.23.x3, ...), custom_call_target="tpu_custom_call" | custom-call | tf_op jit(solution)/shard_map/time_attention/pallas_call | solution.py:255
  126.0 7.6 %collective-permute-start.26 = (f32[64,128]{1,0:T(8,128)S(1)}, f32[64,128]{1,0:T(8,128)S(1)}, u32[]{:S(2)}, u32[]{:S(2)}) collective-permute-start(f32[64,128]{1,0:T(8,128)S(1)} %get-tuple-element.15), channel_id=1, source_target_pairs={{0,8},{8,16},{16,24},{24,0},{1,9},{9,17},{17,25},{25,1},{2,10},{10... | collective-permute-start | bytes 98312 | tf_op jit(solution)/shard_map/ppermute | solution.py:20
  133.6 3.7 %collective-permute-start.27 = (f32[64,128]{1,0:T(8,128)S(1)}, f32[64,128]{1,0:T(8,128)S(1)}, u32[]{:S(2)}, u32[]{:S(2)}) collective-permute-start(f32[64,128]{1,0:T(8,128)S(1)} %get-tuple-element.17), channel_id=1, source_target_pairs={{0,16},{8,24},{16,0},{24,8},{1,17},{9,25},{17,1},{25,9},{2,18},{10... | collective-permute-start | bytes 98312 | tf_op jit(solution)/shard_map/ppermute | solution.py:20
  137.3 1.1 collective-permute-done.28
  138.4 3.3 %collective-permute-done.27 = f32[64,128]{1,0:T(8,128)S(1)} collective-permute-done((f32[64,128]{1,0:T(8,128)S(1)}, f32[64,128]{1,0:T(8,128)S(1)}, u32[]{:S(2)}, u32[]{:S(2)}) %collective-permute-start.27) | collective-permute-done | bytes 32800 | tf_op jit(solution)/shard_map/ppermute | solution.py:20
  141.8 0.7 collective-permute-start.29
  142.5 2.6 %collective-permute-start.31 = (f32[16,128]{1,0:T(8,128)S(1)}, f32[16,128]{1,0:T(8,128)S(1)}, u32[]{:S(2)}, u32[]{:S(2)}) collective-permute-start(f32[16,128]{1,0:T(8,128)S(1)} %get-tuple-element.24), channel_id=1, source_target_pairs={{0,6},{2,0},{4,2},{6,4},{1,7},{3,1},{5,3},{7,5},{8,14},{10,8},{12,... | collective-permute-start | bytes 24584 | tf_op jit(solution)/shard_map/ppermute | solution.py:20
  145.1 0.5 collective-permute-start.30
  146.0 0.7 collective-permute-done.29
  146.7 3.5 %collective-permute-done.30 = f32[16,128]{1,0:T(8,128)S(1)} collective-permute-done((f32[16,128]{1,0:T(8,128)S(1)}, f32[16,128]{1,0:T(8,128)S(1)}, u32[]{:S(2)}, u32[]{:S(2)}) %collective-permute-start.30) | collective-permute-done | bytes 8224 | tf_op jit(solution)/shard_map/ppermute | solution.py:20
  150.3 0.6 fusion.19
  150.9 11.2 %all-to-all-start.1 = ((f32[8,2,128]{2,1,0:T(2,128)}), f32[8,2,128]{2,1,0:T(2,128)S(1)}, u32[]{:S(2)}, u32[]{:S(2)}) async-start(f32[8,2,128]{2,1,0:T(2,128)} %bitcast.39), calls=%async_computation.1 | async-start | bytes 16384 | tf_op jit(solution)/shard_map/all_to_all | solution.py:292
  162.1 0.6 select_reduce_fusion
  165.4 1.4 all-to-all-done.1
  166.8 0.6 divide_add_fusion
  (91 shorter events, 2.4 us)
Async XLA Ops:
  0.6 55.9 %copy-start = (bf16[4096,128]{1,0:T(8,128)(2,1)S(1)}, bf16[4096,128]{1,0:T(8,128)(2,1)}, u32[]{:S(2)}) copy-start(bf16[4096,128]{1,0:T(8,128)(2,1)} %param.21) | copy-start | bytes 3145732
  0.6 9.6 %copy-start.1 = (bf16[128,4096]{1,0:T(8,128)(2,1)S(1)}, bf16[128,4096]{1,0:T(8,128)(2,1)}, u32[]{:S(2)}) copy-start(bf16[128,4096]{1,0:T(8,128)(2,1)} %embed_ref.1) | copy-start | bytes 3145732
  1.5 12.3 %copy-start.12 = (bf16[8,2,128]{2,0,1:T(8,128)(2,1)}, bf16[8,2,128]{2,0,1:T(8,128)(2,1)S(1)}, u32[]{:S(2)}) copy-start(bf16[8,2,128]{2,0,1:T(8,128)(2,1)S(1)} %copy.46) | copy-start | bytes 12292
  1.5 12.3 %collective-permute-start = (bf16[8,128]{1,0:T(8,128)(2,1)S(1)}, bf16[8,128]{1,0:T(8,128)(2,1)S(1)}, u32[]{:S(2)}, u32[]{:S(2)}) collective-permute-start(bf16[8,128]{1,0:T(8,128)(2,1)S(1)} %select_bitcast_fusion.4), channel_id=1, source_target_pairs={{0,1},{1,0},{2,3},{3,2},{4,5},{5,4},{6,7},{7,6},{8,9},{9,8},{10,11... | collective-permute-start | bytes 6152 | tf_op jit(solution)/shard_map/ppermute | solution.py:20
  3.8 34.2 %collective-permute-start.12 = (bf16[128,1024]{1,0:T(8,128)(2,1)}, bf16[128,1024]{1,0:T(8,128)(2,1)}, u32[]{:S(2)}, u32[]{:S(2)}) collective-permute-start(bf16[128,1024]{1,0:T(8,128)(2,1)} %get-tuple-element.7), channel_id=1, source_target_pairs={{0,4},{2,6},{4,0},{6,2},{1,5},{3,7},{5,1},{7,3},{8,12},{10,14},{12... | collective-permute-start | bytes 786440 | tf_op jit(solution)/shard_map/ppermute | solution.py:20
  6.8 31.2 %collective-permute-start.11 = (bf16[128,1024]{1,0:T(8,128)(2,1)}, bf16[128,1024]{1,0:T(8,128)(2,1)}, u32[]{:S(2)}, u32[]{:S(2)}) collective-permute-start(bf16[128,1024]{1,0:T(8,128)(2,1)} %get-tuple-element.8), channel_id=1, source_target_pairs={{0,6},{2,0},{4,2},{6,4},{1,7},{3,1},{5,3},{7,5},{8,14},{10,8},{12,... | collective-permute-start | bytes 786440 | tf_op jit(solution)/shard_map/ppermute | solution.py:20
  8.7 1.6 copy-start.10
  8.7 1.6 copy-start.11
  10.5 2.2 %copy-start.17 = (bf16[3,4096,128]{2,1,0:T(8,128)(2,1)S(1)}, bf16[3,4096,128]{2,1,0:T(8,128)(2,1)}, u32[]{:S(2)}) copy-start(bf16[3,4096,128]{2,1,0:T(8,128)(2,1)} %param.17) | copy-start | bytes 9437188
  13.2 5.5 %copy-start.9 = (bf16[128,1024]{1,0:T(8,128)(2,1)S(1)}, bf16[128,1024]{1,0:T(8,128)(2,1)}, u32[]{:S(2)}) copy-start(bf16[128,1024]{1,0:T(8,128)(2,1)} %get-tuple-element.9) | copy-start | bytes 786436
  13.7 26.5 %copy-start.3 = (f32[4,128]{1,0:T(4,128)S(1)}, f32[4,128]{1,0:T(4,128)}, u32[]{:S(2)}) copy-start(f32[4,128]{1,0:T(4,128)} %head_gain_ref.1) | copy-start | bytes 6148
  13.8 4.9 %collective-permute-start.3 = (bf16[16,128]{1,0:T(8,128)(2,1)S(1)}, bf16[16,128]{1,0:T(8,128)(2,1)S(1)}, u32[]{:S(2)}, u32[]{:S(2)}) collective-permute-start(bf16[16,128]{1,0:T(8,128)(2,1)S(1)} %bitcast.100), channel_id=1, source_target_pairs={{0,2},{2,4},{4,6},{6,0},{1,3},{3,5},{5,7},{7,1},{8,10},{10,12},{12... | collective-permute-start | bytes 12296 | tf_op jit(solution)/shard_map/ppermute | solution.py:20
  14.8 5.1 %collective-permute-start.2 = (bf16[16,128]{1,0:T(8,128)(2,1)S(1)}, bf16[16,128]{1,0:T(8,128)(2,1)S(1)}, u32[]{:S(2)}, u32[]{:S(2)}) collective-permute-start(bf16[16,128]{1,0:T(8,128)(2,1)S(1)} %bitcast.101), channel_id=1, source_target_pairs={{0,4},{2,6},{4,0},{6,2},{1,5},{3,7},{5,1},{7,3},{8,12},{10,14},{12... | collective-permute-start | bytes 12296 | tf_op jit(solution)/shard_map/ppermute | solution.py:20
  15.5 4.5 %collective-permute-start.1 = (bf16[16,128]{1,0:T(8,128)(2,1)S(1)}, bf16[16,128]{1,0:T(8,128)(2,1)S(1)}, u32[]{:S(2)}, u32[]{:S(2)}) collective-permute-start(bf16[16,128]{1,0:T(8,128)(2,1)S(1)} %bitcast.102), channel_id=1, source_target_pairs={{0,6},{2,0},{4,2},{6,4},{1,7},{3,1},{5,3},{7,5},{8,14},{10,8},{12,... | collective-permute-start | bytes 12296 | tf_op jit(solution)/shard_map/ppermute | solution.py:20
  18.7 19.3 %collective-permute-start.13 = (bf16[128,1024]{1,0:T(8,128)(2,1)S(1)}, bf16[128,1024]{1,0:T(8,128)(2,1)S(1)}, u32[]{:S(2)}, u32[]{:S(2)}) collective-permute-start(bf16[128,1024]{1,0:T(8,128)(2,1)S(1)} %copy-done.9), channel_id=1, source_target_pairs={{0,2},{2,4},{4,6},{6,0},{1,3},{3,5},{5,7},{7,1},{8,10},{10,12},{12... | collective-permute-start | bytes 786440 | tf_op jit(solution)/shard_map/ppermute | solution.py:20
  20.1 9.0 %collective-permute-start.5 = (bf16[4,16,128]{2,1,0:T(8,128)(2,1)S(1)}, bf16[4,16,128]{2,1,0:T(8,128)(2,1)S(1)}, u32[]{:S(2)}, u32[]{:S(2)}) collective-permute-start(bf16[4,16,128]{2,1,0:T(8,128)(2,1)S(1)} %get-tuple-element.29), channel_id=1, source_target_pairs={{0,16},{8,24},{16,0},{24,8},{1,17},{9,25},{17,1},{25,9},{2,18},{10... | collective-permute-start | bytes 49160 | tf_op jit(solution)/shard_map/ppermute | solution.py:20
  27.3 4.6 %collective-permute-start.4 = (bf16[4,16,128]{2,1,0:T(8,128)(2,1)S(1)}, bf16[4,16,128]{2,1,0:T(8,128)(2,1)S(1)}, u32[]{:S(2)}, u32[]{:S(2)}) collective-permute-start(bf16[4,16,128]{2,1,0:T(8,128)(2,1)S(1)} %get-tuple-element.29), channel_id=1, source_target_pairs={{0,24},{8,0},{16,8},{24,16},{1,25},{9,1},{17,9},{25,17},{2,26},{10... | collective-permute-start | bytes 49160 | tf_op jit(solution)/shard_map/ppermute | solution.py:20
  29.0 90.1 %collective-permute-start.24 = (bf16[3,4096,128]{2,1,0:T(8,128)(2,1)}, bf16[3,4096,128]{2,1,0:T(8,128)(2,1)}, u32[]{:S(2)}, u32[]{:S(2)}) collective-permute-start(bf16[3,4096,128]{2,1,0:T(8,128)(2,1)} %own_ref.1), channel_id=1, source_target_pairs={{0,1},{1,0},{2,3},{3,2},{4,5},{5,4},{6,7},{7,6},{8,9},{9,8},{10,11... | collective-permute-start | bytes 9437192 | tf_op jit(solution)/shard_map/ppermute | solution.py:20
  31.9 6.0 %collective-permute-start.6 = (bf16[4,16,128]{2,1,0:T(8,128)(2,1)S(1)}, bf16[4,16,128]{2,1,0:T(8,128)(2,1)S(1)}, u32[]{:S(2)}, u32[]{:S(2)}) collective-permute-start(bf16[4,16,128]{2,1,0:T(8,128)(2,1)S(1)} %get-tuple-element.29), channel_id=1, source_target_pairs={{0,8},{8,16},{16,24},{24,0},{1,9},{9,17},{17,25},{25,1},{2,10},{10... | collective-permute-start | bytes 49160 | tf_op jit(solution)/shard_map/ppermute | solution.py:20
  38.0 2.0 %collective-permute-start.7 = (bf16[144,384]{1,0:T(8,128)(2,1)S(1)}, bf16[144,384]{1,0:T(8,128)(2,1)S(1)}, u32[]{:S(2)}, u32[]{:S(2)}) collective-permute-start(bf16[144,384]{1,0:T(8,128)(2,1)S(1)} %maximum_maximum_fusion.1), channel_id=1, source_target_pairs={{0,1},{1,0},{2,3},{3,2},{4,5},{5,4},{6,7},{7,6},{8,9},{9,8},{10,11... | collective-permute-start | bytes 331784 | tf_op jit(solution)/shard_map/ppermute | solution.py:20
  39.2 17.4 %copy-start.5 = (bf16[128,4096]{1,0:T(8,128)(2,1)S(1)}, bf16[128,4096]{1,0:T(8,128)(2,1)}, u32[]{:S(2)}) copy-start(bf16[128,4096]{1,0:T(8,128)(2,1)} %param.18) | copy-start | bytes 3145732
  39.2 23.8 %collective-permute-start.14 = (bf16[4,128,1024]{2,1,0:T(8,128)(2,1)S(1)}, bf16[4,128,1024]{2,1,0:T(8,128)(2,1)}, u32[]{:S(2)}, u32[]{:S(2)}) collective-permute-start(bf16[4,128,1024]{2,1,0:T(8,128)(2,1)S(1)} %pad_maximum_fusion.own_ref), channel_id=1, source_target_pairs={{0,1},{1,0},{2,3},{3,2},{4,5},{5,4},{6,7},{7,6},{8,9},{9,8},{10,11... | collective-permute-start | bytes 3145736 | tf_op jit(solution)/shard_map/ppermute | solution.py:20
  51.7 1.6 copy-start.7
  51.7 7.4 %collective-permute-start.10 = (bf16[256,256]{1,0:T(8,128)(2,1)S(1)}, bf16[256,256]{1,0:T(8,128)(2,1)S(1)}, u32[]{:S(2)}, u32[]{:S(2)}) collective-permute-start(bf16[256,256]{1,0:T(8,128)(2,1)S(1)} %slice.112.a0.att_ref), channel_id=1, source_target_pairs={{0,2},{2,4},{4,6},{6,0},{1,3},{3,5},{5,7},{7,1},{8,10},{10,12},{12... | collective-permute-start | bytes 393224 | tf_op jit(solution)/shard_map/ppermute | solution.py:20
  53.3 9.6 %collective-permute-start.9 = (bf16[256,256]{1,0:T(8,128)(2,1)S(1)}, bf16[256,256]{1,0:T(8,128)(2,1)S(1)}, u32[]{:S(2)}, u32[]{:S(2)}) collective-permute-start(bf16[256,256]{1,0:T(8,128)(2,1)S(1)} %slice.112.a0.att_ref), channel_id=1, source_target_pairs={{0,4},{2,6},{4,0},{6,2},{1,5},{3,7},{5,1},{7,3},{8,12},{10,14},{12... | collective-permute-start | bytes 393224 | tf_op jit(solution)/shard_map/ppermute | solution.py:20
  56.0 7.0 %collective-permute-start.8 = (bf16[256,256]{1,0:T(8,128)(2,1)S(1)}, bf16[256,256]{1,0:T(8,128)(2,1)}, u32[]{:S(2)}, u32[]{:S(2)}) collective-permute-start(bf16[256,256]{1,0:T(8,128)(2,1)S(1)} %slice.112.a0.att_ref), channel_id=1, source_target_pairs={{0,6},{2,0},{4,2},{6,4},{1,7},{3,1},{5,3},{7,5},{8,14},{10,8},{12,... | collective-permute-start | bytes 393224 | tf_op jit(solution)/shard_map/ppermute | solution.py:20
  63.0 26.0 %copy-start.6 = (bf16[128,4096]{1,0:T(8,128)(2,1)S(1)}, bf16[128,4096]{1,0:T(8,128)(2,1)}, u32[]{:S(2)}) copy-start(bf16[128,4096]{1,0:T(8,128)(2,1)} %param.20) | copy-start | bytes 3145732
  66.3 39.3 %copy-start.8 = (bf16[128,128]{1,0:T(8,128)(2,1)S(1)}, bf16[128,128]{1,0:T(8,128)(2,1)}, u32[]{:S(2)}) copy-start(bf16[128,128]{1,0:T(8,128)(2,1)} %convolution_convert_fusion.1) | copy-start | bytes 98308
  66.3 10.0 %collective-permute-start.15 = (bf16[64,1024]{1,0:T(8,128)(2,1)S(1)}, bf16[64,1024]{1,0:T(8,128)(2,1)S(1)}, u32[]{:S(2)}, u32[]{:S(2)}) collective-permute-start(bf16[64,1024]{1,0:T(8,128)(2,1)S(1)} %get-tuple-element.10), channel_id=1, source_target_pairs={{0,8},{8,16},{16,24},{24,0},{1,9},{9,17},{17,25},{25,1},{2,10},{10... | collective-permute-start | bytes 393224 | tf_op jit(solution)/shard_map/ppermute | solution.py:20
  67.9 11.3 %collective-permute-start.17 = (bf16[64,1024]{1,0:T(8,128)(2,1)S(1)}, bf16[64,1024]{1,0:T(8,128)(2,1)S(1)}, u32[]{:S(2)}, u32[]{:S(2)}) collective-permute-start(bf16[64,1024]{1,0:T(8,128)(2,1)S(1)} %get-tuple-element.11), channel_id=1, source_target_pairs={{0,24},{8,0},{16,8},{24,16},{1,25},{9,1},{17,9},{25,17},{2,26},{10... | collective-permute-start | bytes 393224 | tf_op jit(solution)/shard_map/ppermute | solution.py:20
  70.5 10.8 %collective-permute-start.16 = (bf16[64,1024]{1,0:T(8,128)(2,1)S(1)}, bf16[64,1024]{1,0:T(8,128)(2,1)S(1)}, u32[]{:S(2)}, u32[]{:S(2)}) collective-permute-start(bf16[64,1024]{1,0:T(8,128)(2,1)S(1)} %get-tuple-element.12), channel_id=1, source_target_pairs={{0,16},{8,24},{16,0},{24,8},{1,17},{9,25},{17,1},{25,9},{2,18},{10... | collective-permute-start | bytes 393224 | tf_op jit(solution)/shard_map/ppermute | solution.py:20
  74.6 44.6 %copy-start.2 = (f32[1,4096]{1,0:T(1,128)S(1)}, f32[1,4096]{1,0:T(1,128)}, u32[]{:S(2)}) copy-start(f32[1,4096]{1,0:T(1,128)} %get-tuple-element.26) | copy-start | bytes 49156
  74.6 44.5 %copy-start.4 = (f32[4,128]{1,0:T(4,128)S(1)}, f32[4,128]{1,0:T(4,128)}, u32[]{:S(2)}) copy-start(f32[4,128]{1,0:T(4,128)} %head_gain_ref.1) | copy-start | bytes 6148
  81.4 13.0 %collective-permute-start.20 = (bf16[64,1024]{1,0:T(8,128)(2,1)S(1)}, bf16[64,1024]{1,0:T(8,128)(2,1)S(1)}, u32[]{:S(2)}, u32[]{:S(2)}) collective-permute-start(bf16[64,1024]{1,0:T(8,128)(2,1)S(1)} %add_convert_fusion), channel_id=1, source_target_pairs={{0,8},{8,16},{16,24},{24,0},{1,9},{9,17},{17,25},{25,1},{2,10},{10... | collective-permute-start | bytes 393224 | tf_op jit(solution)/shard_map/ppermute | solution.py:20
  83.3 11.1 %collective-permute-start.19 = (bf16[64,1024]{1,0:T(8,128)(2,1)S(1)}, bf16[64,1024]{1,0:T(8,128)(2,1)S(1)}, u32[]{:S(2)}, u32[]{:S(2)}) collective-permute-start(bf16[64,1024]{1,0:T(8,128)(2,1)S(1)} %add_convert_fusion), channel_id=1, source_target_pairs={{0,16},{8,24},{16,0},{24,8},{1,17},{9,25},{17,1},{25,9},{2,18},{10... | collective-permute-start | bytes 393224 | tf_op jit(solution)/shard_map/ppermute | solution.py:20
  86.6 14.2 %collective-permute-start.18 = (bf16[64,1024]{1,0:T(8,128)(2,1)S(1)}, bf16[64,1024]{1,0:T(8,128)(2,1)S(1)}, u32[]{:S(2)}, u32[]{:S(2)}) collective-permute-start(bf16[64,1024]{1,0:T(8,128)(2,1)S(1)} %add_convert_fusion), channel_id=1, source_target_pairs={{0,24},{8,0},{16,8},{24,16},{1,25},{9,1},{17,9},{25,17},{2,26},{10... | collective-permute-start | bytes 393224 | tf_op jit(solution)/shard_map/ppermute | solution.py:20
  100.9 12.6 %collective-permute-start.23 = (bf16[256,1024]{1,0:T(8,128)(2,1)S(1)}, bf16[256,1024]{1,0:T(8,128)(2,1)S(1)}, u32[]{:S(2)}, u32[]{:S(2)}) collective-permute-start(bf16[256,1024]{1,0:T(8,128)(2,1)S(1)} %pad_maximum_fusion.1.x0), channel_id=1, source_target_pairs={{0,2},{2,4},{4,6},{6,0},{1,3},{3,5},{5,7},{7,1},{8,10},{10,12},{12... | collective-permute-start | bytes 1572872 | tf_op jit(solution)/shard_map/ppermute | solution.py:20
  101.6 17.6 %collective-permute-start.22 = (bf16[256,1024]{1,0:T(8,128)(2,1)S(1)}, bf16[256,1024]{1,0:T(8,128)(2,1)S(1)}, u32[]{:S(2)}, u32[]{:S(2)}) collective-permute-start(bf16[256,1024]{1,0:T(8,128)(2,1)S(1)} %pad_maximum_fusion.1.x0), channel_id=1, source_target_pairs={{0,4},{2,6},{4,0},{6,2},{1,5},{3,7},{5,1},{7,3},{8,12},{10,14},{12... | collective-permute-start | bytes 1572872 | tf_op jit(solution)/shard_map/ppermute | solution.py:20
  104.3 14.9 %collective-permute-start.21 = (bf16[256,1024]{1,0:T(8,128)(2,1)S(1)}, bf16[256,1024]{1,0:T(8,128)(2,1)S(1)}, u32[]{:S(2)}, u32[]{:S(2)}) collective-permute-start(bf16[256,1024]{1,0:T(8,128)(2,1)S(1)} %pad_maximum_fusion.1.x0), channel_id=1, source_target_pairs={{0,6},{2,0},{4,2},{6,4},{1,7},{3,1},{5,3},{7,5},{8,14},{10,8},{12,... | collective-permute-start | bytes 1572872 | tf_op jit(solution)/shard_map/ppermute | solution.py:20
  105.6 1.6 collective-permute-start.25
  119.2 18.1 %copy-start.13 = (bf16[8,2,128]{2,0,1:T(8,128)(2,1)S(1)}, bf16[8,2,128]{2,0,1:T(8,128)(2,1)}, u32[]{:S(2)}) copy-start(bf16[8,2,128]{2,0,1:T(8,128)(2,1)} %copy-done.12) | copy-start | bytes 12292
  126.0 36.1 %copy-start.16 = (f32[1000]{0:T(1024)S(1)}, f32[1000]{0:T(1024)}, u32[]{:S(2)}) copy-start(f32[1000]{0:T(1024)} %param.13) | copy-start | bytes 12004
  126.0 40.8 %copy-start.15 = (f32[8,2,128]{2,1,0:T(2,128)S(1)}, f32[8,2,128]{2,1,0:T(2,128)}, u32[]{:S(2)}) copy-start(f32[8,2,128]{2,1,0:T(2,128)} %param.11) | copy-start | bytes 24580
  126.0 11.2 %collective-permute-start.26 = (f32[64,128]{1,0:T(8,128)S(1)}, f32[64,128]{1,0:T(8,128)S(1)}, u32[]{:S(2)}, u32[]{:S(2)}) collective-permute-start(f32[64,128]{1,0:T(8,128)S(1)} %get-tuple-element.15), channel_id=1, source_target_pairs={{0,8},{8,16},{16,24},{24,0},{1,9},{9,17},{17,25},{25,1},{2,10},{10... | collective-permute-start | bytes 98312 | tf_op jit(solution)/shard_map/ppermute | solution.py:20
  133.6 4.8 %collective-permute-start.28 = (f32[64,128]{1,0:T(8,128)S(1)}, f32[64,128]{1,0:T(8,128)S(1)}, u32[]{:S(2)}, u32[]{:S(2)}) collective-permute-start(f32[64,128]{1,0:T(8,128)S(1)} %get-tuple-element.16), channel_id=1, source_target_pairs={{0,24},{8,0},{16,8},{24,16},{1,25},{9,1},{17,9},{25,17},{2,26},{10... | collective-permute-start | bytes 98312 | tf_op jit(solution)/shard_map/ppermute | solution.py:20
  133.6 8.1 %collective-permute-start.27 = (f32[64,128]{1,0:T(8,128)S(1)}, f32[64,128]{1,0:T(8,128)S(1)}, u32[]{:S(2)}, u32[]{:S(2)}) collective-permute-start(f32[64,128]{1,0:T(8,128)S(1)} %get-tuple-element.17), channel_id=1, source_target_pairs={{0,16},{8,24},{16,0},{24,8},{1,17},{9,25},{17,1},{25,9},{2,18},{10... | collective-permute-start | bytes 98312 | tf_op jit(solution)/shard_map/ppermute | solution.py:20
  141.8 4.9 %collective-permute-start.29 = (f32[16,128]{1,0:T(8,128)S(1)}, f32[16,128]{1,0:T(8,128)S(1)}, u32[]{:S(2)}, u32[]{:S(2)}) collective-permute-start(f32[16,128]{1,0:T(8,128)S(1)} %get-tuple-element.23), channel_id=1, source_target_pairs={{0,2},{2,4},{4,6},{6,0},{1,3},{3,5},{5,7},{7,1},{8,10},{10,12},{12... | collective-permute-start | bytes 24584 | tf_op jit(solution)/shard_map/ppermute | solution.py:20
  142.5 4.2 %collective-permute-start.31 = (f32[16,128]{1,0:T(8,128)S(1)}, f32[16,128]{1,0:T(8,128)S(1)}, u32[]{:S(2)}, u32[]{:S(2)}) collective-permute-start(f32[16,128]{1,0:T(8,128)S(1)} %get-tuple-element.24), channel_id=1, source_target_pairs={{0,6},{2,0},{4,2},{6,4},{1,7},{3,1},{5,3},{7,5},{8,14},{10,8},{12,... | collective-permute-start | bytes 24584 | tf_op jit(solution)/shard_map/ppermute | solution.py:20
  145.1 5.2 %collective-permute-start.30 = (f32[16,128]{1,0:T(8,128)S(1)}, f32[16,128]{1,0:T(8,128)S(1)}, u32[]{:S(2)}, u32[]{:S(2)}) collective-permute-start(f32[16,128]{1,0:T(8,128)S(1)} %get-tuple-element.25), channel_id=1, source_target_pairs={{0,4},{2,6},{4,0},{6,2},{1,5},{3,7},{5,1},{7,3},{8,12},{10,14},{12... | collective-permute-start | bytes 24584 | tf_op jit(solution)/shard_map/ppermute | solution.py:20
  150.9 16.0 %all-to-all-start.1 = ((f32[8,2,128]{2,1,0:T(2,128)}), f32[8,2,128]{2,1,0:T(2,128)S(1)}, u32[]{:S(2)}, u32[]{:S(2)}) async-start(f32[8,2,128]{2,1,0:T(2,128)} %bitcast.39), calls=%async_computation.1 | async-start | bytes 16384 | tf_op jit(solution)/shard_map/all_to_all | solution.py:292
  166.8 0.6 copy-start.14

commit v2 on v1

v2 whole, which is shorter than its diff:
```python
import math

import jax
import jax.numpy as jnp
from jax import lax
from jax.experimental import pallas as pl
from jax.experimental.pallas import tpu as pltpu
from jax.sharding import Mesh, PartitionSpec as P

STRIDE = 20
EPS = 1e-06
NX = 4
HD = 128
ORDER = (1, 3, 2)
BF = jnp.bfloat16
F32 = jnp.float32


def shift(value, axis, step):
    size = lax.axis_size(axis)
    return lax.ppermute(value, axis, [(i, (i + step) % size) for i in range(size)])


def time_embedding(step_now, model_width):
    half_width = model_width // 2
    positions = jnp.arange(half_width, dtype=F32)
    frequency = jnp.exp(positions * (-math.log(10000.0) / half_width))
    angles = step_now.astype(F32) * frequency
    return jnp.concatenate([jnp.sin(angles), jnp.cos(angles)])


def head_norm(values, gain):
    mean_square = jnp.mean(values * values, axis=-1, keepdims=True)
    return (values * gain * lax.rsqrt(mean_square + EPS)).astype(BF)


def weigh(scores, mask=None):
    e = jnp.exp(scores * (1.0 / math.sqrt(HD)))
    if mask is not None:
        e = jnp.where(mask, e, 0.0)
    return (e / jnp.sum(e, axis=-1, keepdims=True)).astype(BF)


def dot_t(a, b):
    return lax.dot_general(a, b, (((1,), (1,)), ((), ())), preferred_element_type=F32)


def dot(a, b):
    return jnp.dot(a, b, preferred_element_type=F32)


def reorder(count, source):
    row = lax.broadcasted_iota(jnp.int32, (count, count), 0)
    col = lax.broadcasted_iota(jnp.int32, (count, count), 1)
    return (col == source(row)).astype(BF)


def space_kernel(place_ref, lat_ref, embed_ref, temb_ref, fold_ref, gain_ref, out_ref):
    z_here = place_ref[1]

    def source(row):
        z = (z_here + (row >> 2)) & 3
        return (((z * 4 + (row & 3)) * 2 + ((row >> 4) & 1)) << 3) + (row >> 5)

    lat = dot(reorder(256, source), lat_ref[...]).astype(BF)
    width = embed_ref.shape[1]
    chunk = 512
    total = jnp.zeros((lat.shape[0], 128), F32)
    for start in range(0, width, chunk):
        first = dot(lat, embed_ref[:, start : start + chunk]) + temb_ref[:, start : start + chunk]
        first = first.astype(BF).astype(F32)
        square = first * first
        for lane in range(0, chunk, 128):
            total = total + square[:, lane : lane + 128]
    mean_square = jnp.sum(total, axis=-1, keepdims=True) * (1.0 / width)
    scale = lax.rsqrt(mean_square + EPS)
    bias = fold_ref[128:129, :].astype(F32) + fold_ref[129:130, :].astype(F32)
    proj = (dot(lat, fold_ref[:128, :]) + bias) * scale
    parts = []
    for head in range(2):
        base = head * 3 * HD
        query = head_norm(proj[:, base : base + HD], gain_ref[0:1, :])
        key = head_norm(proj[:, base + HD : base + 2 * HD], gain_ref[1:2, :])
        value = proj[:, base + 2 * HD : base + 3 * HD].astype(BF)
        weights = weigh(dot_t(query, key))
        parts.append(dot(weights, value).astype(BF))
    result = jnp.concatenate(parts + [lat], axis=1)
    for tm in range(8):
        for x in range(NX):
            start = (tm * NX + x) * 32
            out_ref[start : start + 32, :] = result[tm * 32 : (tm + 1) * 32, :]


def output_kernel(
    place_ref, att_ref, embed_ref, temb_ref, own_ref, other_ref, out_ref, base_ref, att_own_ref, lhs_own, lhs_other, lat
):
    @pl.when(pl.program_id(0) == 0)
    def _():
        x_here = place_ref[0]
        core = place_ref[2]
        swap = reorder(256, lambda row: ((row & 15) << 4) + (row >> 4))
        for x in range(NX):
            rows = jnp.concatenate(
                [att_ref[(tm * NX + x) * 32 : (tm * NX + x + 1) * 32, :] for tm in range(8)], axis=0
            )
            rows = dot(swap, rows).astype(BF)
            slot = pl.multiple_of(((x - x_here) & 3) * HD, HD)
            first = rows[:, :HD]
            second = rows[:, HD : 2 * HD]
            lhs_own[:, pl.ds(slot, HD)] = jnp.where(core == 0, first, second)
            lhs_other[:, pl.ds(slot, HD)] = jnp.where(core == 0, second, first)

            @pl.when(x == x_here)
            def _():
                att_own_ref[...] = rows[:, : 2 * HD]

            if x == 0:
                lat[...] = rows[:64, 2 * HD :]

    width = own_ref.shape[2]
    own = own_ref[...].reshape(NX * HD, width)
    other = other_ref[...].reshape(NX * HD, width)
    share = (dot(lhs_own[...], own) + dot(lhs_other[...], other)).astype(BF)
    out_ref[...] = share[64:, :]
    first = (dot(lat[...], embed_ref[...]) + temb_ref[...]).astype(BF)
    base_ref[...] = first.astype(F32) + share[:64, :].astype(F32)


def time_kernel(
    place_ref, x0, x1, x2, x3, gain_ref, own_ref, other_ref, head_gain_ref, att_ref, fold_ref, out_ref, proj, total
):
    step = pl.program_id(0)

    @pl.when(step == 0)
    def _():
        proj[...] = jnp.zeros_like(proj)
        total[...] = jnp.zeros_like(total)

    for k, ref in enumerate((x0, x1, x2, x3)):

        @pl.when(step == k)
        def _(ref=ref):
            rows = ref[...].astype(F32)
            square = rows * rows
            part = total[...]
            for lane in range(0, rows.shape[1], 128):
                part = part + square[:, lane : lane + 128]
            total[...] = part
            gained = (rows * gain_ref[0]).astype(BF)
            for index in range(3):
                pair = jnp.concatenate([own_ref[index], other_ref[index]], axis=1)
                proj[:, index * 2 * HD : (index + 1) * 2 * HD] += dot(gained, pair)

    @pl.when(step == NX - 1)
    def _():
        z_here = place_ref[1]
        width = NX * x0.shape[1]
        mean_square = jnp.sum(total[...], axis=-1, keepdims=True) * (1.0 / width)
        scale = lax.rsqrt(mean_square + EPS)
        count = x0.shape[0]
        row_patch = lax.broadcasted_iota(jnp.int32, (count, count), 0) >> 4
        col_patch = lax.broadcasted_iota(jnp.int32, (count, count), 1) >> 4
        mask = row_patch == col_patch
        parts = [att_ref[...]]
        for side in range(2):
            query, key, value = [
                proj[:, (2 * index + side) * HD : (2 * index + side + 1) * HD] * scale for index in range(3)
            ]
            query = head_norm(query, head_gain_ref[2:3, :])
            key = head_norm(key, head_gain_ref[3:4, :])
            weights = weigh(dot_t(query, key), mask)
            parts.append(dot(weights, value.astype(BF)).astype(BF))

        def source(row):
            z = (((row >> 3) & 3) - z_here) & 3
            return (z << 6) + (((row >> 1) & 3) << 4) + ((row >> 5) << 1) + (row & 1)

        both = dot(reorder(count, source), jnp.concatenate(parts, axis=1)).astype(BF)
        out_ref[...] = dot(both, fold_ref[...])


def body(
    latents,
    timestep,
    alpha_table,
    norm_gain,
    head_gain,
    embed_weight,
    space_project,
    space_output,
    time_project,
    time_output,
    noise_weight,
):
    width = embed_weight.shape[1]
    block = width // NX
    core = lax.axis_index("c")
    place = lax.axis_index("x")
    places = jnp.stack([place, lax.axis_index("zh"), core]).astype(jnp.int32)
    step_now = timestep[0]
    positions = jnp.arange(alpha_table.shape[0], dtype=jnp.int32)
    alpha_now = jnp.sum(jnp.where(positions == step_now, alpha_table, 0.0))
    alpha_next = jnp.sum(jnp.where(positions == step_now + STRIDE, alpha_table, 0.0))
    temb = time_embedding(step_now, width)[None, :]

    def in_order(own, other):
        first = jnp.where(core == 0, own, other)
        second = jnp.where(core == 0, other, own)
        return jnp.stack([first, second])

    lat_bf = latents.astype(BF)
    lat_rows = jnp.broadcast_to(lat_bf.transpose(1, 0, 2)[None], (16, 2, 8, HD)).reshape(256, HD)
    lat_rows = lax.all_to_all(lat_rows, ("zh", "x", "c"), split_axis=0, concat_axis=0, tiled=True)

    scaled = temb * norm_gain[0:1]
    high = scaled.astype(BF)
    low = (scaled - high.astype(F32)).astype(BF)
    lhs = jnp.concatenate(
        [(embed_weight.astype(F32) * norm_gain[0:1]).astype(BF), high, low, jnp.zeros((14, width), BF)]
    )
    fold = jnp.concatenate([dot(lhs, space_project[i]) for i in range(3)], axis=1)
    bias = fold[128:129] + fold[129:130]
    bias_high = bias.astype(BF)
    bias_low = (bias - bias_high.astype(F32)).astype(BF)
    fold = jnp.concatenate([fold[:128].astype(BF), bias_high, bias_low, jnp.zeros((14, 3 * HD), BF)])
    fold = in_order(fold, shift(fold, "c", 1)).transpose(1, 0, 2).reshape(144, 6 * HD)

    time_other = shift(time_project, "c", 1)
    pieces = [
        lax.dynamic_slice(space_output, (0, ((place - d) % NX) * block), (HD, block)) for d in range(NX)
    ]
    got = {d: shift(pieces[d], "x", -d) for d in ORDER}
    out_own = jnp.stack([pieces[0]] + [got[d] for d in range(1, NX)])
    out_other = shift(out_own, "c", 1)
    noise_fold = jnp.concatenate(
        [dot(space_output, noise_weight).astype(BF), dot(time_output, noise_weight).astype(BF)]
    )
    noise_other = shift(noise_fold, "c", 1)
    noise_fold = jnp.concatenate(
        [in_order(noise_fold[:HD], noise_other[:HD]).reshape(2 * HD, HD), noise_fold[HD:], noise_other[HD:]]
    )

    def whole(*shape):
        return pl.BlockSpec(shape, lambda i, s: (0,) * len(shape))

    attended = pl.pallas_call(
        space_kernel,
        out_shape=jax.ShapeDtypeStruct((1024, 3 * HD), BF),
        grid_spec=pltpu.PrefetchScalarGridSpec(
            num_scalar_prefetch=1,
            grid=(1,),
            in_specs=[whole(256, HD), whole(HD, width), whole(1, width), whole(144, 6 * HD), whole(4, HD)],
            out_specs=whole(1024, 3 * HD),
        ),
        compiler_params=pltpu.CompilerParams(vmem_limit_bytes=32 * 1024 * 1024),
        name="space_attention",
    )(places, lat_rows, embed_weight, temb, fold, head_gain)

    regrouped = lax.all_to_all(attended, ("y", "zl", "x", "c"), split_axis=0, concat_axis=0, tiled=True)

    tiles = 4
    tile = block // tiles
    share, base, att_own = pl.pallas_call(
        output_kernel,
        out_shape=(
            jax.ShapeDtypeStruct((192, block), BF),
            jax.ShapeDtypeStruct((64, block), F32),
            jax.ShapeDtypeStruct((256, 2 * HD), BF),
        ),
        grid_spec=pltpu.PrefetchScalarGridSpec(
            num_scalar_prefetch=1,
            grid=(tiles,),
            in_specs=[
                whole(1024, 3 * HD),
                pl.BlockSpec((HD, tile), lambda i, s: (0, s[0] * tiles + i)),
                pl.BlockSpec((1, tile), lambda i, s: (0, s[0] * tiles + i)),
                pl.BlockSpec((NX, HD, tile), lambda i, s: (0, 0, i)),
                pl.BlockSpec((NX, HD, tile), lambda i, s: (0, 0, i)),
            ],
            out_specs=[
                pl.BlockSpec((192, tile), lambda i, s: (0, i)),
                pl.BlockSpec((64, tile), lambda i, s: (0, i)),
                whole(256, 2 * HD),
            ],
            scratch_shapes=[
                pltpu.VMEM((256, NX * HD), BF),
                pltpu.VMEM((256, NX * HD), BF),
                pltpu.VMEM((64, HD), BF),
            ],
        ),
        compiler_params=pltpu.CompilerParams(vmem_limit_bytes=32 * 1024 * 1024),
        name="space_output",
    )(places, regrouped, embed_weight, temb, out_own, out_other)

    sent = {d: shift(share[64 * (d - 1) : 64 * d], "zh", d) for d in ORDER}
    for d in ORDER:
        base = base + sent[d].astype(F32)
    second = base.astype(BF)
    got = {d: shift(second, "zh", -d) for d in ORDER}
    second = jnp.concatenate([second] + [got[d] for d in range(1, NX)])
    got = {d: shift(second, "x", -d) for d in ORDER}
    second_all = [second] + [got[d] for d in range(1, NX)]

    weight_spec = pl.BlockSpec((3, block, HD), lambda i, s: (0, (s[0] + i) % NX, 0))
    noise = pl.pallas_call(
        time_kernel,
        out_shape=jax.ShapeDtypeStruct((256, HD), F32),
        grid_spec=pltpu.PrefetchScalarGridSpec(
            num_scalar_prefetch=1,
            grid=(NX,),
            in_specs=[whole(256, block)] * NX
            + [
                pl.BlockSpec((1, 1, block), lambda i, s: ((s[0] + i) % NX, 0, 0)),
                weight_spec,
                weight_spec,
                whole(4, HD),
                whole(256, 2 * HD),
                whole(4 * HD, HD),
            ],
            out_specs=whole(256, HD),
            scratch_shapes=[pltpu.VMEM((256, 6 * HD), F32), pltpu.VMEM((256, HD), F32)],
        ),
        compiler_params=pltpu.CompilerParams(vmem_limit_bytes=40 * 1024 * 1024),
        name="time_attention",
    )(
        places,
        *second_all,
        norm_gain[1].reshape(NX, 1, block),
        time_project,
        time_other,
        head_gain,
        att_own,
        noise_fold,
    )

    noise = lax.all_to_all(noise, ("y", "zl", "zh", "x"), split_axis=0, concat_axis=0, tiled=True)
    total = jnp.sum(noise.reshape(8, 16, 2, HD), axis=1).reshape(16, HD)

    own_first = (dot(lat_bf.reshape(16, HD), embed_weight) + temb).astype(BF)
    predicted_noise = (total + dot(own_first, noise_weight)).reshape(latents.shape)
    latents_next = (
        jnp.sqrt(alpha_next)
        * (latents - jnp.sqrt(1.0 - alpha_now) * predicted_noise)
        / jnp.sqrt(alpha_now)
        + jnp.sqrt(1.0 - alpha_next) * predicted_noise
    )
    return (predicted_noise, latents_next)


def solution(mesh):
    fine = Mesh(mesh.devices.reshape(4, 2, 4, 4, 2), ("y", "zl", "zh", "x", "c"))
    space = ("zh", "x", "c")
    rows = P(space, ("y", "zl"), None)
    placed = (
        rows,
        P(),
        P(),
        P(),
        P(),
        P(),
        P(None, None, space),
        P(space, None),
        P(None, None, space),
        P(space, None),
        P(),
    )
    return jax.shard_map(
        body,
        mesh=fine,
        in_specs=placed,
        out_specs=(rows, rows),
        check_vma=False,
    )
```

time: 168 us -> 163 us (0.970)
  waiting for transfers between devices: 55.9 us -> 84.5 us
  starting transfers between devices: 70.4 us -> 47.2 us
  blocking collectives: 10 us -> 0 us
  Pallas kernels: 11.4 us -> 13.8 us
    ppermute x32 -> x16, starting transfers between devices: 59.2 us -> 19.8 us  [shift(): lax.ppermute(value, axis, [(i, (i + step) % size) for i in range(size)])]
    all_to_all x1 -> x3, waiting for transfers between devices: 1.39 us -> 18.4 us  [the longest x1 9.73 us: body(): lax.all_to_all(lat_rows, ('zh', 'x', 'c'), split_axis=0, concat_axis=0, t...]
    all_to_all x1 -> x3, starting transfers between devices: 11.2 us -> 27.5 us  [the longest x1 11.4 us: body(): lax.all_to_all(lat_rows, ('zh', 'x', 'c'), split_axis=0, concat_axis=0, t...]
    ppermute x32 -> x16, waiting for transfers between devices: 54.5 us -> 66.1 us  [shift(): lax.ppermute(value, axis, [(i, (i + step) % size) for i in range(size)])]
    all_to_all x1 -> x0, blocking collectives: 10 us -> none  [body(): lax.all_to_all(attended, ('y', 'zl', 'c'), split_axis=0, concat_axis=0, t...]
    pallas_call x2, Pallas kernels: 4.63 us -> 7.22 us  [the longest x1 4.27 us: body(): pl.pallas_call(output_kernel, out_shape=(jax.ShapeDtypeStruct((192, block...]
    another operation x1, local copies, waits for them, and re-layouts: 2.09 us -> 0.09 us  [body(): out_own = jnp.stack([pieces[0]] + [got[d] for d in range(1, NX)])]
    dot_general x7 -> x6, matrix products: 5.71 us -> 4.2 us  [dot(): return jnp.dot(a, b, preferred_element_type=F32)]
  transfers between devices with their start and end apart: 33 -> 19, of which waited for: 22 -> 15; matrix products, arithmetic and copies ran while one was open for 8% -> 2% of each run, Pallas kernels for 3% -> 3%
where the time goes in v2:
time: 163 us; the launch traced here: 162 us
  waiting for transfers between devices  84.5 us (52%)
  starting transfers between devices  47.2 us (29%)
  Pallas kernels  13.8 us (8%)
  between operations  4.57 us (3%)
  other arithmetic  4.25 us (3%)
  matrix products  4.2 us (3%)
  local copies, waits for them, and re-layouts  3.44 us (2%)
    ppermute x16, waiting for transfers between devices, shift(): lax.ppermute(value, axis, [(i, (i + step) % size) for i in range(size)])  66.1 us
    ppermute x16, starting transfers between devices, shift(): lax.ppermute(value, axis, [(i, (i + step) % size) for i in range(size)])  19.8 us
    all_to_all x1, starting transfers between devices, body(): lax.all_to_all(lat_rows, ('zh', 'x', 'c'), split_axis=0, concat_axis=0, t...  11.4 us
    all_to_all x1, waiting for transfers between devices, body(): lax.all_to_all(lat_rows, ('zh', 'x', 'c'), split_axis=0, concat_axis=0, t...  9.73 us
    all_to_all x1, starting transfers between devices, body(): lax.all_to_all(noise, ('y', 'zl', 'zh', 'x'), split_axis=0, concat_axis=0...  9.35 us
    all_to_all x1, waiting for transfers between devices, body(): lax.all_to_all(noise, ('y', 'zl', 'zh', 'x'), split_axis=0, concat_axis=0...  8.66 us
    all_to_all x1, starting transfers between devices, body(): lax.all_to_all(attended, ('y', 'zl', 'x', 'c'), split_axis=0, concat_axis...  6.72 us
    pallas_call x1, Pallas kernels, body(): pl.pallas_call(time_kernel, out_shape=jax.ShapeDtypeStruct((256, HD), F32...  6.61 us
  transfers between devices with their start and end apart: 19, of which 15 were waited for; matrix products, arithmetic and copies ran while one was open for 2% of the time, Pallas kernels for 3%

profile of v2, /device:TPU:8, one launch (start us, length us, event | category | flops | bytes accessed | tf_op | source)
XLA Modules:
  0.0 162.1 jit_solution(9537584862036688721)
XLA Ops:
  0.6 0.0 copy-start
  1.4 0.1 fusion.13
  1.5 0.9 multiply_convert_fusion.1
  2.3 1.4 multiply_convert_fusion
  3.8 0.1 pad.27.clone
  3.9 1.9 %fusion.7 = f32[144,128]{1,0:T(8,128)S(1)} fusion(bf16[3,4096,128]{2,1,0:T(8,128)(2,1)} %param.17, bf16[1,4096]{1,0:T(2,128)(2,1)S(1)} %get-tuple-element.25, bf16[1,4096]{1,0:T(2,128)(2,1)S(1)} %get-tuple-element.24, bf16[128,4096]{1,0:T(8,128)(2,1)S(1)} %multiply_convert_fusion, bf16[144]{0:T(256)(128)(2,1)S(1)} %pad.27.clone), kind=kOutput, calls=%fused_computation.13 | convolution fusion | flops 155713536 | bytes 2187552 | tf_op jit(solution)/shard_map/dot_general | solution.py:49
  5.8 0.3 copy-done.12
  6.1 0.5 fusion.5
  6.6 0.0 copy-start.9
  6.6 0.5 fusion.3
  7.1 0.0 copy-start.1
  7.1 0.0 copy-start.5
  7.2 0.1 maximum_maximum_fusion.1
  7.3 0.1 collective-permute-start
  7.5 0.6 broadcast_in_dim.20
  8.1 11.4 %all-to-all-start = ((bf16[32,8,128]{2,1,0:T(8,128)(2,1)}), bf16[32,8,128]{2,1,0:T(8,128)(2,1)S(1)}, u32[]{:S(2)}, u32[]{:S(2)}) async-start(bf16[32,8,128]{2,1,0:T(8,128)(2,1)} %bitcast.4), calls=%async_computation | async-start | bytes 131072 | tf_op jit(solution)/shard_map/all_to_all | solution.py:213
  19.6 0.1 pad_add_fusion.place_ref
  19.7 0.1 select_bitcast_fusion.1
  19.8 0.0 copy-start.6
  19.9 9.7 %all-to-all-done = bf16[32,8,128]{2,1,0:T(8,128)(2,1)S(1)} async-done(((bf16[32,8,128]{2,1,0:T(8,128)(2,1)}), bf16[32,8,128]{2,1,0:T(8,128)(2,1)S(1)}, u32[]{:S(2)}, u32[]{:S(2)}) %all-to-all-start) | async-done | bytes 65568 | tf_op jit(solution)/shard_map/all_to_all | solution.py:213
  29.6 2.9 %space_attention.1 = bf16[1024,384]{1,0:T(8,128)(2,1)} custom-call(s32[3]{0:T(128)S(1)} %pad_add_fusion.place_ref, bf16[256,128]{1,0:T(8,128)(2,1)S(1)} %bitcast.63, bf16[128,4096]{1,0:T(8,128)(2,1)S(1)} %copy-done.1, f32[1,4096]{1,0:T(1,128)S(1)} %bitcast.61, bf16[144,768]{1,0:T(8,128)(2,1)S(1)} %bitcast.59, f32[4,128]{1,0:T(4,128)S(1)} %copy-done.5), custom_call_target="tpu_custom_call" | custom-call | tf_op jit(solution)/shard_map/space_attention/pallas_call | solution.py:246
  32.6 6.7 %all-to-all-start.1 = ((bf16[64,16,384]{2,1,0:T(8,128)(2,1)}), bf16[64,16,384]{2,1,0:T(8,128)(2,1)}, u32[]{:S(2)}, u32[]{:S(2)}) async-start(bf16[64,16,384]{2,1,0:T(8,128)(2,1)} %bitcast.15), calls=%async_computation.1 | async-start | bytes 1572864 | tf_op jit(solution)/shard_map/all_to_all | solution.py:259
  39.3 0.1 dynamic-slice_bitcast_fusion
  39.4 2.8 %collective-permute-start.1 = (bf16[128,1024]{1,0:T(8,128)(2,1)S(1)}, bf16[128,1024]{1,0:T(8,128)(2,1)S(1)}, u32[]{:S(2)}, u32[]{:S(2)}) collective-permute-start(bf16[128,1024]{1,0:T(8,128)(2,1)S(1)} %get-tuple-element.14), channel_id=1, source_target_pairs={{0,6},{2,0},{4,2},{6,4},{1,7},{3,1},{5,3},{7,5},{8,14},{10,8},{12,... | collective-permute-start | bytes 786440 | tf_op jit(solution)/shard_map/ppermute | solution.py:21
  42.2 0.8 collective-permute-start.2
  43.0 0.9 collective-permute-start.3
  43.9 12.1 %collective-permute-done.1 = bf16[128,1024]{1,0:T(8,128)(2,1)S(1)} collective-permute-done((bf16[128,1024]{1,0:T(8,128)(2,1)S(1)}, bf16[128,1024]{1,0:T(8,128)(2,1)S(1)}, u32[]{:S(2)}, u32[]{:S(2)}) %collective-permute-start.1) | collective-permute-done | bytes 262176 | tf_op jit(solution)/shard_map/ppermute | solution.py:21
  56.0 1.5 collective-permute-done.2
  57.5 4.9 %collective-permute-done.3 = bf16[128,1024]{1,0:T(8,128)(2,1)S(1)} collective-permute-done((bf16[128,1024]{1,0:T(8,128)(2,1)S(1)}, bf16[128,1024]{1,0:T(8,128)(2,1)S(1)}, u32[]{:S(2)}, u32[]{:S(2)}) %collective-permute-start.3) | collective-permute-done | bytes 262176 | tf_op jit(solution)/shard_map/ppermute | solution.py:21
  62.3 0.1 pad_maximum_fusion.own_ref
  62.5 0.1 collective-permute-start.4
  62.6 2.6 %collective-permute-done.4.other_ref = bf16[4,128,1024]{2,1,0:T(8,128)(2,1)S(1)} collective-permute-done((bf16[4,128,1024]{2,1,0:T(8,128)(2,1)S(1)}, bf16[4,128,1024]{2,1,0:T(8,128)(2,1)S(1)}, u32[]{:S(2)}, u32[]{:S(2)}) %collective-permute-start.4) | collective-permute-done | bytes 1048608 | tf_op jit(solution)/shard_map/ppermute | solution.py:21
  65.2 1.0 copy-done.3
  66.2 1.2 copy-done.4
  67.4 4.3 %space_output.1 = (bf16[192,1024]{1,0:T(8,128)(2,1)S(1)}, f32[64,1024]{1,0:T(8,128)S(1)}, bf16[256,256]{1,0:T(8,128)(2,1)S(1)}) custom-call(s32[3]{0:T(128)S(1)} %pad_add_fusion.place_ref, bf16[1024,384]{1,0:T(8,128)(2,1)} %bitcast.16.att_ref, bf16[128,4096]{1,0:T(8,128)(2,1)S(1)} %copy-done.1, f32[1,4096]{1,0:T(1,128)S(1)} %bitcast.62, ...), custom_call_target="tpu_custom_call" | custom-call | tf_op jit(solution)/shard_map/space_output/pallas_call | solution.py:263
  71.7 0.0 copy-start.8
  71.8 0.8 collective-permute-start.5
  72.6 3.4 %collective-permute-start.6 = (bf16[64,1024]{1,0:T(8,128)(2,1)S(1)}, bf16[64,1024]{1,0:T(8,128)(2,1)S(1)}, u32[]{:S(2)}, u32[]{:S(2)}) collective-permute-start(bf16[64,1024]{1,0:T(8,128)(2,1)S(1)} %get-tuple-element.18), channel_id=1, source_target_pairs={{0,24},{8,0},{16,8},{24,16},{1,25},{9,1},{17,9},{25,17},{2,26},{10... | collective-permute-start | bytes 393224 | tf_op jit(solution)/shard_map/ppermute | solution.py:21
  76.0 0.8 collective-permute-start.7
  76.8 0.4 convolution_convert_fusion.1
  77.2 0.0 copy-start.2
  77.2 8.7 %collective-permute-done.5 = bf16[64,1024]{1,0:T(8,128)(2,1)S(1)} collective-permute-done((bf16[64,1024]{1,0:T(8,128)(2,1)S(1)}, bf16[64,1024]{1,0:T(8,128)(2,1)S(1)}, u32[]{:S(2)}, u32[]{:S(2)}) %collective-permute-start.5) | collective-permute-done | bytes 131104 | tf_op jit(solution)/shard_map/ppermute | solution.py:21
  85.9 1.3 collective-permute-done.6
  87.2 0.1 add_convert_fusion
  87.3 3.2 %collective-permute-start.10 = (bf16[64,1024]{1,0:T(8,128)(2,1)S(1)}, bf16[64,1024]{1,0:T(8,128)(2,1)S(1)}, u32[]{:S(2)}, u32[]{:S(2)}) collective-permute-start(bf16[64,1024]{1,0:T(8,128)(2,1)S(1)} %add_convert_fusion), channel_id=1, source_target_pairs={{0,8},{8,16},{16,24},{24,0},{1,9},{9,17},{17,25},{25,1},{2,10},{10... | collective-permute-start | bytes 393224 | tf_op jit(solution)/shard_map/ppermute | solution.py:21
  90.4 1.6 collective-permute-start.8
  92.0 2.3 %collective-permute-start.9 = (bf16[64,1024]{1,0:T(8,128)(2,1)S(1)}, bf16[64,1024]{1,0:T(8,128)(2,1)S(1)}, u32[]{:S(2)}, u32[]{:S(2)}) collective-permute-start(bf16[64,1024]{1,0:T(8,128)(2,1)S(1)} %add_convert_fusion), channel_id=1, source_target_pairs={{0,16},{8,24},{16,0},{24,8},{1,17},{9,25},{17,1},{25,9},{2,18},{10... | collective-permute-start | bytes 393224 | tf_op jit(solution)/shard_map/ppermute | solution.py:21
  94.3 0.4 convolution_convert_fusion
  94.7 0.4 collective-permute-done.10
  95.1 1.6 collective-permute-done.8
  96.7 8.9 %collective-permute-done.9 = bf16[64,1024]{1,0:T(8,128)(2,1)S(1)} collective-permute-done((bf16[64,1024]{1,0:T(8,128)(2,1)S(1)}, bf16[64,1024]{1,0:T(8,128)(2,1)S(1)}, u32[]{:S(2)}, u32[]{:S(2)}) %collective-permute-start.9) | collective-permute-done | bytes 131104 | tf_op jit(solution)/shard_map/ppermute | solution.py:21
  105.7 1.5 collective-permute-start.11
  107.2 1.5 collective-permute-start.12
  108.7 0.1 collective-permute-start.15
  108.8 1.2 collective-permute-done.15
  110.1 10.5 %collective-permute-done.11.x1 = bf16[256,1024]{1,0:T(8,128)(2,1)S(1)} collective-permute-done((bf16[256,1024]{1,0:T(8,128)(2,1)S(1)}, bf16[256,1024]{1,0:T(8,128)(2,1)S(1)}, u32[]{:S(2)}, u32[]{:S(2)}) %collective-permute-start.11) | collective-permute-done | bytes 524320 | tf_op jit(solution)/shard_map/ppermute | solution.py:21
  120.6 3.0 %collective-permute-done.12.x2 = bf16[256,1024]{1,0:T(8,128)(2,1)S(1)} collective-permute-done((bf16[256,1024]{1,0:T(8,128)(2,1)S(1)}, bf16[256,1024]{1,0:T(8,128)(2,1)S(1)}, u32[]{:S(2)}, u32[]{:S(2)}) %collective-permute-start.12) | collective-permute-done | bytes 524320 | tf_op jit(solution)/shard_map/ppermute | solution.py:21
  123.6 9.4 %collective-permute-done.13.x3 = bf16[256,1024]{1,0:T(8,128)(2,1)S(1)} collective-permute-done((bf16[256,1024]{1,0:T(8,128)(2,1)S(1)}, bf16[256,1024]{1,0:T(8,128)(2,1)S(1)}, u32[]{:S(2)}, u32[]{:S(2)}) %collective-permute-start.13) | collective-permute-done | bytes 524320 | tf_op jit(solution)/shard_map/ppermute | solution.py:21
  133.0 6.6 %time_attention.1 = f32[256,128]{1,0:T(8,128)} custom-call(s32[3]{0:T(128)S(1)} %pad_add_fusion.place_ref, bf16[256,1024]{1,0:T(8,128)(2,1)S(1)} %pad_maximum_fusion.1.x0, bf16[256,1024]{1,0:T(8,128)(2,1)S(1)} %collective-permute-done.11.x1, bf16[256,1024]{1,0:T(8,128)(2,1)S(1)} %collective-permute-done.12.x2, ...), custom_call_target="tpu_custom_call" | custom-call | tf_op jit(solution)/shard_map/time_attention/pallas_call | solution.py:305
  139.6 9.4 %all-to-all-start.2 = ((f32[128,2,128]{2,1,0:T(2,128)}), f32[128,2,128]{2,1,0:T(2,128)S(1)}, u32[]{:S(2)}, u32[]{:S(2)}) async-start(f32[128,2,128]{2,1,0:T(2,128)} %bitcast.25), calls=%async_computation.2 | async-start | bytes 262144 | tf_op jit(solution)/shard_map/all_to_all | solution.py:336
  149.0 0.6 select_reduce_fusion
  152.3 8.7 %all-to-all-done.2 = f32[128,2,128]{2,1,0:T(2,128)S(1)} async-done(((f32[128,2,128]{2,1,0:T(2,128)}), f32[128,2,128]{2,1,0:T(2,128)S(1)}, u32[]{:S(2)}, u32[]{:S(2)}) %all-to-all-start.2) | async-done | bytes 131104 | tf_op jit(solution)/shard_map/all_to_all | solution.py:336
  161.0 0.4 fusion.2
  161.4 0.6 divide_add_fusion
  (40 shorter events, 0.3 us)
Async XLA Ops:
  0.6 76.1 %copy-start = (bf16[4096,128]{1,0:T(8,128)(2,1)S(1)}, bf16[4096,128]{1,0:T(8,128)(2,1)}, u32[]{:S(2)}) copy-start(bf16[4096,128]{1,0:T(8,128)(2,1)} %param.21) | copy-start | bytes 3145732
  3.9 2.2 %copy-start.12 = (bf16[3,4096,128]{2,1,0:T(8,128)(2,1)S(1)}, bf16[3,4096,128]{2,1,0:T(8,128)(2,1)}, u32[]{:S(2)}) copy-start(bf16[3,4096,128]{2,1,0:T(8,128)(2,1)} %param.17) | copy-start | bytes 9437188
  6.6 0.8 copy-start.9
  7.1 22.5 %copy-start.1 = (bf16[128,4096]{1,0:T(8,128)(2,1)S(1)}, bf16[128,4096]{1,0:T(8,128)(2,1)}, u32[]{:S(2)}) copy-start(bf16[128,4096]{1,0:T(8,128)(2,1)} %embed_ref.3) | copy-start | bytes 3145732
  7.1 22.5 %copy-start.5 = (f32[4,128]{1,0:T(4,128)S(1)}, f32[4,128]{1,0:T(4,128)}, u32[]{:S(2)}) copy-start(f32[4,128]{1,0:T(4,128)} %head_gain_ref.1) | copy-start | bytes 6148
  7.3 12.3 %collective-permute-start = (bf16[144,384]{1,0:T(8,128)(2,1)S(1)}, bf16[144,384]{1,0:T(8,128)(2,1)S(1)}, u32[]{:S(2)}, u32[]{:S(2)}) collective-permute-start(bf16[144,384]{1,0:T(8,128)(2,1)S(1)} %maximum_maximum_fusion.1), channel_id=1, source_target_pairs={{0,1},{1,0},{2,3},{3,2},{4,5},{5,4},{6,7},{7,6},{8,9},{9,8},{10,11... | collective-permute-start | bytes 331784 | tf_op jit(solution)/shard_map/ppermute | solution.py:21
  8.1 21.5 %all-to-all-start = ((bf16[32,8,128]{2,1,0:T(8,128)(2,1)}), bf16[32,8,128]{2,1,0:T(8,128)(2,1)S(1)}, u32[]{:S(2)}, u32[]{:S(2)}) async-start(bf16[32,8,128]{2,1,0:T(8,128)(2,1)} %bitcast.4), calls=%async_computation | async-start | bytes 131072 | tf_op jit(solution)/shard_map/all_to_all | solution.py:213
  19.8 19.5 %copy-start.6 = (bf16[128,4096]{1,0:T(8,128)(2,1)S(1)}, bf16[128,4096]{1,0:T(8,128)(2,1)}, u32[]{:S(2)}) copy-start(bf16[128,4096]{1,0:T(8,128)(2,1)} %param.18) | copy-start | bytes 3145732
  32.6 33.6 %all-to-all-start.1 = ((bf16[64,16,384]{2,1,0:T(8,128)(2,1)}), bf16[64,16,384]{2,1,0:T(8,128)(2,1)}, u32[]{:S(2)}, u32[]{:S(2)}) async-start(bf16[64,16,384]{2,1,0:T(8,128)(2,1)} %bitcast.15), calls=%async_computation.1 | async-start | bytes 1572864 | tf_op jit(solution)/shard_map/all_to_all | solution.py:259
  39.4 16.5 %collective-permute-start.1 = (bf16[128,1024]{1,0:T(8,128)(2,1)S(1)}, bf16[128,1024]{1,0:T(8,128)(2,1)S(1)}, u32[]{:S(2)}, u32[]{:S(2)}) collective-permute-start(bf16[128,1024]{1,0:T(8,128)(2,1)S(1)} %get-tuple-element.14), channel_id=1, source_target_pairs={{0,6},{2,0},{4,2},{6,4},{1,7},{3,1},{5,3},{7,5},{8,14},{10,8},{12,... | collective-permute-start | bytes 786440 | tf_op jit(solution)/shard_map/ppermute | solution.py:21
  42.2 15.3 %collective-permute-start.2 = (bf16[128,1024]{1,0:T(8,128)(2,1)S(1)}, bf16[128,1024]{1,0:T(8,128)(2,1)S(1)}, u32[]{:S(2)}, u32[]{:S(2)}) collective-permute-start(bf16[128,1024]{1,0:T(8,128)(2,1)S(1)} %get-tuple-element.13), channel_id=1, source_target_pairs={{0,4},{2,6},{4,0},{6,2},{1,5},{3,7},{5,1},{7,3},{8,12},{10,14},{12... | collective-permute-start | bytes 786440 | tf_op jit(solution)/shard_map/ppermute | solution.py:21
  43.0 19.3 %collective-permute-start.3 = (bf16[128,1024]{1,0:T(8,128)(2,1)S(1)}, bf16[128,1024]{1,0:T(8,128)(2,1)S(1)}, u32[]{:S(2)}, u32[]{:S(2)}) collective-permute-start(bf16[128,1024]{1,0:T(8,128)(2,1)S(1)} %get-tuple-element.15), channel_id=1, source_target_pairs={{0,2},{2,4},{4,6},{6,0},{1,3},{3,5},{5,7},{7,1},{8,10},{10,12},{12... | collective-permute-start | bytes 786440 | tf_op jit(solution)/shard_map/ppermute | solution.py:21
  43.9 89.1 %collective-permute-start.14 = (bf16[3,4096,128]{2,1,0:T(8,128)(2,1)}, bf16[3,4096,128]{2,1,0:T(8,128)(2,1)}, u32[]{:S(2)}, u32[]{:S(2)}) collective-permute-start(bf16[3,4096,128]{2,1,0:T(8,128)(2,1)} %own_ref.1), channel_id=1, source_target_pairs={{0,1},{1,0},{2,3},{3,2},{4,5},{5,4},{6,7},{7,6},{8,9},{9,8},{10,11... | collective-permute-start | bytes 9437192 | tf_op jit(solution)/shard_map/ppermute | solution.py:21
  62.5 2.7 %collective-permute-start.4 = (bf16[4,128,1024]{2,1,0:T(8,128)(2,1)S(1)}, bf16[4,128,1024]{2,1,0:T(8,128)(2,1)S(1)}, u32[]{:S(2)}, u32[]{:S(2)}) collective-permute-start(bf16[4,128,1024]{2,1,0:T(8,128)(2,1)S(1)} %pad_maximum_fusion.own_ref), channel_id=1, source_target_pairs={{0,1},{1,0},{2,3},{3,2},{4,5},{5,4},{6,7},{7,6},{8,9},{9,8},{10,11... | collective-permute-start | bytes 3145736 | tf_op jit(solution)/shard_map/ppermute | solution.py:21
  65.2 1.0 copy-start.3
  66.2 1.2 copy-start.4
  67.4 9.3 %copy-start.7 = (bf16[128,4096]{1,0:T(8,128)(2,1)S(1)}, bf16[128,4096]{1,0:T(8,128)(2,1)}, u32[]{:S(2)}) copy-start(bf16[128,4096]{1,0:T(8,128)(2,1)} %param.18) | copy-start | bytes 3145732
  71.7 22.6 %copy-start.8 = (bf16[128,4096]{1,0:T(8,128)(2,1)S(1)}, bf16[128,4096]{1,0:T(8,128)(2,1)}, u32[]{:S(2)}) copy-start(bf16[128,4096]{1,0:T(8,128)(2,1)} %param.20) | copy-start | bytes 3145732
  71.8 14.2 %collective-permute-start.5 = (bf16[64,1024]{1,0:T(8,128)(2,1)S(1)}, bf16[64,1024]{1,0:T(8,128)(2,1)S(1)}, u32[]{:S(2)}, u32[]{:S(2)}) collective-permute-start(bf16[64,1024]{1,0:T(8,128)(2,1)S(1)} %get-tuple-element.16), channel_id=1, source_target_pairs={{0,8},{8,16},{16,24},{24,0},{1,9},{9,17},{17,25},{25,1},{2,10},{10... | collective-permute-start | bytes 393224 | tf_op jit(solution)/shard_map/ppermute | solution.py:21
  72.6 14.6 %collective-permute-start.6 = (bf16[64,1024]{1,0:T(8,128)(2,1)S(1)}, bf16[64,1024]{1,0:T(8,128)(2,1)S(1)}, u32[]{:S(2)}, u32[]{:S(2)}) collective-permute-start(bf16[64,1024]{1,0:T(8,128)(2,1)S(1)} %get-tuple-element.18), channel_id=1, source_target_pairs={{0,24},{8,0},{16,8},{24,16},{1,25},{9,1},{17,9},{25,17},{2,26},{10... | collective-permute-start | bytes 393224 | tf_op jit(solution)/shard_map/ppermute | solution.py:21
  76.0 11.2 %collective-permute-start.7 = (bf16[64,1024]{1,0:T(8,128)(2,1)S(1)}, bf16[64,1024]{1,0:T(8,128)(2,1)S(1)}, u32[]{:S(2)}, u32[]{:S(2)}) collective-permute-start(bf16[64,1024]{1,0:T(8,128)(2,1)S(1)} %get-tuple-element.17), channel_id=1, source_target_pairs={{0,16},{8,24},{16,0},{24,8},{1,17},{9,25},{17,1},{25,9},{2,18},{10... | collective-permute-start | bytes 393224 | tf_op jit(solution)/shard_map/ppermute | solution.py:21
  77.2 55.8 %copy-start.2 = (bf16[3,4096,128]{2,1,0:T(8,128)(2,1)S(1)}, bf16[3,4096,128]{2,1,0:T(8,128)(2,1)}, u32[]{:S(2)}) copy-start(bf16[3,4096,128]{2,1,0:T(8,128)(2,1)} %own_ref.1) | copy-start | bytes 9437188
  87.3 7.9 %collective-permute-start.10 = (bf16[64,1024]{1,0:T(8,128)(2,1)S(1)}, bf16[64,1024]{1,0:T(8,128)(2,1)S(1)}, u32[]{:S(2)}, u32[]{:S(2)}) collective-permute-start(bf16[64,1024]{1,0:T(8,128)(2,1)S(1)} %add_convert_fusion), channel_id=1, source_target_pairs={{0,8},{8,16},{16,24},{24,0},{1,9},{9,17},{17,25},{25,1},{2,10},{10... | collective-permute-start | bytes 393224 | tf_op jit(solution)/shard_map/ppermute | solution.py:21
  90.4 6.3 %collective-permute-start.8 = (bf16[64,1024]{1,0:T(8,128)(2,1)S(1)}, bf16[64,1024]{1,0:T(8,128)(2,1)S(1)}, u32[]{:S(2)}, u32[]{:S(2)}) collective-permute-start(bf16[64,1024]{1,0:T(8,128)(2,1)S(1)} %add_convert_fusion), channel_id=1, source_target_pairs={{0,24},{8,0},{16,8},{24,16},{1,25},{9,1},{17,9},{25,17},{2,26},{10... | collective-permute-start | bytes 393224 | tf_op jit(solution)/shard_map/ppermute | solution.py:21
  92.0 13.6 %collective-permute-start.9 = (bf16[64,1024]{1,0:T(8,128)(2,1)S(1)}, bf16[64,1024]{1,0:T(8,128)(2,1)S(1)}, u32[]{:S(2)}, u32[]{:S(2)}) collective-permute-start(bf16[64,1024]{1,0:T(8,128)(2,1)S(1)} %add_convert_fusion), channel_id=1, source_target_pairs={{0,16},{8,24},{16,0},{24,8},{1,17},{9,25},{17,1},{25,9},{2,18},{10... | collective-permute-start | bytes 393224 | tf_op jit(solution)/shard_map/ppermute | solution.py:21
  105.7 14.9 %collective-permute-start.11 = (bf16[256,1024]{1,0:T(8,128)(2,1)S(1)}, bf16[256,1024]{1,0:T(8,128)(2,1)S(1)}, u32[]{:S(2)}, u32[]{:S(2)}) collective-permute-start(bf16[256,1024]{1,0:T(8,128)(2,1)S(1)} %pad_maximum_fusion.1.x0), channel_id=1, source_target_pairs={{0,6},{2,0},{4,2},{6,4},{1,7},{3,1},{5,3},{7,5},{8,14},{10,8},{12,... | collective-permute-start | bytes 1572872 | tf_op jit(solution)/shard_map/ppermute | solution.py:21
  107.2 16.4 %collective-permute-start.12 = (bf16[256,1024]{1,0:T(8,128)(2,1)S(1)}, bf16[256,1024]{1,0:T(8,128)(2,1)S(1)}, u32[]{:S(2)}, u32[]{:S(2)}) collective-permute-start(bf16[256,1024]{1,0:T(8,128)(2,1)S(1)} %pad_maximum_fusion.1.x0), channel_id=1, source_target_pairs={{0,4},{2,6},{4,0},{6,2},{1,5},{3,7},{5,1},{7,3},{8,12},{10,14},{12... | collective-permute-start | bytes 1572872 | tf_op jit(solution)/shard_map/ppermute | solution.py:21
  108.7 24.3 %collective-permute-start.13 = (bf16[256,1024]{1,0:T(8,128)(2,1)S(1)}, bf16[256,1024]{1,0:T(8,128)(2,1)S(1)}, u32[]{:S(2)}, u32[]{:S(2)}) collective-permute-start(bf16[256,1024]{1,0:T(8,128)(2,1)S(1)} %pad_maximum_fusion.1.x0), channel_id=1, source_target_pairs={{0,2},{2,4},{4,6},{6,0},{1,3},{3,5},{5,7},{7,1},{8,10},{10,12},{12... | collective-permute-start | bytes 1572872 | tf_op jit(solution)/shard_map/ppermute | solution.py:21
  108.7 1.3 collective-permute-start.15
  133.0 16.0 %copy-start.11 = (f32[1000]{0:T(1024)S(1)}, f32[1000]{0:T(1024)}, u32[]{:S(2)}) copy-start(f32[1000]{0:T(1024)} %param.13) | copy-start | bytes 12004
  139.6 21.4 %all-to-all-start.2 = ((f32[128,2,128]{2,1,0:T(2,128)}), f32[128,2,128]{2,1,0:T(2,128)S(1)}, u32[]{:S(2)}, u32[]{:S(2)}) async-start(f32[128,2,128]{2,1,0:T(2,128)} %bitcast.25), calls=%async_computation.2 | async-start | bytes 262144 | tf_op jit(solution)/shard_map/all_to_all | solution.py:336
  161.4 0.6 copy-start.10

commit v3 on v2

v3 whole, which is shorter than its diff:
```python
import math

import jax
import jax.numpy as jnp
from jax import lax
from jax.experimental import pallas as pl
from jax.experimental.pallas import tpu as pltpu
from jax.sharding import Mesh, PartitionSpec as P

STRIDE = 20
EPS = 1e-06
NX = 4
HD = 128
ORDER = (1, 3, 2)
BF = jnp.bfloat16
F32 = jnp.float32


def shift(value, axis, step):
    size = lax.axis_size(axis)
    return lax.ppermute(value, axis, [(i, (i + step) % size) for i in range(size)])


def time_embedding(step_now, model_width):
    half_width = model_width // 2
    positions = jnp.arange(half_width, dtype=F32)
    frequency = jnp.exp(positions * (-math.log(10000.0) / half_width))
    angles = step_now.astype(F32) * frequency
    return jnp.concatenate([jnp.sin(angles), jnp.cos(angles)])


def head_norm(values, gain):
    mean_square = jnp.mean(values * values, axis=-1, keepdims=True)
    return (values * gain * lax.rsqrt(mean_square + EPS)).astype(BF)


def weigh(scores, mask=None):
    e = jnp.exp(scores * (1.0 / math.sqrt(HD)))
    if mask is not None:
        e = jnp.where(mask, e, 0.0)
    return (e / jnp.sum(e, axis=-1, keepdims=True)).astype(BF)


def dot_t(a, b):
    return lax.dot_general(a, b, (((1,), (1,)), ((), ())), preferred_element_type=F32)


def dot(a, b):
    return jnp.dot(a, b, preferred_element_type=F32)


def reorder(count, source):
    row = lax.broadcasted_iota(jnp.int32, (count, count), 0)
    col = lax.broadcasted_iota(jnp.int32, (count, count), 1)
    return (col == source(row)).astype(BF)


def fold_kernel(embed_ref, temb_ref, gain_ref, weight_ref, fold_ref, bias_ref, acc):
    step = pl.program_id(0)

    @pl.when(step == 0)
    def _():
        acc[...] = jnp.zeros_like(acc)

    gain = gain_ref[...]
    scaled = embed_ref[...].astype(F32) * gain
    high = scaled.astype(BF)
    low = (scaled - high.astype(F32)).astype(BF)
    time = temb_ref[...] * gain
    time_high = time.astype(BF).astype(F32)
    row = lax.broadcasted_iota(jnp.int32, (16, time.shape[1]), 0)
    extra = jnp.where(row == 0, time_high, jnp.where(row == 1, time - time_high, 0.0)).astype(BF)
    weights = jnp.concatenate([weight_ref[i] for i in range(3)], axis=1)
    share = dot(jnp.concatenate([high, low], axis=0), weights)
    acc[:HD, :] += share[:HD] + share[HD:]
    share = dot(extra, weights)
    acc[HD:, :] += share

    @pl.when(step == pl.num_programs(0) - 1)
    def _():
        fold = acc[:HD, :]
        fold_high = fold.astype(BF)
        fold_ref[:HD, :] = fold_high
        fold_ref[HD:, :] = (fold - fold_high.astype(F32)).astype(BF)
        bias = acc[HD : HD + 1, :] + acc[HD + 1 : HD + 2, :]
        bias_ref[...] = jnp.broadcast_to(bias, bias_ref.shape)


def space_kernel(place_ref, lat_ref, embed_ref, temb_ref, fold_ref, bias_ref, gain_ref, out_ref):
    z_here = place_ref[1]
    core = place_ref[2]

    def source(row):
        z = (z_here + (row >> 2)) & 3
        frame = (row >> 8) & 1
        return ((((((z * 4 + (row & 3)) * 2 + ((row >> 4) & 1)) << 3) + ((row >> 5) & 7)) << 1) + frame)

    lat = dot(reorder(512, source), lat_ref[...]).astype(BF)
    width = embed_ref.shape[1]
    chunk = 256
    total = jnp.zeros((lat.shape[0], 128), F32)
    for start in range(0, width, chunk):
        first = dot(lat, embed_ref[:, start : start + chunk]) + temb_ref[:, start : start + chunk]
        first = first.astype(BF).astype(F32)
        square = first * first
        for lane in range(0, chunk, 128):
            total = total + square[:, lane : lane + 128]
    mean_square = jnp.sum(total, axis=-1, keepdims=True) * (1.0 / width)
    scale = lax.rsqrt(mean_square + EPS)
    proj = (dot(jnp.concatenate([lat, lat], axis=1), fold_ref[...]) + bias_ref[0:1, :]) * scale
    query = head_norm(proj[:, :HD], gain_ref[0:1, :])
    key = head_norm(proj[:, HD : 2 * HD], gain_ref[1:2, :])
    value = proj[:, 2 * HD :].astype(BF)
    parts = []
    for frame in range(2):
        rows = slice(frame * 256, (frame + 1) * 256)
        weights = weigh(dot_t(query[rows], key[rows]))
        parts.append(dot(weights, value[rows]).astype(BF))
    parts.append(jnp.where(core == 0, lat[:256], lat[256:]))
    for tm in range(8):
        for side in range(2):
            rows = slice(tm * 32 + side * 16, tm * 32 + side * 16 + 16)
            message = jnp.concatenate([part[rows] for part in parts], axis=0)
            for x in range(NX):
                start = ((tm * NX + x) * 2 + side) * 48
                out_ref[start : start + 48, :] = message


def output_kernel(
    place_ref, att_ref, embed_ref, temb_ref, own_ref, other_ref, out_ref, base_ref, att_own_ref, lhs_own, lhs_other, lat
):
    @pl.when(pl.program_id(0) == 0)
    def _():
        x_here = place_ref[0]
        core = place_ref[2]
        swap = reorder(256, lambda row: ((row & 15) << 4) + (row >> 4))

        def part(x, side, first, count):
            starts = [((tm * NX + x) * 2 + side) * 48 + first for tm in range(8)]
            return jnp.concatenate([att_ref[start : start + count, :] for start in starts], axis=0)

        for x in range(NX):
            rows = jnp.concatenate([part(x, side, 0, 32) for side in range(2)], axis=1)
            rows = dot(swap, rows).astype(BF)
            slot = pl.multiple_of(((x - x_here) & 3) * HD, HD)
            lhs_own[:, pl.ds(slot, HD)] = jnp.where(core == 0, rows[:, :HD], rows[:, HD:])
            lhs_other[:, pl.ds(slot, HD)] = jnp.where(core == 0, rows[:, HD:], rows[:, :HD])

            @pl.when(x == x_here)
            def _(rows=rows):
                att_own_ref[...] = rows

        rows = jnp.concatenate(
            [
                att_ref[(tm * NX * 2 + side) * 48 + 32 : (tm * NX * 2 + side) * 48 + 48, :]
                for tm in range(8)
                for side in range(2)
            ],
            axis=0,
        )
        lat[...] = dot(swap[:64, :], rows).astype(BF)

    width = own_ref.shape[2]
    own = own_ref[...].reshape(NX * HD, width)
    other = other_ref[...].reshape(NX * HD, width)
    share = (dot(lhs_own[...], own) + dot(lhs_other[...], other)).astype(BF)
    out_ref[...] = share[64:, :]
    first = (dot(lat[...], embed_ref[...]) + temb_ref[...]).astype(BF)
    base_ref[...] = first.astype(F32) + share[:64, :].astype(F32)


def project_block(rows, gain_ref, own_ref, other_ref, total, add):
    rows = rows.astype(F32)
    square = rows * rows
    for lane in range(0, rows.shape[1], 128):
        total = total + square[:, lane : lane + 128]
    gained = (rows * gain_ref[0]).astype(BF)
    for index in range(3):
        pair = jnp.concatenate([own_ref[index], other_ref[index]], axis=1)
        add(index, dot(gained, pair))
    return total


def time_project_kernel(
    place_ref, a0, b0, a1, b1, a3, b3, gain_ref, own_ref, other_ref, proj_ref, total_ref
):
    step = pl.program_id(0)

    @pl.when(step == 0)
    def _():
        proj_ref[...] = jnp.zeros_like(proj_ref)
        total_ref[...] = jnp.zeros_like(total_ref)

    for k, (a, b) in enumerate(((a0, b0), (a1, b1), (a3, b3))):

        @pl.when(step == k)
        def _(a=a, b=b):
            def add(index, value):
                proj_ref[:, index * 2 * HD : (index + 1) * 2 * HD] += value

            rows = jnp.concatenate([a[...], b[...]], axis=0)
            total_ref[...] = project_block(rows, gain_ref, own_ref, other_ref, total_ref[...], add)


def time_kernel(
    place_ref, a2, b2, gain_ref, own_ref, other_ref, proj_ref, total_ref, head_gain_ref, att_ref, fold_ref, out_ref
):
    parts = {}

    def add(index, value):
        parts[index] = proj_ref[:, index * 2 * HD : (index + 1) * 2 * HD] + value

    rows = jnp.concatenate([a2[...], b2[...]], axis=0)
    total = project_block(rows, gain_ref, own_ref, other_ref, total_ref[...], add)
    z_here = place_ref[1]
    width = NX * a2.shape[1]
    mean_square = jnp.sum(total, axis=-1, keepdims=True) * (1.0 / width)
    scale = lax.rsqrt(mean_square + EPS)
    count = rows.shape[0]
    row_patch = lax.broadcasted_iota(jnp.int32, (count, count), 0) >> 4
    col_patch = lax.broadcasted_iota(jnp.int32, (count, count), 1) >> 4
    mask = row_patch == col_patch
    columns = [att_ref[...]]
    for side in range(2):
        query, key, value = [parts[index][:, side * HD : (side + 1) * HD] * scale for index in range(3)]
        query = head_norm(query, head_gain_ref[2:3, :])
        key = head_norm(key, head_gain_ref[3:4, :])
        weights = weigh(dot_t(query, key), mask)
        columns.append(dot(weights, value.astype(BF)).astype(BF))

    def source(row):
        z = (((row >> 3) & 3) - z_here) & 3
        return (z << 6) + (((row >> 1) & 3) << 4) + ((row >> 5) << 1) + (row & 1)

    both = dot(reorder(count, source), jnp.concatenate(columns, axis=1)).astype(BF)
    out_ref[...] = dot(both, fold_ref[...])


def body(
    latents,
    timestep,
    alpha_table,
    norm_gain,
    head_gain,
    embed_weight,
    space_project,
    space_output,
    time_project,
    time_output,
    noise_weight,
):
    width = embed_weight.shape[1]
    block = width // NX
    core = lax.axis_index("c")
    place = lax.axis_index("x")
    places = jnp.stack([place, lax.axis_index("zh"), core]).astype(jnp.int32)
    step_now = timestep[0]
    positions = jnp.arange(alpha_table.shape[0], dtype=jnp.int32)
    alpha_now = jnp.sum(jnp.where(positions == step_now, alpha_table, 0.0))
    alpha_next = jnp.sum(jnp.where(positions == step_now + STRIDE, alpha_table, 0.0))
    temb = time_embedding(step_now, width)[None, :]

    def in_order(own, other):
        first = jnp.where(core == 0, own, other)
        second = jnp.where(core == 0, other, own)
        return jnp.stack([first, second])

    lat_bf = latents.astype(BF)
    lat_rows = jnp.broadcast_to(lat_bf.reshape(1, 16, HD), (32, 16, HD)).reshape(512, HD)
    lat_rows = lax.all_to_all(lat_rows, ("zh", "x", "c"), split_axis=0, concat_axis=0, tiled=True)

    def whole(*shape):
        return pl.BlockSpec(shape, lambda i, s: (0,) * len(shape))

    chunk = 512
    fold, bias = pl.pallas_call(
        fold_kernel,
        out_shape=(jax.ShapeDtypeStruct((2 * HD, 3 * HD), BF), jax.ShapeDtypeStruct((8, 3 * HD), F32)),
        grid=(width // chunk,),
        in_specs=[
            pl.BlockSpec((HD, chunk), lambda i: (0, i)),
            pl.BlockSpec((1, chunk), lambda i: (0, i)),
            pl.BlockSpec((1, chunk), lambda i: (0, i)),
            pl.BlockSpec((3, chunk, HD), lambda i: (0, i, 0)),
        ],
        out_specs=[
            pl.BlockSpec((2 * HD, 3 * HD), lambda i: (0, 0)),
            pl.BlockSpec((8, 3 * HD), lambda i: (0, 0)),
        ],
        scratch_shapes=[pltpu.VMEM((HD + 16, 3 * HD), F32)],
        compiler_params=pltpu.CompilerParams(vmem_limit_bytes=16 * 1024 * 1024),
        cost_estimate=pl.CostEstimate(flops=2 * 272 * 4096 * 384, bytes_accessed=5 << 20, transcendentals=0),
        name="fold_projection",
    )(embed_weight, temb, norm_gain[0:1], space_project)

    pieces = [
        lax.dynamic_slice(space_output, (0, ((place - d) % NX) * block), (HD, block)) for d in range(NX)
    ]
    got = {d: shift(pieces[d], "x", -d) for d in ORDER}
    out_own = jnp.stack([pieces[0]] + [got[d] for d in range(1, NX)])
    lat_rows, out_own = lax.optimization_barrier((lat_rows, out_own))
    out_other = shift(out_own, "c", 1)
    time_other = shift(time_project, "c", 1)
    noise_fold = jnp.concatenate(
        [dot(space_output, noise_weight).astype(BF), dot(time_output, noise_weight).astype(BF)]
    )
    noise_other = shift(noise_fold, "c", 1)
    noise_fold = jnp.concatenate(
        [in_order(noise_fold[:HD], noise_other[:HD]).reshape(2 * HD, HD), noise_fold[HD:], noise_other[HD:]]
    )

    attended = pl.pallas_call(
        space_kernel,
        out_shape=jax.ShapeDtypeStruct((64 * 48, HD), BF),
        grid_spec=pltpu.PrefetchScalarGridSpec(
            num_scalar_prefetch=1,
            grid=(1,),
            in_specs=[
                whole(512, HD),
                whole(HD, width),
                whole(1, width),
                whole(2 * HD, 3 * HD),
                whole(8, 3 * HD),
                whole(4, HD),
            ],
            out_specs=whole(64 * 48, HD),
        ),
        compiler_params=pltpu.CompilerParams(vmem_limit_bytes=32 * 1024 * 1024),
        name="space_attention",
    )(places, lat_rows, embed_weight, temb, fold, bias, head_gain)

    attended, out_other, noise_fold = lax.optimization_barrier((attended, out_other, noise_fold))
    regrouped = lax.all_to_all(attended, ("y", "zl", "x", "c"), split_axis=0, concat_axis=0, tiled=True)

    tiles = 4
    tile = block // tiles
    share, base, att_own = pl.pallas_call(
        output_kernel,
        out_shape=(
            jax.ShapeDtypeStruct((192, block), BF),
            jax.ShapeDtypeStruct((64, block), F32),
            jax.ShapeDtypeStruct((256, 2 * HD), BF),
        ),
        grid_spec=pltpu.PrefetchScalarGridSpec(
            num_scalar_prefetch=1,
            grid=(tiles,),
            in_specs=[
                whole(64 * 48, HD),
                pl.BlockSpec((HD, tile), lambda i, s: (0, s[0] * tiles + i)),
                pl.BlockSpec((1, tile), lambda i, s: (0, s[0] * tiles + i)),
                pl.BlockSpec((NX, HD, tile), lambda i, s: (0, 0, i)),
                pl.BlockSpec((NX, HD, tile), lambda i, s: (0, 0, i)),
            ],
            out_specs=[
                pl.BlockSpec((192, tile), lambda i, s: (0, i)),
                pl.BlockSpec((64, tile), lambda i, s: (0, i)),
                whole(256, 2 * HD),
            ],
            scratch_shapes=[
                pltpu.VMEM((256, NX * HD), BF),
                pltpu.VMEM((256, NX * HD), BF),
                pltpu.VMEM((64, HD), BF),
            ],
        ),
        compiler_params=pltpu.CompilerParams(vmem_limit_bytes=32 * 1024 * 1024),
        name="space_output",
    )(places, regrouped, embed_weight, temb, out_own, out_other)

    sent = {d: shift(share[64 * (d - 1) : 64 * d], "zh", d) for d in ORDER}
    for d in ORDER:
        base = base + sent[d].astype(F32)
    second = base.astype(BF)
    got = {d: shift(second, "zh", -d) for d in ORDER}
    near = jnp.concatenate([second, got[1]])
    far = jnp.concatenate([got[2], got[3]])
    near_3 = shift(near, "x", 1)
    near_1 = shift(near, "x", -1)
    far_1 = shift(far, "x", -1)
    far_3 = shift(far, "x", 1)
    near_2 = shift(near_3, "x", 1)
    far_2 = shift(far_1, "x", -1)

    half = whole(128, block)

    def time_specs(place_of):
        weights = pl.BlockSpec((3, block, HD), lambda i, s: (0, (s[0] + place_of(i)) % NX, 0))
        return [pl.BlockSpec((1, 1, block), lambda i, s: ((s[0] + place_of(i)) % NX, 0, 0)), weights, weights]

    time_weights = (norm_gain[1].reshape(NX, 1, block), time_project, time_other)
    proj, total = pl.pallas_call(
        time_project_kernel,
        out_shape=(jax.ShapeDtypeStruct((256, 6 * HD), F32), jax.ShapeDtypeStruct((256, HD), F32)),
        grid_spec=pltpu.PrefetchScalarGridSpec(
            num_scalar_prefetch=1,
            grid=(NX - 1,),
            in_specs=[half] * 6 + time_specs(lambda i: i + i // 2),
            out_specs=[whole(256, 6 * HD), whole(256, HD)],
        ),
        compiler_params=pltpu.CompilerParams(vmem_limit_bytes=32 * 1024 * 1024),
        cost_estimate=pl.CostEstimate(flops=2 * 256 * 3072 * 768, bytes_accessed=8 << 20, transcendentals=0),
        name="time_projection",
    )(places, near, far, near_1, far_1, near_3, far_3, *time_weights)
    noise = pl.pallas_call(
        time_kernel,
        out_shape=jax.ShapeDtypeStruct((256, HD), F32),
        grid_spec=pltpu.PrefetchScalarGridSpec(
            num_scalar_prefetch=1,
            grid=(1,),
            in_specs=[half] * 2
            + time_specs(lambda i: 2)
            + [whole(256, 6 * HD), whole(256, HD), whole(4, HD), whole(256, 2 * HD), whole(4 * HD, HD)],
            out_specs=whole(256, HD),
        ),
        compiler_params=pltpu.CompilerParams(vmem_limit_bytes=32 * 1024 * 1024),
        name="time_attention",
    )(places, near_2, far_2, *time_weights, proj, total, head_gain, att_own, noise_fold)

    noise = lax.all_to_all(noise, ("y", "zl", "zh", "x"), split_axis=0, concat_axis=0, tiled=True)
    total = jnp.sum(noise.reshape(8, 16, 2, HD), axis=1).reshape(16, HD)

    own_first = (dot(lat_bf.reshape(16, HD), embed_weight) + temb).astype(BF)
    predicted_noise = (total + dot(own_first, noise_weight)).reshape(latents.shape)
    latents_next = (
        jnp.sqrt(alpha_next)
        * (latents - jnp.sqrt(1.0 - alpha_now) * predicted_noise)
        / jnp.sqrt(alpha_now)
        + jnp.sqrt(1.0 - alpha_next) * predicted_noise
    )
    return (predicted_noise, latents_next)


def solution(mesh):
    fine = Mesh(mesh.devices.reshape(4, 2, 4, 4, 2), ("y", "zl", "zh", "x", "c"))
    space = ("zh", "x", "c")
    rows = P(space, ("y", "zl"), None)
    placed = (
        rows,
        P(),
        P(),
        P(),
        P(),
        P(),
        P(None, None, space),
        P(space, None),
        P(None, None, space),
        P(space, None),
        P(),
    )
    return jax.shard_map(
        body,
        mesh=fine,
        in_specs=placed,
        out_specs=(rows, rows),
        check_vma=False,
    )
```

time: 163 us -> 141 us (0.87)
  waiting for transfers between devices: 84.5 us -> 44.1 us
  blocking collectives: 0 us -> 20.6 us
  starting transfers between devices: 47.2 us -> 42.7 us
  Pallas kernels: 13.8 us -> 18 us
  matrix products: 4.2 us -> 2.54 us
    ppermute x16 -> x18, waiting for transfers between devices: 66.1 us -> 29.6 us  [shift(): lax.ppermute(value, axis, [(i, (i + step) % size) for i in range(size)])]
    all_to_all x0 -> x1, blocking collectives: none -> 20.6 us  [body(): lax.all_to_all(attended, ('y', 'zl', 'x', 'c'), split_axis=0, concat_axis...]
    pallas_call x1 -> x3, Pallas kernels: 2.95 us -> 10.5 us  [the longest x1 4.67 us: body(): pl.pallas_call(time_project_kernel, out_shape=(jax.ShapeDtypeStruct((256,...]
    all_to_all x1 -> x0, starting transfers between devices: 6.72 us -> none  [body(): lax.all_to_all(attended, ('y', 'zl', 'x', 'c'), split_axis=0, concat_axis...]
    all_to_all x1, waiting for transfers between devices: 9.73 us -> 5.96 us  [body(): lax.all_to_all(lat_rows, ('zh', 'x', 'c'), split_axis=0, concat_axis=0, t...]
    ppermute x16 -> x18, starting transfers between devices: 19.8 us -> 22.8 us  [shift(): lax.ppermute(value, axis, [(i, (i + step) % size) for i in range(size)])]
    pallas_call x1, Pallas kernels: 6.61 us -> 4.14 us  [body(): pl.pallas_call(time_kernel, out_shape=jax.ShapeDtypeStruct((256, HD), F32...]
    convert_element_type x4 -> x0, other arithmetic: 2.32 us -> none  [the longest x1 1.42 us: body(): (embed_weight.astype(F32) * norm_gain[0:1]).astype(BF)]
  transfers between devices with their start and end apart: 19 -> 20, of which waited for: 15 -> 11; matrix products, arithmetic and copies ran while one was open for 2% -> 4% of each run, Pallas kernels for 3% -> 10%
where the time goes in v3:
time: 141 us
  waiting for transfers between devices  44.1 us (31%)
  starting transfers between devices  42.7 us (30%)
  blocking collectives  20.6 us (15%)
  Pallas kernels  18 us (13%)
  local copies, waits for them, and re-layouts  5 us (4%)
  between operations  4.44 us (3%)
  other arithmetic  3.54 us (3%)
  matrix products  2.54 us (2%)
    ppermute x18, waiting for transfers between devices, shift(): lax.ppermute(value, axis, [(i, (i + step) % size) for i in range(size)])  29.6 us
    ppermute x18, starting transfers between devices, shift(): lax.ppermute(value, axis, [(i, (i + step) % size) for i in range(size)])  22.8 us
    all_to_all x1, blocking collectives, body(): lax.all_to_all(attended, ('y', 'zl', 'x', 'c'), split_axis=0, concat_axis...  20.6 us
    all_to_all x1, starting transfers between devices, body(): lax.all_to_all(lat_rows, ('zh', 'x', 'c'), split_axis=0, concat_axis=0, t...  10.6 us
    all_to_all x1, starting transfers between devices, body(): lax.all_to_all(noise, ('y', 'zl', 'zh', 'x'), split_axis=0, concat_axis=0...  9.27 us
    all_to_all x1, waiting for transfers between devices, body(): lax.all_to_all(noise, ('y', 'zl', 'zh', 'x'), split_axis=0, concat_axis=0...  8.53 us
    all_to_all x1, waiting for transfers between devices, body(): lax.all_to_all(lat_rows, ('zh', 'x', 'c'), split_axis=0, concat_axis=0, t...  5.96 us
    pallas_call x1, Pallas kernels, body(): pl.pallas_call(time_project_kernel, out_shape=(jax.ShapeDtypeStruct((256,...  4.67 us
  transfers between devices with their start and end apart: 20, of which 11 were waited for; matrix products, arithmetic and copies ran while one was open for 4% of the time, Pallas kernels for 10%

profile of v3, /device:TPU:8, one launch (start us, length us, event | category | flops | bytes accessed | tf_op | source)
XLA Modules:
  0.0 140.9 jit_solution(14121070238836130453)
XLA Ops:
  0.6 0.0 copy-start
  0.7 2.3 %dynamic-slice_bitcast_fusion = (bf16[1,128,1024]{2,1,0:T(8,128)(2,1)}, bf16[128,1024]{1,0:T(8,128)(2,1)}, bf16[128,1024]{1,0:T(8,128)(2,1)}, bf16[128,1024]{1,0:T(8,128)(2,1)}) fusion(bf16[128,4096]{1,0:T(8,128)(2,1)} %param.18, s32[]{:T(128)S(6)} %select_n.51, s32[]{:T(128)S(6)} %select_n.55, s32[]{:T(128)S(6)} %select_n.53, s32[]{:T(128)S(6)} %select_n.57), kind=kLoop, calls=%fused_computation.9 | loop fusion | bytes 2097168 | tf_op jit(solution)/shard_map/stack | solution.py:300
  3.0 2.8 %collective-permute-start = (bf16[128,1024]{1,0:T(8,128)(2,1)}, bf16[128,1024]{1,0:T(8,128)(2,1)}, u32[]{:S(2)}, u32[]{:S(2)}) collective-permute-start(bf16[128,1024]{1,0:T(8,128)(2,1)} %get-tuple-element.30), channel_id=1, source_target_pairs={{0,6},{2,0},{4,2},{6,4},{1,7},{3,1},{5,3},{7,5},{8,14},{10,8},{12,... | collective-permute-start | bytes 786440 | tf_op jit(solution)/shard_map/ppermute | solution.py:21
  5.8 0.8 collective-permute-start.1
  6.6 0.9 collective-permute-start.2
  7.5 0.7 convert_element_type.27
  8.2 0.7 broadcast_in_dim.16
  8.9 10.6 %all-to-all-start = ((bf16[32,16,128]{2,1,0:T(8,128)(2,1)}), bf16[32,16,128]{2,1,0:T(8,128)(2,1)S(1)}, u32[]{:S(2)}, u32[]{:S(2)}) async-start(bf16[32,16,128]{2,1,0:T(8,128)(2,1)} %broadcast_in_dim.16), calls=%async_computation | async-start | bytes 262144 | tf_op jit(solution)/shard_map/all_to_all | solution.py:270
  19.5 0.0 copy-start.6
  19.5 0.0 copy-start.1
  19.6 1.7 %convolution_convert_fusion.1 = bf16[128,128]{1,0:T(8,128)(2,1)S(1)} fusion(bf16[128,4096]{1,0:T(8,128)(2,1)} %param.18, bf16[4096,128]{1,0:T(8,128)(2,1)S(1)} %copy-done), kind=kOutput, calls=%fused_computation.4 | convolution fusion | flops 134234112 | bytes 2129920 | tf_op jit(solution)/shard_map/dot_general | solution.py:49
  21.3 0.4 convolution_convert_fusion
  21.8 0.4 collective-permute-start.4
  22.1 0.2 collective-permute-start.15
  23.0 0.1 fusion.4
  23.1 0.1 pad_add_fusion.place_ref
  23.2 0.0 collective-permute-done
  23.2 0.0 collective-permute-done.1
  23.2 0.0 collective-permute-done.2
  23.2 0.0 copy-start.3
  23.2 1.3 pad_maximum_fusion.own_ref
  24.5 6.0 %all-to-all-done = bf16[32,16,128]{2,1,0:T(8,128)(2,1)S(1)} async-done(((bf16[32,16,128]{2,1,0:T(8,128)(2,1)}), bf16[32,16,128]{2,1,0:T(8,128)(2,1)S(1)}, u32[]{:S(2)}, u32[]{:S(2)}) %all-to-all-start) | async-done | bytes 131104 | tf_op jit(solution)/shard_map/all_to_all | solution.py:270
  30.5 0.3 collective-permute-start.3
  30.8 0.0 copy-start.2
  30.8 1.9 %copy-done.2 = bf16[3,4096,128]{2,1,0:T(8,128)(2,1)S(1)} copy-done((bf16[3,4096,128]{2,1,0:T(8,128)(2,1)S(1)}, bf16[3,4096,128]{2,1,0:T(8,128)(2,1)}, u32[]{:S(2)}) %copy-start.2) | copy-done | bytes 3145752
  32.7 3.0 %fold_projection.1 = (bf16[256,384]{1,0:T(8,128)(2,1)S(1)}, f32[8,384]{1,0:T(8,128)S(1)}) custom-call(bf16[128,4096]{1,0:T(8,128)(2,1)S(1)} %copy-done.1, f32[1,4096]{1,0:T(1,128)S(1)} %bitcast.41, f32[1,4096]{1,0:T(1,128)S(1)} %get-tuple-element.39.gain_ref, bf16[3,4096,128]{2,1,0:T(8,128)(2,1)S(1)} %copy-done.2), custom_call_target="tpu_custom_call" | custom-call | flops 855638016 | bytes 5242880 | tf_op jit(solution)/shard_map/fold_projection/pallas_call | solution.py:276
  35.8 2.9 %space_attention.1 = bf16[3072,128]{1,0:T(8,128)(2,1)S(1)} custom-call(s32[3]{0:T(128)S(1)} %pad_add_fusion.place_ref, bf16[512,128]{1,0:T(8,128)(2,1)S(1)} %bitcast.40, bf16[128,4096]{1,0:T(8,128)(2,1)S(1)} %copy-done.1, f32[1,4096]{1,0:T(1,128)S(1)} %bitcast.42, bf16[256,384]{1,0:T(8,128)(2,1)S(1)} %get-tuple-element.15.fold_ref, ...), custom_call_target="tpu_custom_call" | custom-call | tf_op jit(solution)/shard_map/space_attention/pallas_call | solution.py:312
  38.7 20.6 %all_to_all.29 = bf16[64,48,128]{2,1,0:T(8,128)(2,1)S(1)} all-to-all(bf16[64,48,128]{2,1,0:T(8,128)(2,1)S(1)} %bitcast.38), channel_id=1, replica_groups=mesh['y'=4,'zl'=2,'zh'=4,'x'=4,'c'=2] {'y','zl','x','c'}, dimensions={0} | all-to-all | bytes 1572864 | tf_op jit(solution)/shard_map/all_to_all | solution.py:333
  59.3 3.4 %space_output.1 = (bf16[192,1024]{1,0:T(8,128)(2,1)S(1)}, f32[64,1024]{1,0:T(8,128)S(1)}, bf16[256,256]{1,0:T(8,128)(2,1)S(1)}) custom-call(s32[3]{0:T(128)S(1)} %pad_add_fusion.place_ref, bf16[3072,128]{1,0:T(8,128)(2,1)S(1)} %bitcast.39, bf16[128,4096]{1,0:T(8,128)(2,1)S(1)} %copy-done.1, f32[1,4096]{1,0:T(1,128)S(1)} %bitcast.43, ...), custom_call_target="tpu_custom_call" | custom-call | tf_op jit(solution)/shard_map/space_output/pallas_call | solution.py:337
  62.7 0.8 collective-permute-start.5
  63.5 3.4 %collective-permute-start.6 = (bf16[64,1024]{1,0:T(8,128)(2,1)S(1)}, bf16[64,1024]{1,0:T(8,128)(2,1)S(1)}, u32[]{:S(2)}, u32[]{:S(2)}) collective-permute-start(bf16[64,1024]{1,0:T(8,128)(2,1)S(1)} %get-tuple-element.34), channel_id=1, source_target_pairs={{0,24},{8,0},{16,8},{24,16},{1,25},{9,1},{17,9},{25,17},{2,26},{10... | collective-permute-start | bytes 393224 | tf_op jit(solution)/shard_map/ppermute | solution.py:21
  66.9 1.5 %collective-permute-start.7 = (bf16[64,1024]{1,0:T(8,128)(2,1)S(1)}, bf16[64,1024]{1,0:T(8,128)(2,1)S(1)}, u32[]{:S(2)}, u32[]{:S(2)}) collective-permute-start(bf16[64,1024]{1,0:T(8,128)(2,1)S(1)} %get-tuple-element.33), channel_id=1, source_target_pairs={{0,16},{8,24},{16,0},{24,8},{1,17},{9,25},{17,1},{25,9},{2,18},{10... | collective-permute-start | bytes 393224 | tf_op jit(solution)/shard_map/ppermute | solution.py:21
  68.3 3.3 %collective-permute-done.5 = bf16[64,1024]{1,0:T(8,128)(2,1)S(1)} collective-permute-done((bf16[64,1024]{1,0:T(8,128)(2,1)S(1)}, bf16[64,1024]{1,0:T(8,128)(2,1)S(1)}, u32[]{:S(2)}, u32[]{:S(2)}) %collective-permute-start.5) | collective-permute-done | bytes 131104 | tf_op jit(solution)/shard_map/ppermute | solution.py:21
  71.7 3.4 %collective-permute-done.6 = bf16[64,1024]{1,0:T(8,128)(2,1)S(1)} collective-permute-done((bf16[64,1024]{1,0:T(8,128)(2,1)S(1)}, bf16[64,1024]{1,0:T(8,128)(2,1)S(1)}, u32[]{:S(2)}, u32[]{:S(2)}) %collective-permute-start.6) | collective-permute-done | bytes 131104 | tf_op jit(solution)/shard_map/ppermute | solution.py:21
  75.1 3.4 %collective-permute-done.7 = bf16[64,1024]{1,0:T(8,128)(2,1)S(1)} collective-permute-done((bf16[64,1024]{1,0:T(8,128)(2,1)S(1)}, bf16[64,1024]{1,0:T(8,128)(2,1)S(1)}, u32[]{:S(2)}, u32[]{:S(2)}) %collective-permute-start.7) | collective-permute-done | bytes 131104 | tf_op jit(solution)/shard_map/ppermute | solution.py:21
  78.5 0.1 add_convert_fusion
  78.6 2.2 %collective-permute-start.11 = (bf16[64,1024]{1,0:T(8,128)(2,1)S(1)}, bf16[64,1024]{1,0:T(8,128)(2,1)S(1)}, u32[]{:S(2)}, u32[]{:S(2)}) collective-permute-start(bf16[64,1024]{1,0:T(8,128)(2,1)S(1)} %add_convert_fusion), channel_id=1, source_target_pairs={{0,16},{8,24},{16,0},{24,8},{1,17},{9,25},{17,1},{25,9},{2,18},{10... | collective-permute-start | bytes 393224 | tf_op jit(solution)/shard_map/ppermute | solution.py:21
  80.7 4.2 %collective-permute-start.12 = (bf16[64,1024]{1,0:T(8,128)(2,1)S(1)}, bf16[64,1024]{1,0:T(8,128)(2,1)S(1)}, u32[]{:S(2)}, u32[]{:S(2)}) collective-permute-start(bf16[64,1024]{1,0:T(8,128)(2,1)S(1)} %add_convert_fusion), channel_id=1, source_target_pairs={{0,8},{8,16},{16,24},{24,0},{1,9},{9,17},{17,25},{25,1},{2,10},{10... | collective-permute-start | bytes 393224 | tf_op jit(solution)/shard_map/ppermute | solution.py:21
  84.9 0.0 collective-permute-start.8
  84.9 5.5 %collective-permute-done.11 = bf16[64,1024]{1,0:T(8,128)(2,1)S(1)} collective-permute-done((bf16[64,1024]{1,0:T(8,128)(2,1)S(1)}, bf16[64,1024]{1,0:T(8,128)(2,1)S(1)}, u32[]{:S(2)}, u32[]{:S(2)}) %collective-permute-start.11) | collective-permute-done | bytes 131104 | tf_op jit(solution)/shard_map/ppermute | solution.py:21
  90.4 0.8 collective-permute-done.12
  91.3 0.5 collective-permute-start.13
  91.8 3.0 %collective-permute-done.8 = bf16[64,1024]{1,0:T(8,128)(2,1)S(1)} collective-permute-done((bf16[64,1024]{1,0:T(8,128)(2,1)S(1)}, bf16[64,1024]{1,0:T(8,128)(2,1)S(1)}, u32[]{:S(2)}, u32[]{:S(2)}) %collective-permute-start.8) | collective-permute-done | bytes 131104 | tf_op jit(solution)/shard_map/ppermute | solution.py:21
  94.7 0.1 collective-permute-start.9
  94.8 1.5 %collective-permute-start.17 = (bf16[128,1024]{1,0:T(8,128)(2,1)S(1)}, bf16[128,1024]{1,0:T(8,128)(2,1)S(1)}, u32[]{:S(2)}, u32[]{:S(2)}) collective-permute-start(bf16[128,1024]{1,0:T(8,128)(2,1)S(1)} %constant_dynamic-update-slice_fusion.b0), channel_id=1, source_target_pairs={{0,2},{2,4},{4,6},{6,0},{1,3},{3,5},{5,7},{7,1},{8,10},{10,12},{12... | collective-permute-start | bytes 786440 | tf_op jit(solution)/shard_map/ppermute | solution.py:21
  96.3 1.8 %collective-permute-start.16 = (bf16[128,1024]{1,0:T(8,128)(2,1)S(1)}, bf16[128,1024]{1,0:T(8,128)(2,1)S(1)}, u32[]{:S(2)}, u32[]{:S(2)}) collective-permute-start(bf16[128,1024]{1,0:T(8,128)(2,1)S(1)} %pad_maximum_fusion.1.a0), channel_id=1, source_target_pairs={{0,6},{2,0},{4,2},{6,4},{1,7},{3,1},{5,3},{7,5},{8,14},{10,8},{12,... | collective-permute-start | bytes 786440 | tf_op jit(solution)/shard_map/ppermute | solution.py:21
  98.1 1.8 %collective-permute-done.13.b1 = bf16[128,1024]{1,0:T(8,128)(2,1)S(1)} collective-permute-done((bf16[128,1024]{1,0:T(8,128)(2,1)S(1)}, bf16[128,1024]{1,0:T(8,128)(2,1)S(1)}, u32[]{:S(2)}, u32[]{:S(2)}) %collective-permute-start.13) | collective-permute-done | bytes 262176 | tf_op jit(solution)/shard_map/ppermute | solution.py:21
  99.9 1.5 %collective-permute-start.14 = (bf16[128,1024]{1,0:T(8,128)(2,1)S(1)}, bf16[128,1024]{1,0:T(8,128)(2,1)S(1)}, u32[]{:S(2)}, u32[]{:S(2)}) collective-permute-start(bf16[128,1024]{1,0:T(8,128)(2,1)S(1)} %collective-permute-done.13.b1), channel_id=1, source_target_pairs={{0,6},{2,0},{4,2},{6,4},{1,7},{3,1},{5,3},{7,5},{8,14},{10,8},{12,... | collective-permute-start | bytes 786440 | tf_op jit(solution)/shard_map/ppermute | solution.py:21
  101.4 3.8 %collective-permute-done.9.a3 = bf16[128,1024]{1,0:T(8,128)(2,1)S(1)} collective-permute-done((bf16[128,1024]{1,0:T(8,128)(2,1)S(1)}, bf16[128,1024]{1,0:T(8,128)(2,1)S(1)}, u32[]{:S(2)}, u32[]{:S(2)}) %collective-permute-start.9) | collective-permute-done | bytes 262176 | tf_op jit(solution)/shard_map/ppermute | solution.py:21
  105.3 0.0 collective-permute-start.10
  105.3 0.0 collective-permute-done.15.other_ref
  105.3 4.5 %collective-permute-done.17.b3 = bf16[128,1024]{1,0:T(8,128)(2,1)S(1)} collective-permute-done((bf16[128,1024]{1,0:T(8,128)(2,1)S(1)}, bf16[128,1024]{1,0:T(8,128)(2,1)S(1)}, u32[]{:S(2)}, u32[]{:S(2)}) %collective-permute-start.17) | collective-permute-done | bytes 262176 | tf_op jit(solution)/shard_map/ppermute | solution.py:21
  109.8 0.0 collective-permute-done.16.a1
  109.8 4.7 %time_projection.1 = (f32[256,768]{1,0:T(8,128)S(1)}, f32[256,128]{1,0:T(8,128)S(1)}) custom-call(s32[3]{0:T(128)S(1)} %pad_add_fusion.place_ref, bf16[128,1024]{1,0:T(8,128)(2,1)S(1)} %pad_maximum_fusion.1.a0, bf16[128,1024]{1,0:T(8,128)(2,1)S(1)} %constant_dynamic-update-slice_fusion.b0, bf16[128,1024]{1,0:T(8,128)(2,1)S(1)} %collective-permute-done.16.a1, ...), custom_call_target="tpu_custom_call" | custom-call | flops 1207959552 | bytes 8388608 | tf_op jit(solution)/shard_map/time_projection/pallas_call | solution.py:390
  114.4 0.0 collective-permute-done.14.b2
  114.5 0.0 copy-start.8
  114.5 0.0 copy-start.7
  114.5 4.1 %time_attention.1 = f32[256,128]{1,0:T(8,128)} custom-call(s32[3]{0:T(128)S(1)} %pad_add_fusion.place_ref, bf16[128,1024]{1,0:T(8,128)(2,1)S(1)} %collective-permute-done.10.a2, bf16[128,1024]{1,0:T(8,128)(2,1)S(1)} %collective-permute-done.14.b2, f32[4,1,1024]{2,1,0:T(1,128)S(1)} %bitcast.45, bf16[3,4096,128]{2,1,0:T(8,128)(2,1)} %own_ref.3, ...), custom_call_target="tpu_custom_call" | custom-call | tf_op jit(solution)/shard_map/time_attention/pallas_call | solution.py:403
  118.6 9.3 %all-to-all-start.2 = ((f32[128,2,128]{2,1,0:T(2,128)}), f32[128,2,128]{2,1,0:T(2,128)S(1)}, u32[]{:S(2)}, u32[]{:S(2)}) async-start(f32[128,2,128]{2,1,0:T(2,128)} %bitcast.17), calls=%async_computation.2 | async-start | bytes 262144 | tf_op jit(solution)/shard_map/all_to_all | solution.py:418
  127.9 0.6 select_reduce_fusion
  131.3 8.5 %all-to-all-done.2 = f32[128,2,128]{2,1,0:T(2,128)S(1)} async-done(((f32[128,2,128]{2,1,0:T(2,128)}), f32[128,2,128]{2,1,0:T(2,128)S(1)}, u32[]{:S(2)}, u32[]{:S(2)}) %all-to-all-start.2) | async-done | bytes 131104 | tf_op jit(solution)/shard_map/all_to_all | solution.py:418
  139.8 0.4 fusion.2
  140.2 0.0 copy-done.7
  140.3 0.6 divide_add_fusion
  (23 shorter events, 0.2 us)
Async XLA Ops:
  0.6 18.9 %copy-start = (bf16[4096,128]{1,0:T(8,128)(2,1)S(1)}, bf16[4096,128]{1,0:T(8,128)(2,1)}, u32[]{:S(2)}) copy-start(bf16[4096,128]{1,0:T(8,128)(2,1)} %param.21) | copy-start | bytes 3145732
  0.6 20.7 %copy-start.4 = (bf16[128,4096]{1,0:T(8,128)(2,1)S(1)}, bf16[128,4096]{1,0:T(8,128)(2,1)}, u32[]{:S(2)}) copy-start(bf16[128,4096]{1,0:T(8,128)(2,1)} %param.20) | copy-start | bytes 3145732
  3.0 20.1 %collective-permute-start = (bf16[128,1024]{1,0:T(8,128)(2,1)}, bf16[128,1024]{1,0:T(8,128)(2,1)}, u32[]{:S(2)}, u32[]{:S(2)}) collective-permute-start(bf16[128,1024]{1,0:T(8,128)(2,1)} %get-tuple-element.30), channel_id=1, source_target_pairs={{0,6},{2,0},{4,2},{6,4},{1,7},{3,1},{5,3},{7,5},{8,14},{10,8},{12,... | collective-permute-start | bytes 786440 | tf_op jit(solution)/shard_map/ppermute | solution.py:21
  5.8 17.4 %collective-permute-start.1 = (bf16[128,1024]{1,0:T(8,128)(2,1)}, bf16[128,1024]{1,0:T(8,128)(2,1)}, u32[]{:S(2)}, u32[]{:S(2)}) collective-permute-start(bf16[128,1024]{1,0:T(8,128)(2,1)} %get-tuple-element.29), channel_id=1, source_target_pairs={{0,4},{2,6},{4,0},{6,2},{1,5},{3,7},{5,1},{7,3},{8,12},{10,14},{12... | collective-permute-start | bytes 786440 | tf_op jit(solution)/shard_map/ppermute | solution.py:21
  6.6 16.6 %collective-permute-start.2 = (bf16[128,1024]{1,0:T(8,128)(2,1)}, bf16[128,1024]{1,0:T(8,128)(2,1)}, u32[]{:S(2)}, u32[]{:S(2)}) collective-permute-start(bf16[128,1024]{1,0:T(8,128)(2,1)} %get-tuple-element.31), channel_id=1, source_target_pairs={{0,2},{2,4},{4,6},{6,0},{1,3},{3,5},{5,7},{7,1},{8,10},{10,12},{12... | collective-permute-start | bytes 786440 | tf_op jit(solution)/shard_map/ppermute | solution.py:21
  8.9 21.6 %all-to-all-start = ((bf16[32,16,128]{2,1,0:T(8,128)(2,1)}), bf16[32,16,128]{2,1,0:T(8,128)(2,1)S(1)}, u32[]{:S(2)}, u32[]{:S(2)}) async-start(bf16[32,16,128]{2,1,0:T(8,128)(2,1)} %broadcast_in_dim.16), calls=%async_computation | async-start | bytes 262144 | tf_op jit(solution)/shard_map/all_to_all | solution.py:270
  19.5 11.3 %copy-start.6 = (f32[2,4096]{1,0:T(2,128)S(1)}, f32[2,4096]{1,0:T(2,128)}, u32[]{:S(2)}) copy-start(f32[2,4096]{1,0:T(2,128)} %param.14) | copy-start | bytes 98308
  19.5 11.3 %copy-start.1 = (bf16[128,4096]{1,0:T(8,128)(2,1)S(1)}, bf16[128,4096]{1,0:T(8,128)(2,1)}, u32[]{:S(2)}) copy-start(bf16[128,4096]{1,0:T(8,128)(2,1)} %embed_ref.5) | copy-start | bytes 3145732
  21.8 14.0 %collective-permute-start.4 = (bf16[256,128]{1,0:T(8,128)(2,1)S(1)}, bf16[256,128]{1,0:T(8,128)(2,1)S(1)}, u32[]{:S(2)}, u32[]{:S(2)}) collective-permute-start(bf16[256,128]{1,0:T(8,128)(2,1)S(1)} %pad_maximum_fusion.3), channel_id=1, source_target_pairs={{0,1},{1,0},{2,3},{3,2},{4,5},{5,4},{6,7},{7,6},{8,9},{9,8},{10,11... | collective-permute-start | bytes 196616 | tf_op jit(solution)/shard_map/ppermute | solution.py:21
  22.1 83.2 %collective-permute-start.15 = (bf16[3,4096,128]{2,1,0:T(8,128)(2,1)}, bf16[3,4096,128]{2,1,0:T(8,128)(2,1)}, u32[]{:S(2)}, u32[]{:S(2)}) collective-permute-start(bf16[3,4096,128]{2,1,0:T(8,128)(2,1)} %own_ref.3), channel_id=1, source_target_pairs={{0,1},{1,0},{2,3},{3,2},{4,5},{5,4},{6,7},{7,6},{8,9},{9,8},{10,11... | collective-permute-start | bytes 9437192 | tf_op jit(solution)/shard_map/ppermute | solution.py:21
  23.2 12.6 %copy-start.3 = (f32[4,128]{1,0:T(4,128)S(1)}, f32[4,128]{1,0:T(4,128)}, u32[]{:S(2)}) copy-start(f32[4,128]{1,0:T(4,128)} %head_gain_ref.1) | copy-start | bytes 6148
  30.5 8.2 %collective-permute-start.3 = (bf16[4,128,1024]{2,1,0:T(8,128)(2,1)S(1)}, bf16[4,128,1024]{2,1,0:T(8,128)(2,1)S(1)}, u32[]{:S(2)}, u32[]{:S(2)}) collective-permute-start(bf16[4,128,1024]{2,1,0:T(8,128)(2,1)S(1)} %pad_maximum_fusion.own_ref), channel_id=1, source_target_pairs={{0,1},{1,0},{2,3},{3,2},{4,5},{5,4},{6,7},{7,6},{8,9},{9,8},{10,11... | collective-permute-start | bytes 3145736 | tf_op jit(solution)/shard_map/ppermute | solution.py:21
  30.8 1.9 %copy-start.2 = (bf16[3,4096,128]{2,1,0:T(8,128)(2,1)S(1)}, bf16[3,4096,128]{2,1,0:T(8,128)(2,1)}, u32[]{:S(2)}) copy-start(bf16[3,4096,128]{2,1,0:T(8,128)(2,1)} %weight_ref.1) | copy-start | bytes 9437188
  62.7 9.0 %collective-permute-start.5 = (bf16[64,1024]{1,0:T(8,128)(2,1)S(1)}, bf16[64,1024]{1,0:T(8,128)(2,1)S(1)}, u32[]{:S(2)}, u32[]{:S(2)}) collective-permute-start(bf16[64,1024]{1,0:T(8,128)(2,1)S(1)} %get-tuple-element.32), channel_id=1, source_target_pairs={{0,8},{8,16},{16,24},{24,0},{1,9},{9,17},{17,25},{25,1},{2,10},{10... | collective-permute-start | bytes 393224 | tf_op jit(solution)/shard_map/ppermute | solution.py:21
  63.5 11.6 %collective-permute-start.6 = (bf16[64,1024]{1,0:T(8,128)(2,1)S(1)}, bf16[64,1024]{1,0:T(8,128)(2,1)S(1)}, u32[]{:S(2)}, u32[]{:S(2)}) collective-permute-start(bf16[64,1024]{1,0:T(8,128)(2,1)S(1)} %get-tuple-element.34), channel_id=1, source_target_pairs={{0,24},{8,0},{16,8},{24,16},{1,25},{9,1},{17,9},{25,17},{2,26},{10... | collective-permute-start | bytes 393224 | tf_op jit(solution)/shard_map/ppermute | solution.py:21
  66.9 11.6 %collective-permute-start.7 = (bf16[64,1024]{1,0:T(8,128)(2,1)S(1)}, bf16[64,1024]{1,0:T(8,128)(2,1)S(1)}, u32[]{:S(2)}, u32[]{:S(2)}) collective-permute-start(bf16[64,1024]{1,0:T(8,128)(2,1)S(1)} %get-tuple-element.33), channel_id=1, source_target_pairs={{0,16},{8,24},{16,0},{24,8},{1,17},{9,25},{17,1},{25,9},{2,18},{10... | collective-permute-start | bytes 393224 | tf_op jit(solution)/shard_map/ppermute | solution.py:21
  78.6 11.8 %collective-permute-start.11 = (bf16[64,1024]{1,0:T(8,128)(2,1)S(1)}, bf16[64,1024]{1,0:T(8,128)(2,1)S(1)}, u32[]{:S(2)}, u32[]{:S(2)}) collective-permute-start(bf16[64,1024]{1,0:T(8,128)(2,1)S(1)} %add_convert_fusion), channel_id=1, source_target_pairs={{0,16},{8,24},{16,0},{24,8},{1,17},{9,25},{17,1},{25,9},{2,18},{10... | collective-permute-start | bytes 393224 | tf_op jit(solution)/shard_map/ppermute | solution.py:21
  80.7 10.5 %collective-permute-start.12 = (bf16[64,1024]{1,0:T(8,128)(2,1)S(1)}, bf16[64,1024]{1,0:T(8,128)(2,1)S(1)}, u32[]{:S(2)}, u32[]{:S(2)}) collective-permute-start(bf16[64,1024]{1,0:T(8,128)(2,1)S(1)} %add_convert_fusion), channel_id=1, source_target_pairs={{0,8},{8,16},{16,24},{24,0},{1,9},{9,17},{17,25},{25,1},{2,10},{10... | collective-permute-start | bytes 393224 | tf_op jit(solution)/shard_map/ppermute | solution.py:21
  84.9 9.8 %collective-permute-start.8 = (bf16[64,1024]{1,0:T(8,128)(2,1)S(1)}, bf16[64,1024]{1,0:T(8,128)(2,1)S(1)}, u32[]{:S(2)}, u32[]{:S(2)}) collective-permute-start(bf16[64,1024]{1,0:T(8,128)(2,1)S(1)} %add_convert_fusion), channel_id=1, source_target_pairs={{0,24},{8,0},{16,8},{24,16},{1,25},{9,1},{17,9},{25,17},{2,26},{10... | collective-permute-start | bytes 393224 | tf_op jit(solution)/shard_map/ppermute | solution.py:21
  91.3 8.7 %collective-permute-start.13 = (bf16[128,1024]{1,0:T(8,128)(2,1)S(1)}, bf16[128,1024]{1,0:T(8,128)(2,1)S(1)}, u32[]{:S(2)}, u32[]{:S(2)}) collective-permute-start(bf16[128,1024]{1,0:T(8,128)(2,1)S(1)} %constant_dynamic-update-slice_fusion.b0), channel_id=1, source_target_pairs={{0,6},{2,0},{4,2},{6,4},{1,7},{3,1},{5,3},{7,5},{8,14},{10,8},{12,... | collective-permute-start | bytes 786440 | tf_op jit(solution)/shard_map/ppermute | solution.py:21
  94.7 10.5 %collective-permute-start.9 = (bf16[128,1024]{1,0:T(8,128)(2,1)S(1)}, bf16[128,1024]{1,0:T(8,128)(2,1)S(1)}, u32[]{:S(2)}, u32[]{:S(2)}) collective-permute-start(bf16[128,1024]{1,0:T(8,128)(2,1)S(1)} %pad_maximum_fusion.1.a0), channel_id=1, source_target_pairs={{0,2},{2,4},{4,6},{6,0},{1,3},{3,5},{5,7},{7,1},{8,10},{10,12},{12... | collective-permute-start | bytes 786440 | tf_op jit(solution)/shard_map/ppermute | solution.py:21
  94.8 14.9 %collective-permute-start.17 = (bf16[128,1024]{1,0:T(8,128)(2,1)S(1)}, bf16[128,1024]{1,0:T(8,128)(2,1)S(1)}, u32[]{:S(2)}, u32[]{:S(2)}) collective-permute-start(bf16[128,1024]{1,0:T(8,128)(2,1)S(1)} %constant_dynamic-update-slice_fusion.b0), channel_id=1, source_target_pairs={{0,2},{2,4},{4,6},{6,0},{1,3},{3,5},{5,7},{7,1},{8,10},{10,12},{12... | collective-permute-start | bytes 786440 | tf_op jit(solution)/shard_map/ppermute | solution.py:21
  96.3 13.5 %collective-permute-start.16 = (bf16[128,1024]{1,0:T(8,128)(2,1)S(1)}, bf16[128,1024]{1,0:T(8,128)(2,1)S(1)}, u32[]{:S(2)}, u32[]{:S(2)}) collective-permute-start(bf16[128,1024]{1,0:T(8,128)(2,1)S(1)} %pad_maximum_fusion.1.a0), channel_id=1, source_target_pairs={{0,6},{2,0},{4,2},{6,4},{1,7},{3,1},{5,3},{7,5},{8,14},{10,8},{12,... | collective-permute-start | bytes 786440 | tf_op jit(solution)/shard_map/ppermute | solution.py:21
  99.9 14.5 %collective-permute-start.14 = (bf16[128,1024]{1,0:T(8,128)(2,1)S(1)}, bf16[128,1024]{1,0:T(8,128)(2,1)S(1)}, u32[]{:S(2)}, u32[]{:S(2)}) collective-permute-start(bf16[128,1024]{1,0:T(8,128)(2,1)S(1)} %collective-permute-done.13.b1), channel_id=1, source_target_pairs={{0,6},{2,0},{4,2},{6,4},{1,7},{3,1},{5,3},{7,5},{8,14},{10,8},{12,... | collective-permute-start | bytes 786440 | tf_op jit(solution)/shard_map/ppermute | solution.py:21
  105.3 9.2 %collective-permute-start.10 = (bf16[128,1024]{1,0:T(8,128)(2,1)S(1)}, bf16[128,1024]{1,0:T(8,128)(2,1)S(1)}, u32[]{:S(2)}, u32[]{:S(2)}) collective-permute-start(bf16[128,1024]{1,0:T(8,128)(2,1)S(1)} %collective-permute-done.9.a3), channel_id=1, source_target_pairs={{0,2},{2,4},{4,6},{6,0},{1,3},{3,5},{5,7},{7,1},{8,10},{10,12},{12... | collective-permute-start | bytes 786440 | tf_op jit(solution)/shard_map/ppermute | solution.py:21
  114.5 13.4 %copy-start.8 = (f32[1000]{0:T(1024)S(1)}, f32[1000]{0:T(1024)}, u32[]{:S(2)}) copy-start(f32[1000]{0:T(1024)} %param.13) | copy-start | bytes 12004
  114.5 25.8 %copy-start.7 = (f32[8,2,128]{2,1,0:T(2,128)S(1)}, f32[8,2,128]{2,1,0:T(2,128)}, u32[]{:S(2)}) copy-start(f32[8,2,128]{2,1,0:T(2,128)} %param.11) | copy-start | bytes 24580
  118.6 21.2 %all-to-all-start.2 = ((f32[128,2,128]{2,1,0:T(2,128)}), f32[128,2,128]{2,1,0:T(2,128)S(1)}, u32[]{:S(2)}, u32[]{:S(2)}) async-start(f32[128,2,128]{2,1,0:T(2,128)} %bitcast.17), calls=%async_computation.2 | async-start | bytes 262144 | tf_op jit(solution)/shard_map/all_to_all | solution.py:418
  140.2 0.6 copy-start.5

commit v4 on v3

v4 whole, which is shorter than its diff:
```python
import math

import jax
import jax.numpy as jnp
from jax import lax
from jax.experimental import pallas as pl
from jax.experimental.pallas import tpu as pltpu
from jax.sharding import Mesh, PartitionSpec as P

STRIDE = 20
EPS = 1e-06
NX = 4
HD = 128
ORDER = (1, 3, 2)
BF = jnp.bfloat16
F32 = jnp.float32


def shift(value, axis, step):
    size = lax.axis_size(axis)
    return lax.ppermute(value, axis, [(i, (i + step) % size) for i in range(size)])


def time_embedding(step_now, model_width):
    half_width = model_width // 2
    positions = jnp.arange(half_width, dtype=F32)
    frequency = jnp.exp(positions * (-math.log(10000.0) / half_width))
    angles = step_now.astype(F32) * frequency
    return jnp.concatenate([jnp.sin(angles), jnp.cos(angles)])


def head_norm(values, gain):
    mean_square = jnp.mean(values * values, axis=-1, keepdims=True)
    return (values * gain * lax.rsqrt(mean_square + EPS)).astype(BF)


def weigh(scores, mask=None):
    e = jnp.exp(scores * (1.0 / math.sqrt(HD)))
    if mask is not None:
        e = jnp.where(mask, e, 0.0)
    return (e / jnp.sum(e, axis=-1, keepdims=True)).astype(BF)


def dot_t(a, b):
    return lax.dot_general(a, b, (((1,), (1,)), ((), ())), preferred_element_type=F32)


def dot(a, b):
    return jnp.dot(a, b, preferred_element_type=F32)


def reorder(count, source):
    row = lax.broadcasted_iota(jnp.int32, (count, count), 0)
    col = lax.broadcasted_iota(jnp.int32, (count, count), 1)
    return (col == source(row)).astype(BF)


def fold_kernel(embed_ref, temb_ref, gain_ref, weight_ref, fold_ref, bias_ref, held, sems):
    width = embed_ref.shape[1]
    chunk = width // sems.shape[0]
    copies = []
    for step in range(sems.shape[0]):
        rows = pl.ds(step * chunk, chunk)
        copies.append(pltpu.make_async_copy(weight_ref.at[:, rows, :], held.at[:, rows, :], sems.at[step]))
        copies[-1].start()
    fold = jnp.zeros((HD, 3 * HD), F32)
    bias = jnp.zeros((16, 3 * HD), F32)
    row = lax.broadcasted_iota(jnp.int32, (16, chunk), 0)
    for step in range(sems.shape[0]):
        columns = slice(step * chunk, (step + 1) * chunk)
        gain = gain_ref[:, columns]
        scaled = embed_ref[:, columns].astype(F32) * gain
        high = scaled.astype(BF)
        low = (scaled - high.astype(F32)).astype(BF)
        time = temb_ref[:, columns] * gain
        time_high = time.astype(BF).astype(F32)
        extra = jnp.where(row == 0, time_high, jnp.where(row == 1, time - time_high, 0.0)).astype(BF)
        copies[step].wait()
        weights = jnp.concatenate([held[i, columns, :] for i in range(3)], axis=1)
        share = dot(jnp.concatenate([high, low, extra], axis=0), weights)
        fold = fold + (share[:HD] + share[HD : 2 * HD])
        bias = bias + share[2 * HD :]
    fold_high = fold.astype(BF)
    fold_ref[:HD, :] = fold_high
    fold_ref[HD:, :] = (fold - fold_high.astype(F32)).astype(BF)
    bias_ref[...] = jnp.broadcast_to(bias[0:1, :] + bias[1:2, :], bias_ref.shape)


def space_kernel(place_ref, lat_ref, embed_ref, temb_ref, fold_ref, bias_ref, gain_ref, out_ref):
    z_here = place_ref[1]
    core = place_ref[2]

    def source(row):
        z = (z_here + (row >> 2)) & 3
        frame = (row >> 8) & 1
        return ((((((z * 4 + (row & 3)) * 2 + ((row >> 4) & 1)) << 3) + ((row >> 5) & 7)) << 1) + frame)

    lat = dot(reorder(512, source), lat_ref[...]).astype(BF)
    width = embed_ref.shape[1]
    chunk = 256
    total = jnp.zeros((lat.shape[0], 128), F32)
    for start in range(0, width, chunk):
        first = dot(lat, embed_ref[:, start : start + chunk]) + temb_ref[:, start : start + chunk]
        first = first.astype(BF).astype(F32)
        square = first * first
        for lane in range(0, chunk, 128):
            total = total + square[:, lane : lane + 128]
    mean_square = jnp.sum(total, axis=-1, keepdims=True) * (1.0 / width)
    scale = lax.rsqrt(mean_square + EPS)
    proj = (dot(jnp.concatenate([lat, lat], axis=1), fold_ref[...]) + bias_ref[0:1, :]) * scale
    query = head_norm(proj[:, :HD], gain_ref[0:1, :])
    key = head_norm(proj[:, HD : 2 * HD], gain_ref[1:2, :])
    value = proj[:, 2 * HD :].astype(BF)
    parts = []
    for frame in range(2):
        rows = slice(frame * 256, (frame + 1) * 256)
        weights = weigh(dot_t(query[rows], key[rows]))
        parts.append(dot(weights, value[rows]).astype(BF))
    parts.append(jnp.where(core == 0, lat[:256], lat[256:]))
    for tm in range(8):
        for side in range(2):
            rows = slice(tm * 32 + side * 16, tm * 32 + side * 16 + 16)
            message = jnp.concatenate([part[rows] for part in parts[:2]], axis=0)
            extra = parts[2][rows][:8]
            for x in range(NX):
                place = (tm * NX + x) * 2 + side
                out_ref[place, :32, :] = message
                out_ref[place, 32:40, :] = extra


def output_kernel(
    place_ref, att_ref, embed_ref, temb_ref, own_ref, other_ref, out_ref, base_ref, att_own_ref, lhs_own, lhs_other
):
    x_here = place_ref[0]
    core = place_ref[2]
    swap = reorder(256, lambda row: ((row & 15) << 4) + (row >> 4))
    for x in range(NX):
        sides = [
            jnp.concatenate([att_ref[(tm * NX + x) * 2 + side, :32, :] for tm in range(8)], axis=0)
            for side in range(2)
        ]
        rows = dot(swap, jnp.concatenate(sides, axis=1)).astype(BF)
        slot = pl.multiple_of(((x - x_here) & 3) * HD, HD)
        lhs_own[:, pl.ds(slot, HD)] = jnp.where(core == 0, rows[:, :HD], rows[:, HD:])
        lhs_other[:, pl.ds(slot, HD)] = jnp.where(core == 0, rows[:, HD:], rows[:, :HD])

        @pl.when(x == x_here)
        def _(rows=rows):
            att_own_ref[...] = rows

    rows = jnp.concatenate(
        [att_ref[tm * NX * 2 + side, 32:40, :].astype(F32) for tm in range(8) for side in range(2)], axis=0
    ).astype(BF)
    pick = reorder(128, lambda row: ((row & 15) << 3) + (row >> 4))
    lat = dot(pick[:64, :], rows).astype(BF)

    tile = 256
    for start in range(0, own_ref.shape[2], tile):
        columns = slice(start, start + tile)
        own = own_ref[:, :, columns].reshape(NX * HD, tile)
        other = other_ref[:, :, columns].reshape(NX * HD, tile)
        share = (dot(lhs_own[...], own) + dot(lhs_other[...], other)).astype(BF)
        out_ref[:, columns] = share[64:, :]
        first = (dot(lat, embed_ref[:, columns]) + temb_ref[:, columns]).astype(BF)
        base_ref[:, columns] = first.astype(F32) + share[:64, :].astype(F32)


def load_kernel(place_ref, own_ref, other_ref, held_ref, sems):
    block = held_ref.shape[2]
    copies = []
    for d in range(NX):
        rows = pl.ds(pl.multiple_of(((place_ref[0] + d) & 3) * block, block), block)
        for side, ref in enumerate((own_ref, other_ref)):
            target = held_ref.at[d, pl.ds(side * 3, 3)]
            copies.append(pltpu.make_async_copy(ref.at[:, rows, :], target, sems.at[d, side]))
            copies[-1].start()
    for copy in copies:
        copy.wait()


def project_block(place_ref, d, rows, gain_ref, held_ref, total, add):
    rows = rows.astype(F32)
    square = rows * rows
    for lane in range(0, rows.shape[1], 128):
        total = total + square[:, lane : lane + 128]
    gained = (rows * gain_ref[(place_ref[0] + d) & 3]).astype(BF)
    for index in range(3):
        pair = jnp.concatenate([held_ref[d, index], held_ref[d, 3 + index]], axis=1)
        add(index, dot(gained, pair))
    return total


def time_project_kernel(place_ref, a0, b0, a1, b1, a3, b3, gain_ref, held_ref, proj_ref, total_ref):
    parts = {}

    def add(index, value):
        parts[index] = parts[index] + value if index in parts else value

    total = jnp.zeros(total_ref.shape, F32)
    for d, a, b in ((0, a0, b0), (1, a1, b1), (3, a3, b3)):
        rows = jnp.concatenate([a[...], b[...]], axis=0)
        total = project_block(place_ref, d, rows, gain_ref, held_ref, total, add)
    total_ref[...] = total
    for index in range(3):
        proj_ref[:, index * 2 * HD : (index + 1) * 2 * HD] = parts[index]


def time_kernel(
    place_ref, a2, b2, gain_ref, held_ref, proj_ref, total_ref, head_gain_ref, att_ref, fold_ref, out_ref
):
    parts = {}

    def add(index, value):
        parts[index] = proj_ref[:, index * 2 * HD : (index + 1) * 2 * HD] + value

    rows = jnp.concatenate([a2[...], b2[...]], axis=0)
    total = project_block(place_ref, 2, rows, gain_ref, held_ref, total_ref[...], add)
    z_here = place_ref[1]
    width = NX * a2.shape[1]
    mean_square = jnp.sum(total, axis=-1, keepdims=True) * (1.0 / width)
    scale = lax.rsqrt(mean_square + EPS)
    count = rows.shape[0]
    row_patch = lax.broadcasted_iota(jnp.int32, (count, count), 0) >> 4
    col_patch = lax.broadcasted_iota(jnp.int32, (count, count), 1) >> 4
    mask = row_patch == col_patch
    columns = [att_ref[...]]
    for side in range(2):
        query, key, value = [parts[index][:, side * HD : (side + 1) * HD] * scale for index in range(3)]
        query = head_norm(query, head_gain_ref[2:3, :])
        key = head_norm(key, head_gain_ref[3:4, :])
        weights = weigh(dot_t(query, key), mask)
        columns.append(dot(weights, value.astype(BF)).astype(BF))

    def source(row):
        z = (((row >> 3) & 3) - z_here) & 3
        return (z << 6) + (((row >> 1) & 3) << 4) + ((row >> 5) << 1) + (row & 1)

    both = dot(reorder(count, source), jnp.concatenate(columns, axis=1)).astype(BF)
    out_ref[...] = dot(both, fold_ref[...])


def body(
    latents,
    timestep,
    alpha_table,
    norm_gain,
    head_gain,
    embed_weight,
    space_project,
    space_output,
    time_project,
    time_output,
    noise_weight,
):
    width = embed_weight.shape[1]
    block = width // NX
    core = lax.axis_index("c")
    place = lax.axis_index("x")
    places = jnp.stack([place, lax.axis_index("zh"), core]).astype(jnp.int32)
    step_now = timestep[0]
    positions = jnp.arange(alpha_table.shape[0], dtype=jnp.int32)
    alpha_now = jnp.sum(jnp.where(positions == step_now, alpha_table, 0.0))
    alpha_next = jnp.sum(jnp.where(positions == step_now + STRIDE, alpha_table, 0.0))
    temb = time_embedding(step_now, width)[None, :]

    def in_order(own, other):
        first = jnp.where(core == 0, own, other)
        second = jnp.where(core == 0, other, own)
        return jnp.stack([first, second])

    lat_bf = latents.astype(BF)
    lat_rows = jnp.broadcast_to(lat_bf.reshape(1, 16, HD), (32, 16, HD)).reshape(512, HD)
    lat_rows = lax.all_to_all(lat_rows, ("zh", "x", "c"), split_axis=0, concat_axis=0, tiled=True)

    vmem = pl.BlockSpec(memory_space=pltpu.VMEM)
    anywhere = pl.BlockSpec(memory_space=pltpu.HBM)

    def whole(*shape):
        return pl.BlockSpec(shape, lambda i, s: (0,) * len(shape))

    fold, bias = pl.pallas_call(
        fold_kernel,
        out_shape=(jax.ShapeDtypeStruct((2 * HD, 3 * HD), BF), jax.ShapeDtypeStruct((8, 3 * HD), F32)),
        in_specs=[vmem, vmem, vmem, anywhere],
        out_specs=(vmem, vmem),
        scratch_shapes=[pltpu.VMEM((3, width, HD), BF), pltpu.SemaphoreType.DMA((8,))],
        compiler_params=pltpu.CompilerParams(vmem_limit_bytes=16 * 1024 * 1024),
        cost_estimate=pl.CostEstimate(flops=2 * 272 * 4096 * 384, bytes_accessed=1024, transcendentals=0),
        name="fold_projection",
    )(embed_weight, temb, norm_gain[0:1], space_project)

    def piece_of(weight, d):
        return lax.dynamic_slice(weight, (0, ((place - d) % NX) * block), (HD, block))

    got = {d: shift(piece_of(space_output, d), "x", -d) for d in ORDER}
    got[1], late_output = lax.optimization_barrier((got[1], space_output))
    got[0] = piece_of(late_output, 0)
    out_own = jnp.stack([got[d] for d in range(NX)])
    out_other = shift(out_own, "c", 1)
    time_other = shift(time_project, "c", 1)
    attended = pl.pallas_call(
        space_kernel,
        out_shape=jax.ShapeDtypeStruct((64, 40, HD), BF),
        grid_spec=pltpu.PrefetchScalarGridSpec(
            num_scalar_prefetch=1,
            grid=(1,),
            in_specs=[vmem] * 6,
            out_specs=vmem,
        ),
        compiler_params=pltpu.CompilerParams(vmem_limit_bytes=32 * 1024 * 1024),
        name="space_attention",
    )(places, lat_rows, embed_weight, temb, fold, bias, head_gain)

    attended, out_other, time_other = lax.optimization_barrier((attended, out_other, time_other))
    regrouped = lax.all_to_all(attended, ("y", "zl", "x", "c"), split_axis=0, concat_axis=0, tiled=True)

    regrouped, late_weight = lax.optimization_barrier((regrouped, noise_weight))
    noise_fold = jnp.concatenate(
        [dot(space_output, late_weight).astype(BF), dot(time_output, late_weight).astype(BF)]
    )
    noise_other = shift(noise_fold, "c", 1)

    share, base, att_own = pl.pallas_call(
        output_kernel,
        out_shape=(
            jax.ShapeDtypeStruct((192, block), BF),
            jax.ShapeDtypeStruct((64, block), F32),
            jax.ShapeDtypeStruct((256, 2 * HD), BF),
        ),
        grid_spec=pltpu.PrefetchScalarGridSpec(
            num_scalar_prefetch=1,
            grid=(1,),
            in_specs=[
                vmem,
                pl.BlockSpec((HD, block), lambda i, s: (0, s[0])),
                pl.BlockSpec((1, block), lambda i, s: (0, s[0])),
                vmem,
                vmem,
            ],
            out_specs=[vmem, vmem, vmem],
            scratch_shapes=[pltpu.VMEM((256, NX * HD), BF), pltpu.VMEM((256, NX * HD), BF)],
        ),
        compiler_params=pltpu.CompilerParams(vmem_limit_bytes=32 * 1024 * 1024),
        name="space_output",
    )(places, regrouped, embed_weight, temb, out_own, out_other)

    sent = {d: shift(share[64 * (d - 1) : 64 * d], "zh", d) for d in ORDER}
    for d in ORDER:
        base = base + sent[d].astype(F32)
    second = base.astype(BF)
    second, noise_other = lax.optimization_barrier((second, noise_other))
    noise_fold = jnp.concatenate(
        [in_order(noise_fold[:HD], noise_other[:HD]).reshape(2 * HD, HD), noise_fold[HD:], noise_other[HD:]]
    )
    got = {d: shift(second, "zh", -d) for d in ORDER}
    near = jnp.concatenate([second, got[1]])
    far = jnp.concatenate([got[2], got[3]])
    near_3 = shift(near, "x", 1)
    near_1 = shift(near, "x", -1)
    far_1 = shift(far, "x", -1)
    far_3 = shift(far, "x", 1)
    _, time_other = lax.optimization_barrier((near, time_other))
    held = pl.pallas_call(
        load_kernel,
        out_shape=jax.ShapeDtypeStruct((NX, 6, block, HD), BF),
        in_specs=[pl.BlockSpec(memory_space=pltpu.SMEM), anywhere, anywhere],
        out_specs=vmem,
        scratch_shapes=[pltpu.SemaphoreType.DMA((NX, 2))],
        compiler_params=pltpu.CompilerParams(vmem_limit_bytes=16 * 1024 * 1024),
        cost_estimate=pl.CostEstimate(flops=2 * 272 * 4096 * 384, bytes_accessed=1024, transcendentals=0),
        name="time_weights",
    )(places, time_project, time_other)
    near_2 = shift(near_3, "x", 1)
    far_2 = shift(far_1, "x", -1)

    smem = pl.BlockSpec(memory_space=pltpu.SMEM)
    gains = norm_gain[1].reshape(NX, 1, block)
    proj, total = pl.pallas_call(
        time_project_kernel,
        out_shape=(jax.ShapeDtypeStruct((256, 6 * HD), F32), jax.ShapeDtypeStruct((256, HD), F32)),
        in_specs=[smem] + [vmem] * 8,
        out_specs=(vmem, vmem),
        compiler_params=pltpu.CompilerParams(vmem_limit_bytes=24 * 1024 * 1024),
        cost_estimate=pl.CostEstimate(flops=2 * 256 * 3072 * 768, bytes_accessed=8 << 20, transcendentals=0),
        name="time_projection",
    )(places, near, far, near_1, far_1, near_3, far_3, gains, held)
    noise = pl.pallas_call(
        time_kernel,
        out_shape=jax.ShapeDtypeStruct((256, HD), F32),
        in_specs=[smem] + [vmem] * 9,
        out_specs=vmem,
        compiler_params=pltpu.CompilerParams(vmem_limit_bytes=24 * 1024 * 1024),
        name="time_attention",
    )(places, near_2, far_2, gains, held, proj, total, head_gain, att_own, noise_fold)

    noise = lax.all_to_all(noise, ("y", "zl", "zh", "x"), split_axis=0, concat_axis=0, tiled=True)
    total = jnp.sum(noise.reshape(8, 16, 2, HD), axis=1).reshape(16, HD)

    own_first = (dot(lat_bf.reshape(16, HD), embed_weight) + temb).astype(BF)
    predicted_noise = (total + dot(own_first, noise_weight)).reshape(latents.shape)
    latents_next = (
        jnp.sqrt(alpha_next)
        * (latents - jnp.sqrt(1.0 - alpha_now) * predicted_noise)
        / jnp.sqrt(alpha_now)
        + jnp.sqrt(1.0 - alpha_next) * predicted_noise
    )
    return (predicted_noise, latents_next)


def solution(mesh):
    fine = Mesh(mesh.devices.reshape(4, 2, 4, 4, 2), ("y", "zl", "zh", "x", "c"))
    space = ("zh", "x", "c")
    rows = P(space, ("y", "zl"), None)
    placed = (
        rows,
        P(),
        P(),
        P(),
        P(),
        P(),
        P(None, None, space),
        P(space, None),
        P(None, None, space),
        P(space, None),
        P(),
    )
    return jax.shard_map(
        body,
        mesh=fine,
        in_specs=placed,
        out_specs=(rows, rows),
        check_vma=False,
    )
```

time: 141 us -> 134 us (0.950)
  waiting for transfers between devices: 44.1 us -> 32 us
  starting transfers between devices: 42.7 us -> 50.2 us
  local copies, waits for them, and re-layouts: 5 us -> 7.01 us
  Pallas kernels: 18 us -> 16.3 us
    ppermute x18, waiting for transfers between devices: 29.6 us -> 20.5 us  [shift(): lax.ppermute(value, axis, [(i, (i + step) % size) for i in range(size)])]
    ppermute x18, starting transfers between devices: 22.8 us -> 28.8 us  [shift(): lax.ppermute(value, axis, [(i, (i + step) % size) for i in range(size)])]
    all_to_all x1, waiting for transfers between devices: 5.96 us -> 2.91 us  [body(): lax.all_to_all(lat_rows, ('zh', 'x', 'c'), split_axis=0, concat_axis=0, t...]
    pallas_call x1 -> x2, Pallas kernels: 2.91 us -> 5.58 us  [the longest x1 2.91 us: body(): pl.pallas_call(space_kernel, out_shape=jax.ShapeDtypeStruct((64, 40, HD),...]
    pallas_call x1, Pallas kernels: 4.67 us -> 2.01 us  [body(): pl.pallas_call(time_project_kernel, out_shape=(jax.ShapeDtypeStruct((256,...]
    all_to_all x1, starting transfers between devices: 9.27 us -> 11.3 us  [body(): lax.all_to_all(noise, ('y', 'zl', 'zh', 'x'), split_axis=0, concat_axis=0...]
    unnamed x19 -> x26, local copies, waits for them, and re-layouts: 1.95 us -> 3.84 us
  transfers between devices with their start and end apart: 20 -> 20, of which waited for: 11 -> 13; matrix products, arithmetic and copies ran while one was open for 4% -> 5% of each run, Pallas kernels for 10% -> 8%
where the time goes in v4:
time: 134 us
  starting transfers between devices  50.2 us (37%)
  waiting for transfers between devices  32 us (24%)
  blocking collectives  19.2 us (14%)
  Pallas kernels  16.3 us (12%)
  local copies, waits for them, and re-layouts  7.01 us (5%)
  between operations  4.45 us (3%)
  other arithmetic  3.44 us (3%)
    ppermute x18, starting transfers between devices, shift(): lax.ppermute(value, axis, [(i, (i + step) % size) for i in range(size)])  28.8 us
    ppermute x18, waiting for transfers between devices, shift(): lax.ppermute(value, axis, [(i, (i + step) % size) for i in range(size)])  20.5 us
    all_to_all x1, blocking collectives, body(): lax.all_to_all(attended, ('y', 'zl', 'x', 'c'), split_axis=0, concat_axis...  19.2 us
    all_to_all x1, starting transfers between devices, body(): lax.all_to_all(noise, ('y', 'zl', 'zh', 'x'), split_axis=0, concat_axis=0...  11.3 us
    all_to_all x1, starting transfers between devices, body(): lax.all_to_all(lat_rows, ('zh', 'x', 'c'), split_axis=0, concat_axis=0, t...  10.1 us
    all_to_all x1, waiting for transfers between devices, body(): lax.all_to_all(noise, ('y', 'zl', 'zh', 'x'), split_axis=0, concat_axis=0...  8.53 us
    unnamed x26, local copies, waits for them, and re-layouts  3.84 us
    pallas_call x1, Pallas kernels, body(): pl.pallas_call(output_kernel, out_shape=(jax.ShapeDtypeStruct((192, block...  3.44 us
  transfers between devices with their start and end apart: 20, of which 13 were waited for; matrix products, arithmetic and copies ran while one was open for 5% of the time, Pallas kernels for 8%

profile of v4, /device:TPU:8, one launch (start us, length us, event | category | flops | bytes accessed | tf_op | source)
XLA Modules:
  0.0 133.9 jit_solution(2995544697789302101)
XLA Ops:
  0.6 0.0 copy-start
  0.7 0.1 collective-permute-start.4
  0.8 1.4 %constant_dynamic-slice_fusion.2 = (bf16[128,1024]{1,0:T(8,128)(2,1)S(1)}, bf16[128,1024]{1,0:T(8,128)(2,1)S(1)}, bf16[128,1024]{1,0:T(8,128)(2,1)S(1)}) fusion(bf16[128,4096]{1,0:T(8,128)(2,1)} %param.18, s32[]{:T(128)S(6)} %select_n.51, s32[]{:T(128)S(6)} %select_n.55, s32[]{:T(128)S(6)} %select_n.57), kind=kLoop, calls=%fused_computation.33 | loop fusion | bytes 1572876 | tf_op jit(solution)/shard_map/dynamic_slice | solution.py:293
  2.2 2.8 %collective-permute-start = (bf16[128,1024]{1,0:T(8,128)(2,1)S(1)}, bf16[128,1024]{1,0:T(8,128)(2,1)S(1)}, u32[]{:S(2)}, u32[]{:S(2)}) collective-permute-start(bf16[128,1024]{1,0:T(8,128)(2,1)S(1)} %get-tuple-element.38), channel_id=1, source_target_pairs={{0,6},{2,0},{4,2},{6,4},{1,7},{3,1},{5,3},{7,5},{8,14},{10,8},{12,... | collective-permute-start | bytes 786440 | tf_op jit(solution)/shard_map/ppermute | solution.py:21
  5.0 0.0 collective-permute-start.2
  5.0 2.3 %collective-permute-start.1 = (bf16[128,1024]{1,0:T(8,128)(2,1)S(1)}, bf16[128,1024]{1,0:T(8,128)(2,1)}, u32[]{:S(2)}, u32[]{:S(2)}) collective-permute-start(bf16[128,1024]{1,0:T(8,128)(2,1)S(1)} %get-tuple-element.39), channel_id=1, source_target_pairs={{0,4},{2,6},{4,0},{6,2},{1,5},{3,7},{5,1},{7,3},{8,12},{10,14},{12... | collective-permute-start | bytes 786440 | tf_op jit(solution)/shard_map/ppermute | solution.py:21
  7.3 0.7 convert_element_type.33
  8.0 0.7 broadcast_in_dim.16
  8.7 10.1 %all-to-all-start = ((bf16[32,16,128]{2,1,0:T(8,128)(2,1)}), bf16[32,16,128]{2,1,0:T(8,128)(2,1)S(1)}, u32[]{:S(2)}, u32[]{:S(2)}) async-start(bf16[32,16,128]{2,1,0:T(8,128)(2,1)} %broadcast_in_dim.16), calls=%async_computation | async-start | bytes 262144 | tf_op jit(solution)/shard_map/all_to_all | solution.py:273
  19.5 0.1 fusion.6
  19.6 1.1 dynamic-slice_bitcast_fusion
  20.6 0.0 collective-permute-done.2
  20.7 0.0 copy-start.4
  20.7 1.2 pad_maximum_fusion.own_ref
  21.9 0.4 collective-permute-start.3
  22.3 0.0 copy-start.2
  22.4 1.9 %copy-done.2 = bf16[3,4096,128]{2,1,0:T(8,128)(2,1)S(1)} copy-done((bf16[3,4096,128]{2,1,0:T(8,128)(2,1)S(1)}, bf16[3,4096,128]{2,1,0:T(8,128)(2,1)}, u32[]{:S(2)}) %copy-start.2) | copy-done | bytes 3145752
  24.2 2.5 %fold_projection.1 = (bf16[256,384]{1,0:T(8,128)(2,1)S(1)}, f32[8,384]{1,0:T(8,128)S(1)}) custom-call(bf16[128,4096]{1,0:T(8,128)(2,1)S(1)} %copy-done.1, f32[1,4096]{1,0:T(1,128)S(1)} %bitcast.41, f32[1,4096]{1,0:T(1,128)S(1)} %get-tuple-element.48.gain_ref, bf16[3,4096,128]{2,1,0:T(8,128)(2,1)S(1)} %copy-done.2), custom_call_target="tpu_custom_call" | custom-call | flops 855638016 | bytes 1024 | tf_op jit(solution)/shard_map/fold_projection/pallas_call | solution.py:281
  26.8 0.1 pad_add_fusion.place_ref
  26.8 2.9 %all-to-all-done = bf16[32,16,128]{2,1,0:T(8,128)(2,1)S(1)} async-done(((bf16[32,16,128]{2,1,0:T(8,128)(2,1)}), bf16[32,16,128]{2,1,0:T(8,128)(2,1)S(1)}, u32[]{:S(2)}, u32[]{:S(2)}) %all-to-all-start) | async-done | bytes 131104 | tf_op jit(solution)/shard_map/all_to_all | solution.py:273
  29.8 2.9 %space_attention.1 = bf16[64,40,128]{2,1,0:T(8,128)(2,1)S(1)} custom-call(s32[3]{0:T(128)S(1)} %pad_add_fusion.place_ref, bf16[512,128]{1,0:T(8,128)(2,1)S(1)} %bitcast.40, bf16[128,4096]{1,0:T(8,128)(2,1)S(1)} %copy-done.1, f32[1,4096]{1,0:T(1,128)S(1)} %bitcast.42, bf16[256,384]{1,0:T(8,128)(2,1)S(1)} %get-tuple-element.19.fold_ref, ...), custom_call_target="tpu_custom_call" | custom-call | tf_op jit(solution)/shard_map/space_attention/pallas_call | solution.py:301
  32.7 0.0 collective-permute-done.3.other_ref
  32.7 0.0 collective-permute-done.4.other_ref
  32.7 19.2 %all_to_all.22.att_ref = bf16[64,40,128]{2,1,0:T(8,128)(2,1)S(1)} all-to-all(bf16[64,40,128]{2,1,0:T(8,128)(2,1)S(1)} %space_attention.1), channel_id=1, replica_groups=mesh['y'=4,'zl'=2,'zh'=4,'x'=4,'c'=2] {'y','zl','x','c'}, dimensions={0} | all-to-all | bytes 1310720 | tf_op jit(solution)/shard_map/all_to_all | solution.py:315
  51.9 0.4 fusion.2
  52.4 3.4 %space_output.1 = (bf16[192,1024]{1,0:T(8,128)(2,1)S(1)}, f32[64,1024]{1,0:T(8,128)S(1)}, bf16[256,256]{1,0:T(8,128)(2,1)S(1)}) custom-call(s32[3]{0:T(128)S(1)} %pad_add_fusion.place_ref, bf16[64,40,128]{2,1,0:T(8,128)(2,1)S(1)} %all_to_all.22.att_ref, bf16[128,4096]{1,0:T(8,128)(2,1)S(1)} %copy-done.1, f32[1,4096]{1,0:T(1,128)S(1)} %bitcast.43, ...), custom_call_target="tpu_custom_call" | custom-call | tf_op jit(solution)/shard_map/space_output/pallas_call | solution.py:323
  55.9 1.5 %collective-permute-start.5 = (bf16[64,1024]{1,0:T(8,128)(2,1)S(1)}, bf16[64,1024]{1,0:T(8,128)(2,1)S(1)}, u32[]{:S(2)}, u32[]{:S(2)}) collective-permute-start(bf16[64,1024]{1,0:T(8,128)(2,1)S(1)} %get-tuple-element.41), channel_id=1, source_target_pairs={{0,8},{8,16},{16,24},{24,0},{1,9},{9,17},{17,25},{25,1},{2,10},{10... | collective-permute-start | bytes 393224 | tf_op jit(solution)/shard_map/ppermute | solution.py:21
  57.4 2.7 %collective-permute-start.6 = (bf16[64,1024]{1,0:T(8,128)(2,1)S(1)}, bf16[64,1024]{1,0:T(8,128)(2,1)S(1)}, u32[]{:S(2)}, u32[]{:S(2)}) collective-permute-start(bf16[64,1024]{1,0:T(8,128)(2,1)S(1)} %get-tuple-element.43), channel_id=1, source_target_pairs={{0,24},{8,0},{16,8},{24,16},{1,25},{9,1},{17,9},{25,17},{2,26},{10... | collective-permute-start | bytes 393224 | tf_op jit(solution)/shard_map/ppermute | solution.py:21
  60.1 4.4 %collective-permute-start.7 = (bf16[64,1024]{1,0:T(8,128)(2,1)S(1)}, bf16[64,1024]{1,0:T(8,128)(2,1)S(1)}, u32[]{:S(2)}, u32[]{:S(2)}) collective-permute-start(bf16[64,1024]{1,0:T(8,128)(2,1)S(1)} %get-tuple-element.42), channel_id=1, source_target_pairs={{0,16},{8,24},{16,0},{24,8},{1,17},{9,25},{17,1},{25,9},{2,18},{10... | collective-permute-start | bytes 393224 | tf_op jit(solution)/shard_map/ppermute | solution.py:21
  64.5 0.4 fusion.3
  65.0 0.1 collective-permute-start.8
  65.1 1.5 %collective-permute-done.5 = bf16[64,1024]{1,0:T(8,128)(2,1)S(1)} collective-permute-done((bf16[64,1024]{1,0:T(8,128)(2,1)S(1)}, bf16[64,1024]{1,0:T(8,128)(2,1)S(1)}, u32[]{:S(2)}, u32[]{:S(2)}) %collective-permute-start.5) | collective-permute-done | bytes 131104 | tf_op jit(solution)/shard_map/ppermute | solution.py:21
  66.6 3.6 %collective-permute-done.6 = bf16[64,1024]{1,0:T(8,128)(2,1)S(1)} collective-permute-done((bf16[64,1024]{1,0:T(8,128)(2,1)S(1)}, bf16[64,1024]{1,0:T(8,128)(2,1)S(1)}, u32[]{:S(2)}, u32[]{:S(2)}) %collective-permute-start.6) | collective-permute-done | bytes 131104 | tf_op jit(solution)/shard_map/ppermute | solution.py:21
  70.2 0.9 collective-permute-done.7
  71.1 0.1 add_convert_fusion
  71.2 3.6 %collective-permute-start.12 = (bf16[64,1024]{1,0:T(8,128)(2,1)S(1)}, bf16[64,1024]{1,0:T(8,128)(2,1)S(1)}, u32[]{:S(2)}, u32[]{:S(2)}) collective-permute-start(bf16[64,1024]{1,0:T(8,128)(2,1)S(1)} %add_convert_fusion), channel_id=1, source_target_pairs={{0,16},{8,24},{16,0},{24,8},{1,17},{9,25},{17,1},{25,9},{2,18},{10... | collective-permute-start | bytes 393224 | tf_op jit(solution)/shard_map/ppermute | solution.py:21
  74.8 3.3 %collective-permute-start.13 = (bf16[64,1024]{1,0:T(8,128)(2,1)S(1)}, bf16[64,1024]{1,0:T(8,128)(2,1)S(1)}, u32[]{:S(2)}, u32[]{:S(2)}) collective-permute-start(bf16[64,1024]{1,0:T(8,128)(2,1)S(1)} %add_convert_fusion), channel_id=1, source_target_pairs={{0,8},{8,16},{16,24},{24,0},{1,9},{9,17},{17,25},{25,1},{2,10},{10... | collective-permute-start | bytes 393224 | tf_op jit(solution)/shard_map/ppermute | solution.py:21
  78.1 0.9 collective-permute-start.9
  79.0 1.2 collective-permute-done.12
  80.3 5.7 %collective-permute-done.13 = bf16[64,1024]{1,0:T(8,128)(2,1)S(1)} collective-permute-done((bf16[64,1024]{1,0:T(8,128)(2,1)S(1)}, bf16[64,1024]{1,0:T(8,128)(2,1)S(1)}, u32[]{:S(2)}, u32[]{:S(2)}) %collective-permute-start.13) | collective-permute-done | bytes 131104 | tf_op jit(solution)/shard_map/ppermute | solution.py:21
  86.0 0.1 collective-permute-start.14
  86.1 0.7 collective-permute-done.9
  86.8 1.7 %collective-permute-start.10 = (bf16[128,1024]{1,0:T(8,128)(2,1)S(1)}, bf16[128,1024]{1,0:T(8,128)(2,1)S(1)}, u32[]{:S(2)}, u32[]{:S(2)}) collective-permute-start(bf16[128,1024]{1,0:T(8,128)(2,1)S(1)} %constant_dynamic-update-slice_fusion.a0), channel_id=1, source_target_pairs={{0,2},{2,4},{4,6},{6,0},{1,3},{3,5},{5,7},{7,1},{8,10},{10,12},{12... | collective-permute-start | bytes 786440 | tf_op jit(solution)/shard_map/ppermute | solution.py:21
  88.5 1.5 %collective-permute-start.17 = (bf16[128,1024]{1,0:T(8,128)(2,1)S(1)}, bf16[128,1024]{1,0:T(8,128)(2,1)S(1)}, u32[]{:S(2)}, u32[]{:S(2)}) collective-permute-start(bf16[128,1024]{1,0:T(8,128)(2,1)S(1)} %constant_dynamic-update-slice_fusion.2.b0), channel_id=1, source_target_pairs={{0,2},{2,4},{4,6},{6,0},{1,3},{3,5},{5,7},{7,1},{8,10},{10,12},{12... | collective-permute-start | bytes 786440 | tf_op jit(solution)/shard_map/ppermute | solution.py:21
  90.0 1.8 %collective-permute-start.16 = (bf16[128,1024]{1,0:T(8,128)(2,1)S(1)}, bf16[128,1024]{1,0:T(8,128)(2,1)S(1)}, u32[]{:S(2)}, u32[]{:S(2)}) collective-permute-start(bf16[128,1024]{1,0:T(8,128)(2,1)S(1)} %constant_dynamic-update-slice_fusion.a0), channel_id=1, source_target_pairs={{0,6},{2,0},{4,2},{6,4},{1,7},{3,1},{5,3},{7,5},{8,14},{10,8},{12,... | collective-permute-start | bytes 786440 | tf_op jit(solution)/shard_map/ppermute | solution.py:21
  91.8 3.4 %collective-permute-done.14.b1 = bf16[128,1024]{1,0:T(8,128)(2,1)S(1)} collective-permute-done((bf16[128,1024]{1,0:T(8,128)(2,1)S(1)}, bf16[128,1024]{1,0:T(8,128)(2,1)S(1)}, u32[]{:S(2)}, u32[]{:S(2)}) %collective-permute-start.14) | collective-permute-done | bytes 262176 | tf_op jit(solution)/shard_map/ppermute | solution.py:21
  95.2 1.2 collective-permute-start.15
  96.4 0.9 collective-permute-done.10.a3
  97.3 0.4 collective-permute-start.11
  97.7 0.0 copy-start.3
  97.7 1.9 %copy-done.3 = bf16[3,4096,128]{2,1,0:T(8,128)(2,1)S(1)} copy-done((bf16[3,4096,128]{2,1,0:T(8,128)(2,1)S(1)}, bf16[3,4096,128]{2,1,0:T(8,128)(2,1)}, u32[]{:S(2)}) %copy-start.3) | copy-done | bytes 3145752
  99.6 2.7 %time_weights.1.held_ref = bf16[4,6,1024,128]{3,2,1,0:T(8,128)(2,1)S(1)} custom-call(s32[3]{0:T(128)S(1)} %pad_add_fusion.place_ref, bf16[3,4096,128]{2,1,0:T(8,128)(2,1)S(1)} %copy-done.3, bf16[3,4096,128]{2,1,0:T(8,128)(2,1)} %collective-permute-done.4.other_ref), custom_call_target="tpu_custom_call" | custom-call | flops 855638016 | bytes 1024 | tf_op jit(solution)/shard_map/time_weights/pallas_call | solution.py:363
  102.3 0.6 collective-permute-done.17.b3
  102.9 0.0 collective-permute-done.16.a1
  102.9 2.0 %time_projection.1 = (f32[256,768]{1,0:T(8,128)S(1)}, f32[256,128]{1,0:T(8,128)S(1)}) custom-call(s32[3]{0:T(128)S(1)} %pad_add_fusion.place_ref, bf16[128,1024]{1,0:T(8,128)(2,1)S(1)} %constant_dynamic-update-slice_fusion.a0, bf16[128,1024]{1,0:T(8,128)(2,1)S(1)} %constant_dynamic-update-slice_fusion.2.b0, ...), custom_call_target="tpu_custom_call" | custom-call | flops 1207959552 | bytes 8388608 | tf_op jit(solution)/shard_map/time_projection/pallas_call | solution.py:378
  105.0 0.6 collective-permute-done.15.b2
  105.5 1.3 collective-permute-done.11.a2
  106.9 2.8 %time_attention.1 = f32[256,128]{1,0:T(8,128)} custom-call(s32[3]{0:T(128)S(1)} %pad_add_fusion.place_ref, bf16[128,1024]{1,0:T(8,128)(2,1)S(1)} %collective-permute-done.11.a2, bf16[128,1024]{1,0:T(8,128)(2,1)S(1)} %collective-permute-done.15.b2, f32[4,1,1024]{2,1,0:T(1,128)S(1)} %bitcast.45, bf16[4,6,1024,128]{3,2,1,0:T(8,128)(2,1)S(1)} %time_weights.1.held_ref, ...), custom_call_target="tpu_custom_call" | custom-call | tf_op jit(solution)/shard_map/time_attention/pallas_call | solution.py:387
  109.6 11.3 %all-to-all-start.2 = ((f32[128,2,128]{2,1,0:T(2,128)}), f32[128,2,128]{2,1,0:T(2,128)S(1)}, u32[]{:S(2)}, u32[]{:S(2)}) async-start(f32[128,2,128]{2,1,0:T(2,128)} %bitcast.17), calls=%async_computation.2 | async-start | bytes 262144 | tf_op jit(solution)/shard_map/all_to_all | solution.py:396
  120.9 0.6 select_reduce_fusion
  124.3 8.5 %all-to-all-done.2 = f32[128,2,128]{2,1,0:T(2,128)S(1)} async-done(((f32[128,2,128]{2,1,0:T(2,128)}), f32[128,2,128]{2,1,0:T(2,128)S(1)}, u32[]{:S(2)}, u32[]{:S(2)}) %all-to-all-start.2) | async-done | bytes 131104 | tf_op jit(solution)/shard_map/all_to_all | solution.py:396
  132.9 0.4 fusion.4
  133.3 0.0 copy-done.10
  133.3 0.6 divide_add_fusion
  (32 shorter events, 0.2 us)
Async XLA Ops:
  0.6 51.3 %copy-start = (bf16[4096,128]{1,0:T(8,128)(2,1)S(1)}, bf16[4096,128]{1,0:T(8,128)(2,1)}, u32[]{:S(2)}) copy-start(bf16[4096,128]{1,0:T(8,128)(2,1)} %param.21) | copy-start | bytes 3145732
  0.6 21.6 %copy-start.9 = (f32[2,4096]{1,0:T(2,128)S(1)}, f32[2,4096]{1,0:T(2,128)}, u32[]{:S(2)}) copy-start(f32[2,4096]{1,0:T(2,128)} %param.14) | copy-start | bytes 98308
  0.7 21.7 %copy-start.1 = (bf16[128,4096]{1,0:T(8,128)(2,1)S(1)}, bf16[128,4096]{1,0:T(8,128)(2,1)}, u32[]{:S(2)}) copy-start(bf16[128,4096]{1,0:T(8,128)(2,1)} %embed_ref.5) | copy-start | bytes 3145732
  0.7 32.0 %collective-permute-start.4 = (bf16[3,4096,128]{2,1,0:T(8,128)(2,1)}, bf16[3,4096,128]{2,1,0:T(8,128)(2,1)}, u32[]{:S(2)}, u32[]{:S(2)}) collective-permute-start(bf16[3,4096,128]{2,1,0:T(8,128)(2,1)} %own_ref.1), channel_id=1, source_target_pairs={{0,1},{1,0},{2,3},{3,2},{4,5},{5,4},{6,7},{7,6},{8,9},{9,8},{10,11... | collective-permute-start | bytes 9437192 | tf_op jit(solution)/shard_map/ppermute | solution.py:21
  2.2 17.3 %collective-permute-start = (bf16[128,1024]{1,0:T(8,128)(2,1)S(1)}, bf16[128,1024]{1,0:T(8,128)(2,1)S(1)}, u32[]{:S(2)}, u32[]{:S(2)}) collective-permute-start(bf16[128,1024]{1,0:T(8,128)(2,1)S(1)} %get-tuple-element.38), channel_id=1, source_target_pairs={{0,6},{2,0},{4,2},{6,4},{1,7},{3,1},{5,3},{7,5},{8,14},{10,8},{12,... | collective-permute-start | bytes 786440 | tf_op jit(solution)/shard_map/ppermute | solution.py:21
  5.0 15.6 %collective-permute-start.2 = (bf16[128,1024]{1,0:T(8,128)(2,1)S(1)}, bf16[128,1024]{1,0:T(8,128)(2,1)}, u32[]{:S(2)}, u32[]{:S(2)}) collective-permute-start(bf16[128,1024]{1,0:T(8,128)(2,1)S(1)} %get-tuple-element.40), channel_id=1, source_target_pairs={{0,2},{2,4},{4,6},{6,0},{1,3},{3,5},{5,7},{7,1},{8,10},{10,12},{12... | collective-permute-start | bytes 786440 | tf_op jit(solution)/shard_map/ppermute | solution.py:21
  5.0 15.6 %collective-permute-start.1 = (bf16[128,1024]{1,0:T(8,128)(2,1)S(1)}, bf16[128,1024]{1,0:T(8,128)(2,1)}, u32[]{:S(2)}, u32[]{:S(2)}) collective-permute-start(bf16[128,1024]{1,0:T(8,128)(2,1)S(1)} %get-tuple-element.39), channel_id=1, source_target_pairs={{0,4},{2,6},{4,0},{6,2},{1,5},{3,7},{5,1},{7,3},{8,12},{10,14},{12... | collective-permute-start | bytes 786440 | tf_op jit(solution)/shard_map/ppermute | solution.py:21
  8.7 21.1 %all-to-all-start = ((bf16[32,16,128]{2,1,0:T(8,128)(2,1)}), bf16[32,16,128]{2,1,0:T(8,128)(2,1)S(1)}, u32[]{:S(2)}, u32[]{:S(2)}) async-start(bf16[32,16,128]{2,1,0:T(8,128)(2,1)} %broadcast_in_dim.16), calls=%async_computation | async-start | bytes 262144 | tf_op jit(solution)/shard_map/all_to_all | solution.py:273
  19.6 1.1 copy-start.7
  20.7 9.1 %copy-start.4 = (f32[4,128]{1,0:T(4,128)S(1)}, f32[4,128]{1,0:T(4,128)}, u32[]{:S(2)}) copy-start(f32[4,128]{1,0:T(4,128)} %head_gain_ref.1) | copy-start | bytes 6148
  21.9 10.8 %collective-permute-start.3 = (bf16[4,128,1024]{2,1,0:T(8,128)(2,1)S(1)}, bf16[4,128,1024]{2,1,0:T(8,128)(2,1)}, u32[]{:S(2)}, u32[]{:S(2)}) collective-permute-start(bf16[4,128,1024]{2,1,0:T(8,128)(2,1)S(1)} %pad_maximum_fusion.own_ref), channel_id=1, source_target_pairs={{0,1},{1,0},{2,3},{3,2},{4,5},{5,4},{6,7},{7,6},{8,9},{9,8},{10,11... | collective-permute-start | bytes 3145736 | tf_op jit(solution)/shard_map/ppermute | solution.py:21
  22.3 1.9 %copy-start.2 = (bf16[3,4096,128]{2,1,0:T(8,128)(2,1)S(1)}, bf16[3,4096,128]{2,1,0:T(8,128)(2,1)}, u32[]{:S(2)}) copy-start(bf16[3,4096,128]{2,1,0:T(8,128)(2,1)} %weight_ref.1) | copy-start | bytes 9437188
  29.8 22.2 %copy-start.5 = (bf16[128,4096]{1,0:T(8,128)(2,1)S(1)}, bf16[128,4096]{1,0:T(8,128)(2,1)}, u32[]{:S(2)}) copy-start(bf16[128,4096]{1,0:T(8,128)(2,1)} %param.18) | copy-start | bytes 3145732
  51.9 12.6 %copy-start.6 = (bf16[128,4096]{1,0:T(8,128)(2,1)S(1)}, bf16[128,4096]{1,0:T(8,128)(2,1)}, u32[]{:S(2)}) copy-start(bf16[128,4096]{1,0:T(8,128)(2,1)} %param.20) | copy-start | bytes 3145732
  55.9 10.7 %collective-permute-start.5 = (bf16[64,1024]{1,0:T(8,128)(2,1)S(1)}, bf16[64,1024]{1,0:T(8,128)(2,1)S(1)}, u32[]{:S(2)}, u32[]{:S(2)}) collective-permute-start(bf16[64,1024]{1,0:T(8,128)(2,1)S(1)} %get-tuple-element.41), channel_id=1, source_target_pairs={{0,8},{8,16},{16,24},{24,0},{1,9},{9,17},{17,25},{25,1},{2,10},{10... | collective-permute-start | bytes 393224 | tf_op jit(solution)/shard_map/ppermute | solution.py:21
  57.4 12.8 %collective-permute-start.6 = (bf16[64,1024]{1,0:T(8,128)(2,1)S(1)}, bf16[64,1024]{1,0:T(8,128)(2,1)S(1)}, u32[]{:S(2)}, u32[]{:S(2)}) collective-permute-start(bf16[64,1024]{1,0:T(8,128)(2,1)S(1)} %get-tuple-element.43), channel_id=1, source_target_pairs={{0,24},{8,0},{16,8},{24,16},{1,25},{9,1},{17,9},{25,17},{2,26},{10... | collective-permute-start | bytes 393224 | tf_op jit(solution)/shard_map/ppermute | solution.py:21
  60.1 11.0 %collective-permute-start.7 = (bf16[64,1024]{1,0:T(8,128)(2,1)S(1)}, bf16[64,1024]{1,0:T(8,128)(2,1)S(1)}, u32[]{:S(2)}, u32[]{:S(2)}) collective-permute-start(bf16[64,1024]{1,0:T(8,128)(2,1)S(1)} %get-tuple-element.42), channel_id=1, source_target_pairs={{0,16},{8,24},{16,0},{24,8},{1,17},{9,25},{17,1},{25,9},{2,18},{10... | collective-permute-start | bytes 393224 | tf_op jit(solution)/shard_map/ppermute | solution.py:21
  65.0 6.2 %collective-permute-start.8 = (bf16[256,128]{1,0:T(8,128)(2,1)S(1)}, bf16[256,128]{1,0:T(8,128)(2,1)S(1)}, u32[]{:S(2)}, u32[]{:S(2)}) collective-permute-start(bf16[256,128]{1,0:T(8,128)(2,1)S(1)} %pad_maximum_fusion.2), channel_id=1, source_target_pairs={{0,1},{1,0},{2,3},{3,2},{4,5},{5,4},{6,7},{7,6},{8,9},{9,8},{10,11... | collective-permute-start | bytes 196616 | tf_op jit(solution)/shard_map/ppermute | solution.py:21
  71.2 9.1 %collective-permute-start.12 = (bf16[64,1024]{1,0:T(8,128)(2,1)S(1)}, bf16[64,1024]{1,0:T(8,128)(2,1)S(1)}, u32[]{:S(2)}, u32[]{:S(2)}) collective-permute-start(bf16[64,1024]{1,0:T(8,128)(2,1)S(1)} %add_convert_fusion), channel_id=1, source_target_pairs={{0,16},{8,24},{16,0},{24,8},{1,17},{9,25},{17,1},{25,9},{2,18},{10... | collective-permute-start | bytes 393224 | tf_op jit(solution)/shard_map/ppermute | solution.py:21
  74.8 11.2 %collective-permute-start.13 = (bf16[64,1024]{1,0:T(8,128)(2,1)S(1)}, bf16[64,1024]{1,0:T(8,128)(2,1)S(1)}, u32[]{:S(2)}, u32[]{:S(2)}) collective-permute-start(bf16[64,1024]{1,0:T(8,128)(2,1)S(1)} %add_convert_fusion), channel_id=1, source_target_pairs={{0,8},{8,16},{16,24},{24,0},{1,9},{9,17},{17,25},{25,1},{2,10},{10... | collective-permute-start | bytes 393224 | tf_op jit(solution)/shard_map/ppermute | solution.py:21
  78.1 8.6 %collective-permute-start.9 = (bf16[64,1024]{1,0:T(8,128)(2,1)S(1)}, bf16[64,1024]{1,0:T(8,128)(2,1)S(1)}, u32[]{:S(2)}, u32[]{:S(2)}) collective-permute-start(bf16[64,1024]{1,0:T(8,128)(2,1)S(1)} %add_convert_fusion), channel_id=1, source_target_pairs={{0,24},{8,0},{16,8},{24,16},{1,25},{9,1},{17,9},{25,17},{2,26},{10... | collective-permute-start | bytes 393224 | tf_op jit(solution)/shard_map/ppermute | solution.py:21
  86.0 9.2 %collective-permute-start.14 = (bf16[128,1024]{1,0:T(8,128)(2,1)S(1)}, bf16[128,1024]{1,0:T(8,128)(2,1)S(1)}, u32[]{:S(2)}, u32[]{:S(2)}) collective-permute-start(bf16[128,1024]{1,0:T(8,128)(2,1)S(1)} %constant_dynamic-update-slice_fusion.2.b0), channel_id=1, source_target_pairs={{0,6},{2,0},{4,2},{6,4},{1,7},{3,1},{5,3},{7,5},{8,14},{10,8},{12,... | collective-permute-start | bytes 786440 | tf_op jit(solution)/shard_map/ppermute | solution.py:21
  86.8 10.5 %collective-permute-start.10 = (bf16[128,1024]{1,0:T(8,128)(2,1)S(1)}, bf16[128,1024]{1,0:T(8,128)(2,1)S(1)}, u32[]{:S(2)}, u32[]{:S(2)}) collective-permute-start(bf16[128,1024]{1,0:T(8,128)(2,1)S(1)} %constant_dynamic-update-slice_fusion.a0), channel_id=1, source_target_pairs={{0,2},{2,4},{4,6},{6,0},{1,3},{3,5},{5,7},{7,1},{8,10},{10,12},{12... | collective-permute-start | bytes 786440 | tf_op jit(solution)/shard_map/ppermute | solution.py:21
  88.5 14.4 %collective-permute-start.17 = (bf16[128,1024]{1,0:T(8,128)(2,1)S(1)}, bf16[128,1024]{1,0:T(8,128)(2,1)S(1)}, u32[]{:S(2)}, u32[]{:S(2)}) collective-permute-start(bf16[128,1024]{1,0:T(8,128)(2,1)S(1)} %constant_dynamic-update-slice_fusion.2.b0), channel_id=1, source_target_pairs={{0,2},{2,4},{4,6},{6,0},{1,3},{3,5},{5,7},{7,1},{8,10},{10,12},{12... | collective-permute-start | bytes 786440 | tf_op jit(solution)/shard_map/ppermute | solution.py:21
  90.0 12.9 %collective-permute-start.16 = (bf16[128,1024]{1,0:T(8,128)(2,1)S(1)}, bf16[128,1024]{1,0:T(8,128)(2,1)S(1)}, u32[]{:S(2)}, u32[]{:S(2)}) collective-permute-start(bf16[128,1024]{1,0:T(8,128)(2,1)S(1)} %constant_dynamic-update-slice_fusion.a0), channel_id=1, source_target_pairs={{0,6},{2,0},{4,2},{6,4},{1,7},{3,1},{5,3},{7,5},{8,14},{10,8},{12,... | collective-permute-start | bytes 786440 | tf_op jit(solution)/shard_map/ppermute | solution.py:21
  95.2 10.3 %collective-permute-start.15 = (bf16[128,1024]{1,0:T(8,128)(2,1)S(1)}, bf16[128,1024]{1,0:T(8,128)(2,1)S(1)}, u32[]{:S(2)}, u32[]{:S(2)}) collective-permute-start(bf16[128,1024]{1,0:T(8,128)(2,1)S(1)} %collective-permute-done.14.b1), channel_id=1, source_target_pairs={{0,6},{2,0},{4,2},{6,4},{1,7},{3,1},{5,3},{7,5},{8,14},{10,8},{12,... | collective-permute-start | bytes 786440 | tf_op jit(solution)/shard_map/ppermute | solution.py:21
  97.3 9.5 %collective-permute-start.11 = (bf16[128,1024]{1,0:T(8,128)(2,1)S(1)}, bf16[128,1024]{1,0:T(8,128)(2,1)S(1)}, u32[]{:S(2)}, u32[]{:S(2)}) collective-permute-start(bf16[128,1024]{1,0:T(8,128)(2,1)S(1)} %collective-permute-done.10.a3), channel_id=1, source_target_pairs={{0,2},{2,4},{4,6},{6,0},{1,3},{3,5},{5,7},{7,1},{8,10},{10,12},{12... | collective-permute-start | bytes 786440 | tf_op jit(solution)/shard_map/ppermute | solution.py:21
  97.7 1.9 %copy-start.3 = (bf16[3,4096,128]{2,1,0:T(8,128)(2,1)S(1)}, bf16[3,4096,128]{2,1,0:T(8,128)(2,1)}, u32[]{:S(2)}) copy-start(bf16[3,4096,128]{2,1,0:T(8,128)(2,1)} %own_ref.1) | copy-start | bytes 9437188
  106.9 14.1 %copy-start.11 = (f32[1000]{0:T(1024)S(1)}, f32[1000]{0:T(1024)}, u32[]{:S(2)}) copy-start(f32[1000]{0:T(1024)} %param.13) | copy-start | bytes 12004
  106.9 26.4 %copy-start.10 = (f32[8,2,128]{2,1,0:T(2,128)S(1)}, f32[8,2,128]{2,1,0:T(2,128)}, u32[]{:S(2)}) copy-start(f32[8,2,128]{2,1,0:T(2,128)} %param.11) | copy-start | bytes 24580
  109.6 23.2 %all-to-all-start.2 = ((f32[128,2,128]{2,1,0:T(2,128)}), f32[128,2,128]{2,1,0:T(2,128)S(1)}, u32[]{:S(2)}, u32[]{:S(2)}) async-start(f32[128,2,128]{2,1,0:T(2,128)} %bitcast.17), calls=%async_computation.2 | async-start | bytes 262144 | tf_op jit(solution)/shard_map/all_to_all | solution.py:396
  133.3 0.6 copy-start.8

commit v5 on v4

--- a/solution.py
+++ b/solution.py
@@ -55,18 +55,13 @@
     return (col == source(row)).astype(BF)
 
 
-def fold_kernel(embed_ref, temb_ref, gain_ref, weight_ref, fold_ref, bias_ref, held, sems):
+def fold_kernel(embed_ref, temb_ref, gain_ref, weight_ref, fold_ref, bias_ref):
     width = embed_ref.shape[1]
-    chunk = width // sems.shape[0]
-    copies = []
-    for step in range(sems.shape[0]):
-        rows = pl.ds(step * chunk, chunk)
-        copies.append(pltpu.make_async_copy(weight_ref.at[:, rows, :], held.at[:, rows, :], sems.at[step]))
-        copies[-1].start()
+    chunk = 512
     fold = jnp.zeros((HD, 3 * HD), F32)
     bias = jnp.zeros((16, 3 * HD), F32)
     row = lax.broadcasted_iota(jnp.int32, (16, chunk), 0)
-    for step in range(sems.shape[0]):
+    for step in range(width // chunk):
         columns = slice(step * chunk, (step + 1) * chunk)
         gain = gain_ref[:, columns]
         scaled = embed_ref[:, columns].astype(F32) * gain
@@ -75,8 +70,7 @@
         time = temb_ref[:, columns] * gain
         time_high = time.astype(BF).astype(F32)
         extra = jnp.where(row == 0, time_high, jnp.where(row == 1, time - time_high, 0.0)).astype(BF)
-        copies[step].wait()
-        weights = jnp.concatenate([held[i, columns, :] for i in range(3)], axis=1)
+        weights = jnp.concatenate([weight_ref[i, columns, :] for i in range(3)], axis=1)
         share = dot(jnp.concatenate([high, low, extra], axis=0), weights)
         fold = fold + (share[:HD] + share[HD : 2 * HD])
         bias = bias + share[2 * HD :]
@@ -281,9 +275,8 @@
     fold, bias = pl.pallas_call(
         fold_kernel,
         out_shape=(jax.ShapeDtypeStruct((2 * HD, 3 * HD), BF), jax.ShapeDtypeStruct((8, 3 * HD), F32)),
-        in_specs=[vmem, vmem, vmem, anywhere],
+        in_specs=[vmem] * 4,
         out_specs=(vmem, vmem),
-        scratch_shapes=[pltpu.VMEM((3, width, HD), BF), pltpu.SemaphoreType.DMA((8,))],
         compiler_params=pltpu.CompilerParams(vmem_limit_bytes=16 * 1024 * 1024),
         cost_estimate=pl.CostEstimate(flops=2 * 272 * 4096 * 384, bytes_accessed=1024, transcendentals=0),
         name="fold_projection",
@@ -314,11 +307,6 @@
     attended, out_other, time_other = lax.optimization_barrier((attended, out_other, time_other))
     regrouped = lax.all_to_all(attended, ("y", "zl", "x", "c"), split_axis=0, concat_axis=0, tiled=True)
 
-    regrouped, late_weight = lax.optimization_barrier((regrouped, noise_weight))
-    noise_fold = jnp.concatenate(
-        [dot(space_output, late_weight).astype(BF), dot(time_output, late_weight).astype(BF)]
-    )
-    noise_other = shift(noise_fold, "c", 1)
 
     share, base, att_own = pl.pallas_call(
         output_kernel,
@@ -343,6 +331,12 @@
         compiler_params=pltpu.CompilerParams(vmem_limit_bytes=32 * 1024 * 1024),
         name="space_output",
     )(places, regrouped, embed_weight, temb, out_own, out_other)
+
+    share, late_weight, late_latents = lax.optimization_barrier((share, noise_weight, latents))
+    noise_fold = jnp.concatenate(
+        [dot(space_output, late_weight).astype(BF), dot(time_output, late_weight).astype(BF)]
+    )
+    noise_other = shift(noise_fold, "c", 1)
 
     sent = {d: shift(share[64 * (d - 1) : 64 * d], "zh", d) for d in ORDER}
     for d in ORDER:
@@ -396,7 +390,8 @@
     noise = lax.all_to_all(noise, ("y", "zl", "zh", "x"), split_axis=0, concat_axis=0, tiled=True)
     total = jnp.sum(noise.reshape(8, 16, 2, HD), axis=1).reshape(16, HD)
 
-    own_first = (dot(lat_bf.reshape(16, HD), embed_weight) + temb).astype(BF)
+    lat_end = late_latents.astype(BF).reshape(16, HD)
+    own_first = (dot(lat_end, embed_weight) + temb).astype(BF)
     predicted_noise = (total + dot(own_first, noise_weight)).reshape(latents.shape)
     latents_next = (
         jnp.sqrt(alpha_next)

time: 134 us -> 134 us (level)
  starting transfers between devices: 50.2 us -> 51.9 us
    ppermute x18, starting transfers between devices: 28.8 us -> 32.8 us  [shift(): lax.ppermute(value, axis, [(i, (i + step) % size) for i in range(size)])]
    ppermute x18, waiting for transfers between devices: 20.5 us -> 18.2 us  [shift(): lax.ppermute(value, axis, [(i, (i + step) % size) for i in range(size)])]
    all_to_all x1, starting transfers between devices: 11.3 us -> 9.08 us  [body(): lax.all_to_all(noise, ('y', 'zl', 'zh', 'x'), split_axis=0, concat_axis=0...]
  transfers between devices with their start and end apart: 20 -> 20, of which waited for: 13 -> 10; matrix products, arithmetic and copies ran while one was open for 5% -> 5% of each run, Pallas kernels for 8% -> 7%
where the time goes in v5:
time: 134 us; the launch traced here: 133 us
  starting transfers between devices  51.9 us (39%)
  waiting for transfers between devices  30.8 us (23%)
  blocking collectives  19.2 us (14%)
  Pallas kernels  15 us (11%)
  local copies, waits for them, and re-layouts  7.01 us (5%)
  between operations  4.49 us (3%)
  other arithmetic  3.46 us (3%)
    ppermute x18, starting transfers between devices, shift(): lax.ppermute(value, axis, [(i, (i + step) % size) for i in range(size)])  32.8 us
    all_to_all x1, blocking collectives, body(): lax.all_to_all(attended, ('y', 'zl', 'x', 'c'), split_axis=0, concat_axis...  19.2 us
    ppermute x18, waiting for transfers between devices, shift(): lax.ppermute(value, axis, [(i, (i + step) % size) for i in range(size)])  18.2 us
    all_to_all x1, starting transfers between devices, body(): lax.all_to_all(lat_rows, ('zh', 'x', 'c'), split_axis=0, concat_axis=0, t...  10.1 us
    all_to_all x1, starting transfers between devices, body(): lax.all_to_all(noise, ('y', 'zl', 'zh', 'x'), split_axis=0, concat_axis=0...  9.08 us
    all_to_all x1, waiting for transfers between devices, body(): lax.all_to_all(noise, ('y', 'zl', 'zh', 'x'), split_axis=0, concat_axis=0...  8.49 us
    all_to_all x1, waiting for transfers between devices, body(): lax.all_to_all(lat_rows, ('zh', 'x', 'c'), split_axis=0, concat_axis=0, t...  4.12 us
    unnamed x26, local copies, waits for them, and re-layouts  3.84 us
  transfers between devices with their start and end apart: 20, of which 10 were waited for; matrix products, arithmetic and copies ran while one was open for 5% of the time, Pallas kernels for 7%

profile of v5, /device:TPU:8, one launch (start us, length us, event | category | flops | bytes accessed | tf_op | source)
XLA Modules:
  0.0 133.2 jit_solution(11894830669595819342)
XLA Ops:
  0.6 0.0 copy-start
  0.7 0.1 collective-permute-start.4
  0.8 1.4 %constant_dynamic-slice_fusion.2 = (bf16[128,1024]{1,0:T(8,128)(2,1)S(1)}, bf16[128,1024]{1,0:T(8,128)(2,1)S(1)}, bf16[128,1024]{1,0:T(8,128)(2,1)S(1)}) fusion(bf16[128,4096]{1,0:T(8,128)(2,1)} %param.18, s32[]{:T(128)S(6)} %select_n.51, s32[]{:T(128)S(6)} %select_n.55, s32[]{:T(128)S(6)} %select_n.57), kind=kLoop, calls=%fused_computation.33 | loop fusion | bytes 1572876 | tf_op jit(solution)/shard_map/dynamic_slice | solution.py:286
  2.2 2.8 %collective-permute-start = (bf16[128,1024]{1,0:T(8,128)(2,1)S(1)}, bf16[128,1024]{1,0:T(8,128)(2,1)S(1)}, u32[]{:S(2)}, u32[]{:S(2)}) collective-permute-start(bf16[128,1024]{1,0:T(8,128)(2,1)S(1)} %get-tuple-element.40), channel_id=1, source_target_pairs={{0,6},{2,0},{4,2},{6,4},{1,7},{3,1},{5,3},{7,5},{8,14},{10,8},{12,... | collective-permute-start | bytes 786440 | tf_op jit(solution)/shard_map/ppermute | solution.py:21
  5.0 0.0 collective-permute-start.2
  5.0 2.3 %collective-permute-start.1 = (bf16[128,1024]{1,0:T(8,128)(2,1)S(1)}, bf16[128,1024]{1,0:T(8,128)(2,1)}, u32[]{:S(2)}, u32[]{:S(2)}) collective-permute-start(bf16[128,1024]{1,0:T(8,128)(2,1)S(1)} %get-tuple-element.41), channel_id=1, source_target_pairs={{0,4},{2,6},{4,0},{6,2},{1,5},{3,7},{5,1},{7,3},{8,12},{10,14},{12... | collective-permute-start | bytes 786440 | tf_op jit(solution)/shard_map/ppermute | solution.py:21
  7.3 0.7 convert_element_type.36
  8.0 0.7 broadcast_in_dim.16
  8.7 10.1 %all-to-all-start = ((bf16[32,16,128]{2,1,0:T(8,128)(2,1)}), bf16[32,16,128]{2,1,0:T(8,128)(2,1)S(1)}, u32[]{:S(2)}, u32[]{:S(2)}) async-start(bf16[32,16,128]{2,1,0:T(8,128)(2,1)} %broadcast_in_dim.16), calls=%async_computation | async-start | bytes 262144 | tf_op jit(solution)/shard_map/all_to_all | solution.py:267
  19.5 0.1 fusion.6
  19.5 0.0 collective-permute-done
  19.6 1.1 dynamic-slice_bitcast_fusion
  20.6 0.0 collective-permute-done.2
  20.6 0.0 collective-permute-done.1
  20.7 0.0 copy-start.4
  20.7 1.2 pad_maximum_fusion.own_ref
  21.9 0.4 collective-permute-start.3
  22.3 0.0 copy-start.2
  22.4 1.9 %copy-done.2 = bf16[3,4096,128]{2,1,0:T(8,128)(2,1)S(1)} copy-done((bf16[3,4096,128]{2,1,0:T(8,128)(2,1)S(1)}, bf16[3,4096,128]{2,1,0:T(8,128)(2,1)}, u32[]{:S(2)}) %copy-start.2) | copy-done | bytes 3145752
  24.2 1.3 fold_projection.1
  25.6 0.1 pad_add_fusion.place_ref
  25.6 4.1 %all-to-all-done = bf16[32,16,128]{2,1,0:T(8,128)(2,1)S(1)} async-done(((bf16[32,16,128]{2,1,0:T(8,128)(2,1)}), bf16[32,16,128]{2,1,0:T(8,128)(2,1)S(1)}, u32[]{:S(2)}, u32[]{:S(2)}) %all-to-all-start) | async-done | bytes 131104 | tf_op jit(solution)/shard_map/all_to_all | solution.py:267
  29.8 2.9 %space_attention.1 = bf16[64,40,128]{2,1,0:T(8,128)(2,1)S(1)} custom-call(s32[3]{0:T(128)S(1)} %pad_add_fusion.place_ref, bf16[512,128]{1,0:T(8,128)(2,1)S(1)} %bitcast.41, bf16[128,4096]{1,0:T(8,128)(2,1)S(1)} %copy-done.1, f32[1,4096]{1,0:T(1,128)S(1)} %bitcast.43, bf16[256,384]{1,0:T(8,128)(2,1)S(1)} %get-tuple-element.20.fold_ref, ...), custom_call_target="tpu_custom_call" | custom-call | tf_op jit(solution)/shard_map/space_attention/pallas_call | solution.py:294
  32.7 0.0 collective-permute-done.3.other_ref
  32.7 0.0 collective-permute-done.4.other_ref
  32.7 19.2 %all_to_all.22.att_ref = bf16[64,40,128]{2,1,0:T(8,128)(2,1)S(1)} all-to-all(bf16[64,40,128]{2,1,0:T(8,128)(2,1)S(1)} %space_attention.1), channel_id=1, replica_groups=mesh['y'=4,'zl'=2,'zh'=4,'x'=4,'c'=2] {'y','zl','x','c'}, dimensions={0} | all-to-all | bytes 1310720 | tf_op jit(solution)/shard_map/all_to_all | solution.py:308
  51.9 3.4 %space_output.1 = (bf16[192,1024]{1,0:T(8,128)(2,1)S(1)}, f32[64,1024]{1,0:T(8,128)S(1)}, bf16[256,256]{1,0:T(8,128)(2,1)S(1)}) custom-call(s32[3]{0:T(128)S(1)} %pad_add_fusion.place_ref, bf16[64,40,128]{2,1,0:T(8,128)(2,1)S(1)} %all_to_all.22.att_ref, bf16[128,4096]{1,0:T(8,128)(2,1)S(1)} %copy-done.1, f32[1,4096]{1,0:T(1,128)S(1)} %bitcast.44, ...), custom_call_target="tpu_custom_call" | custom-call | tf_op jit(solution)/shard_map/space_output/pallas_call | solution.py:311
  55.4 0.4 fusion.2
  55.9 0.9 collective-permute-start.5
  56.8 3.3 %collective-permute-start.6 = (bf16[64,1024]{1,0:T(8,128)(2,1)S(1)}, bf16[64,1024]{1,0:T(8,128)(2,1)S(1)}, u32[]{:S(2)}, u32[]{:S(2)}) collective-permute-start(bf16[64,1024]{1,0:T(8,128)(2,1)S(1)} %get-tuple-element.45), channel_id=1, source_target_pairs={{0,24},{8,0},{16,8},{24,16},{1,25},{9,1},{17,9},{25,17},{2,26},{10... | collective-permute-start | bytes 393224 | tf_op jit(solution)/shard_map/ppermute | solution.py:21
  60.1 3.2 %collective-permute-start.7 = (bf16[64,1024]{1,0:T(8,128)(2,1)S(1)}, bf16[64,1024]{1,0:T(8,128)(2,1)S(1)}, u32[]{:S(2)}, u32[]{:S(2)}) collective-permute-start(bf16[64,1024]{1,0:T(8,128)(2,1)S(1)} %get-tuple-element.44), channel_id=1, source_target_pairs={{0,16},{8,24},{16,0},{24,8},{1,17},{9,25},{17,1},{25,9},{2,18},{10... | collective-permute-start | bytes 393224 | tf_op jit(solution)/shard_map/ppermute | solution.py:21
  63.3 0.4 fusion.3
  63.8 0.1 collective-permute-start.8
  63.9 2.4 %collective-permute-done.5 = bf16[64,1024]{1,0:T(8,128)(2,1)S(1)} collective-permute-done((bf16[64,1024]{1,0:T(8,128)(2,1)S(1)}, bf16[64,1024]{1,0:T(8,128)(2,1)S(1)}, u32[]{:S(2)}, u32[]{:S(2)}) %collective-permute-start.5) | collective-permute-done | bytes 131104 | tf_op jit(solution)/shard_map/ppermute | solution.py:21
  66.3 2.7 %collective-permute-done.6 = bf16[64,1024]{1,0:T(8,128)(2,1)S(1)} collective-permute-done((bf16[64,1024]{1,0:T(8,128)(2,1)S(1)}, bf16[64,1024]{1,0:T(8,128)(2,1)S(1)}, u32[]{:S(2)}, u32[]{:S(2)}) %collective-permute-start.6) | collective-permute-done | bytes 131104 | tf_op jit(solution)/shard_map/ppermute | solution.py:21
  69.0 3.6 %collective-permute-done.7 = bf16[64,1024]{1,0:T(8,128)(2,1)S(1)} collective-permute-done((bf16[64,1024]{1,0:T(8,128)(2,1)S(1)}, bf16[64,1024]{1,0:T(8,128)(2,1)S(1)}, u32[]{:S(2)}, u32[]{:S(2)}) %collective-permute-start.7) | collective-permute-done | bytes 131104 | tf_op jit(solution)/shard_map/ppermute | solution.py:21
  72.6 0.1 add_convert_fusion
  72.7 0.0 collective-permute-done.8
  72.7 3.3 %collective-permute-start.12 = (bf16[64,1024]{1,0:T(8,128)(2,1)S(1)}, bf16[64,1024]{1,0:T(8,128)(2,1)S(1)}, u32[]{:S(2)}, u32[]{:S(2)}) collective-permute-start(bf16[64,1024]{1,0:T(8,128)(2,1)S(1)} %add_convert_fusion), channel_id=1, source_target_pairs={{0,16},{8,24},{16,0},{24,8},{1,17},{9,25},{17,1},{25,9},{2,18},{10... | collective-permute-start | bytes 393224 | tf_op jit(solution)/shard_map/ppermute | solution.py:21
  76.0 0.0 collective-permute-start.13
  76.0 4.2 %collective-permute-start.9 = (bf16[64,1024]{1,0:T(8,128)(2,1)S(1)}, bf16[64,1024]{1,0:T(8,128)(2,1)S(1)}, u32[]{:S(2)}, u32[]{:S(2)}) collective-permute-start(bf16[64,1024]{1,0:T(8,128)(2,1)S(1)} %add_convert_fusion), channel_id=1, source_target_pairs={{0,24},{8,0},{16,8},{24,16},{1,25},{9,1},{17,9},{25,17},{2,26},{10... | collective-permute-start | bytes 393224 | tf_op jit(solution)/shard_map/ppermute | solution.py:21
  80.2 4.5 %collective-permute-done.12 = bf16[64,1024]{1,0:T(8,128)(2,1)S(1)} collective-permute-done((bf16[64,1024]{1,0:T(8,128)(2,1)S(1)}, bf16[64,1024]{1,0:T(8,128)(2,1)S(1)}, u32[]{:S(2)}, u32[]{:S(2)}) %collective-permute-start.12) | collective-permute-done | bytes 131104 | tf_op jit(solution)/shard_map/ppermute | solution.py:21
  84.7 0.5 collective-permute-done.13
  85.3 5.0 %collective-permute-start.14 = (bf16[128,1024]{1,0:T(8,128)(2,1)S(1)}, bf16[128,1024]{1,0:T(8,128)(2,1)S(1)}, u32[]{:S(2)}, u32[]{:S(2)}) collective-permute-start(bf16[128,1024]{1,0:T(8,128)(2,1)S(1)} %constant_dynamic-update-slice_fusion.2.b0), channel_id=1, source_target_pairs={{0,6},{2,0},{4,2},{6,4},{1,7},{3,1},{5,3},{7,5},{8,14},{10,8},{12,... | collective-permute-start | bytes 786440 | tf_op jit(solution)/shard_map/ppermute | solution.py:21
  90.3 0.0 collective-permute-done.9
  90.3 0.1 collective-permute-start.10
  90.4 0.1 collective-permute-start.17
  90.5 3.3 %collective-permute-start.16 = (bf16[128,1024]{1,0:T(8,128)(2,1)S(1)}, bf16[128,1024]{1,0:T(8,128)(2,1)S(1)}, u32[]{:S(2)}, u32[]{:S(2)}) collective-permute-start(bf16[128,1024]{1,0:T(8,128)(2,1)S(1)} %constant_dynamic-update-slice_fusion.a0), channel_id=1, source_target_pairs={{0,6},{2,0},{4,2},{6,4},{1,7},{3,1},{5,3},{7,5},{8,14},{10,8},{12,... | collective-permute-start | bytes 786440 | tf_op jit(solution)/shard_map/ppermute | solution.py:21
  93.8 3.1 %collective-permute-done.14.b1 = bf16[128,1024]{1,0:T(8,128)(2,1)S(1)} collective-permute-done((bf16[128,1024]{1,0:T(8,128)(2,1)S(1)}, bf16[128,1024]{1,0:T(8,128)(2,1)S(1)}, u32[]{:S(2)}, u32[]{:S(2)}) %collective-permute-start.14) | collective-permute-done | bytes 262176 | tf_op jit(solution)/shard_map/ppermute | solution.py:21
  96.9 3.7 %collective-permute-start.15 = (bf16[128,1024]{1,0:T(8,128)(2,1)S(1)}, bf16[128,1024]{1,0:T(8,128)(2,1)S(1)}, u32[]{:S(2)}, u32[]{:S(2)}) collective-permute-start(bf16[128,1024]{1,0:T(8,128)(2,1)S(1)} %collective-permute-done.14.b1), channel_id=1, source_target_pairs={{0,6},{2,0},{4,2},{6,4},{1,7},{3,1},{5,3},{7,5},{8,14},{10,8},{12,... | collective-permute-start | bytes 786440 | tf_op jit(solution)/shard_map/ppermute | solution.py:21
  100.6 0.2 collective-permute-done.10.a3
  100.8 0.0 collective-permute-start.11
  100.9 0.0 copy-start.3
  100.9 1.9 %copy-done.3 = bf16[3,4096,128]{2,1,0:T(8,128)(2,1)S(1)} copy-done((bf16[3,4096,128]{2,1,0:T(8,128)(2,1)S(1)}, bf16[3,4096,128]{2,1,0:T(8,128)(2,1)}, u32[]{:S(2)}) %copy-start.3) | copy-done | bytes 3145752
  102.8 2.7 %time_weights.1.held_ref = bf16[4,6,1024,128]{3,2,1,0:T(8,128)(2,1)S(1)} custom-call(s32[3]{0:T(128)S(1)} %pad_add_fusion.place_ref, bf16[3,4096,128]{2,1,0:T(8,128)(2,1)S(1)} %copy-done.3, bf16[3,4096,128]{2,1,0:T(8,128)(2,1)} %collective-permute-done.4.other_ref), custom_call_target="tpu_custom_call" | custom-call | flops 855638016 | bytes 1024 | tf_op jit(solution)/shard_map/time_weights/pallas_call | solution.py:357
  105.4 0.0 collective-permute-done.17.b3
  105.5 1.9 %time_projection.1 = (f32[256,768]{1,0:T(8,128)S(1)}, f32[256,128]{1,0:T(8,128)S(1)}) custom-call(s32[3]{0:T(128)S(1)} %pad_add_fusion.place_ref, bf16[128,1024]{1,0:T(8,128)(2,1)S(1)} %constant_dynamic-update-slice_fusion.a0, bf16[128,1024]{1,0:T(8,128)(2,1)S(1)} %constant_dynamic-update-slice_fusion.2.b0, ...), custom_call_target="tpu_custom_call" | custom-call | flops 1207959552 | bytes 8388608 | tf_op jit(solution)/shard_map/time_projection/pallas_call | solution.py:372
  107.4 1.0 collective-permute-done.11.a2
  108.4 2.7 %time_attention.1 = f32[256,128]{1,0:T(8,128)} custom-call(s32[3]{0:T(128)S(1)} %pad_add_fusion.place_ref, bf16[128,1024]{1,0:T(8,128)(2,1)S(1)} %collective-permute-done.11.a2, bf16[128,1024]{1,0:T(8,128)(2,1)S(1)} %collective-permute-done.15.b2, f32[4,1,1024]{2,1,0:T(1,128)S(1)} %bitcast.46, bf16[4,6,1024,128]{3,2,1,0:T(8,128)(2,1)S(1)} %time_weights.1.held_ref, ...), custom_call_target="tpu_custom_call" | custom-call | tf_op jit(solution)/shard_map/time_attention/pallas_call | solution.py:381
  111.2 9.1 %all-to-all-start.2 = ((f32[128,2,128]{2,1,0:T(2,128)}), f32[128,2,128]{2,1,0:T(2,128)S(1)}, u32[]{:S(2)}, u32[]{:S(2)}) async-start(f32[128,2,128]{2,1,0:T(2,128)} %bitcast.17), calls=%async_computation.2 | async-start | bytes 262144 | tf_op jit(solution)/shard_map/all_to_all | solution.py:390
  120.3 0.6 select_reduce_fusion
  123.7 8.5 %all-to-all-done.2 = f32[128,2,128]{2,1,0:T(2,128)S(1)} async-done(((f32[128,2,128]{2,1,0:T(2,128)}), f32[128,2,128]{2,1,0:T(2,128)S(1)}, u32[]{:S(2)}, u32[]{:S(2)}) %all-to-all-start.2) | async-done | bytes 131104 | tf_op jit(solution)/shard_map/all_to_all | solution.py:390
  132.2 0.4 fusion.4
  132.6 0.6 divide_add_fusion
  (33 shorter events, 0.2 us)
Async XLA Ops:
  0.6 54.8 %copy-start = (bf16[4096,128]{1,0:T(8,128)(2,1)S(1)}, bf16[4096,128]{1,0:T(8,128)(2,1)}, u32[]{:S(2)}) copy-start(bf16[4096,128]{1,0:T(8,128)(2,1)} %param.21) | copy-start | bytes 3145732
  0.6 21.6 %copy-start.10 = (f32[2,4096]{1,0:T(2,128)S(1)}, f32[2,4096]{1,0:T(2,128)}, u32[]{:S(2)}) copy-start(f32[2,4096]{1,0:T(2,128)} %param.14) | copy-start | bytes 98308
  0.7 21.7 %copy-start.1 = (bf16[128,4096]{1,0:T(8,128)(2,1)S(1)}, bf16[128,4096]{1,0:T(8,128)(2,1)}, u32[]{:S(2)}) copy-start(bf16[128,4096]{1,0:T(8,128)(2,1)} %embed_ref.5) | copy-start | bytes 3145732
  0.7 32.0 %collective-permute-start.4 = (bf16[3,4096,128]{2,1,0:T(8,128)(2,1)}, bf16[3,4096,128]{2,1,0:T(8,128)(2,1)}, u32[]{:S(2)}, u32[]{:S(2)}) collective-permute-start(bf16[3,4096,128]{2,1,0:T(8,128)(2,1)} %own_ref.1), channel_id=1, source_target_pairs={{0,1},{1,0},{2,3},{3,2},{4,5},{5,4},{6,7},{7,6},{8,9},{9,8},{10,11... | collective-permute-start | bytes 9437192 | tf_op jit(solution)/shard_map/ppermute | solution.py:21
  2.2 17.3 %collective-permute-start = (bf16[128,1024]{1,0:T(8,128)(2,1)S(1)}, bf16[128,1024]{1,0:T(8,128)(2,1)S(1)}, u32[]{:S(2)}, u32[]{:S(2)}) collective-permute-start(bf16[128,1024]{1,0:T(8,128)(2,1)S(1)} %get-tuple-element.40), channel_id=1, source_target_pairs={{0,6},{2,0},{4,2},{6,4},{1,7},{3,1},{5,3},{7,5},{8,14},{10,8},{12,... | collective-permute-start | bytes 786440 | tf_op jit(solution)/shard_map/ppermute | solution.py:21
  5.0 15.6 %collective-permute-start.2 = (bf16[128,1024]{1,0:T(8,128)(2,1)S(1)}, bf16[128,1024]{1,0:T(8,128)(2,1)}, u32[]{:S(2)}, u32[]{:S(2)}) collective-permute-start(bf16[128,1024]{1,0:T(8,128)(2,1)S(1)} %get-tuple-element.42), channel_id=1, source_target_pairs={{0,2},{2,4},{4,6},{6,0},{1,3},{3,5},{5,7},{7,1},{8,10},{10,12},{12... | collective-permute-start | bytes 786440 | tf_op jit(solution)/shard_map/ppermute | solution.py:21
  5.0 15.6 %collective-permute-start.1 = (bf16[128,1024]{1,0:T(8,128)(2,1)S(1)}, bf16[128,1024]{1,0:T(8,128)(2,1)}, u32[]{:S(2)}, u32[]{:S(2)}) collective-permute-start(bf16[128,1024]{1,0:T(8,128)(2,1)S(1)} %get-tuple-element.41), channel_id=1, source_target_pairs={{0,4},{2,6},{4,0},{6,2},{1,5},{3,7},{5,1},{7,3},{8,12},{10,14},{12... | collective-permute-start | bytes 786440 | tf_op jit(solution)/shard_map/ppermute | solution.py:21
  8.7 21.1 %all-to-all-start = ((bf16[32,16,128]{2,1,0:T(8,128)(2,1)}), bf16[32,16,128]{2,1,0:T(8,128)(2,1)S(1)}, u32[]{:S(2)}, u32[]{:S(2)}) async-start(bf16[32,16,128]{2,1,0:T(8,128)(2,1)} %broadcast_in_dim.16), calls=%async_computation | async-start | bytes 262144 | tf_op jit(solution)/shard_map/all_to_all | solution.py:267
  19.6 1.1 copy-start.7
  20.7 9.1 %copy-start.4 = (f32[4,128]{1,0:T(4,128)S(1)}, f32[4,128]{1,0:T(4,128)}, u32[]{:S(2)}) copy-start(f32[4,128]{1,0:T(4,128)} %head_gain_ref.1) | copy-start | bytes 6148
  21.9 10.8 %collective-permute-start.3 = (bf16[4,128,1024]{2,1,0:T(8,128)(2,1)S(1)}, bf16[4,128,1024]{2,1,0:T(8,128)(2,1)}, u32[]{:S(2)}, u32[]{:S(2)}) collective-permute-start(bf16[4,128,1024]{2,1,0:T(8,128)(2,1)S(1)} %pad_maximum_fusion.own_ref), channel_id=1, source_target_pairs={{0,1},{1,0},{2,3},{3,2},{4,5},{5,4},{6,7},{7,6},{8,9},{9,8},{10,11... | collective-permute-start | bytes 3145736 | tf_op jit(solution)/shard_map/ppermute | solution.py:21
  22.3 1.9 %copy-start.2 = (bf16[3,4096,128]{2,1,0:T(8,128)(2,1)S(1)}, bf16[3,4096,128]{2,1,0:T(8,128)(2,1)}, u32[]{:S(2)}) copy-start(bf16[3,4096,128]{2,1,0:T(8,128)(2,1)} %weight_ref.1) | copy-start | bytes 9437188
  29.8 25.6 %copy-start.5 = (bf16[128,4096]{1,0:T(8,128)(2,1)S(1)}, bf16[128,4096]{1,0:T(8,128)(2,1)}, u32[]{:S(2)}) copy-start(bf16[128,4096]{1,0:T(8,128)(2,1)} %param.18) | copy-start | bytes 3145732
  51.9 11.4 %copy-start.6 = (bf16[128,4096]{1,0:T(8,128)(2,1)S(1)}, bf16[128,4096]{1,0:T(8,128)(2,1)}, u32[]{:S(2)}) copy-start(bf16[128,4096]{1,0:T(8,128)(2,1)} %param.20) | copy-start | bytes 3145732
  55.9 10.4 %collective-permute-start.5 = (bf16[64,1024]{1,0:T(8,128)(2,1)S(1)}, bf16[64,1024]{1,0:T(8,128)(2,1)S(1)}, u32[]{:S(2)}, u32[]{:S(2)}) collective-permute-start(bf16[64,1024]{1,0:T(8,128)(2,1)S(1)} %get-tuple-element.43), channel_id=1, source_target_pairs={{0,8},{8,16},{16,24},{24,0},{1,9},{9,17},{17,25},{25,1},{2,10},{10... | collective-permute-start | bytes 393224 | tf_op jit(solution)/shard_map/ppermute | solution.py:21
  56.8 12.2 %collective-permute-start.6 = (bf16[64,1024]{1,0:T(8,128)(2,1)S(1)}, bf16[64,1024]{1,0:T(8,128)(2,1)S(1)}, u32[]{:S(2)}, u32[]{:S(2)}) collective-permute-start(bf16[64,1024]{1,0:T(8,128)(2,1)S(1)} %get-tuple-element.45), channel_id=1, source_target_pairs={{0,24},{8,0},{16,8},{24,16},{1,25},{9,1},{17,9},{25,17},{2,26},{10... | collective-permute-start | bytes 393224 | tf_op jit(solution)/shard_map/ppermute | solution.py:21
  60.1 12.6 %collective-permute-start.7 = (bf16[64,1024]{1,0:T(8,128)(2,1)S(1)}, bf16[64,1024]{1,0:T(8,128)(2,1)S(1)}, u32[]{:S(2)}, u32[]{:S(2)}) collective-permute-start(bf16[64,1024]{1,0:T(8,128)(2,1)S(1)} %get-tuple-element.44), channel_id=1, source_target_pairs={{0,16},{8,24},{16,0},{24,8},{1,17},{9,25},{17,1},{25,9},{2,18},{10... | collective-permute-start | bytes 393224 | tf_op jit(solution)/shard_map/ppermute | solution.py:21
  63.8 9.0 %collective-permute-start.8 = (bf16[256,128]{1,0:T(8,128)(2,1)S(1)}, bf16[256,128]{1,0:T(8,128)(2,1)S(1)}, u32[]{:S(2)}, u32[]{:S(2)}) collective-permute-start(bf16[256,128]{1,0:T(8,128)(2,1)S(1)} %pad_maximum_fusion.2), channel_id=1, source_target_pairs={{0,1},{1,0},{2,3},{3,2},{4,5},{5,4},{6,7},{7,6},{8,9},{9,8},{10,11... | collective-permute-start | bytes 196616 | tf_op jit(solution)/shard_map/ppermute | solution.py:21
  72.7 12.0 %collective-permute-start.12 = (bf16[64,1024]{1,0:T(8,128)(2,1)S(1)}, bf16[64,1024]{1,0:T(8,128)(2,1)S(1)}, u32[]{:S(2)}, u32[]{:S(2)}) collective-permute-start(bf16[64,1024]{1,0:T(8,128)(2,1)S(1)} %add_convert_fusion), channel_id=1, source_target_pairs={{0,16},{8,24},{16,0},{24,8},{1,17},{9,25},{17,1},{25,9},{2,18},{10... | collective-permute-start | bytes 393224 | tf_op jit(solution)/shard_map/ppermute | solution.py:21
  76.0 9.3 %collective-permute-start.13 = (bf16[64,1024]{1,0:T(8,128)(2,1)S(1)}, bf16[64,1024]{1,0:T(8,128)(2,1)S(1)}, u32[]{:S(2)}, u32[]{:S(2)}) collective-permute-start(bf16[64,1024]{1,0:T(8,128)(2,1)S(1)} %add_convert_fusion), channel_id=1, source_target_pairs={{0,8},{8,16},{16,24},{24,0},{1,9},{9,17},{17,25},{25,1},{2,10},{10... | collective-permute-start | bytes 393224 | tf_op jit(solution)/shard_map/ppermute | solution.py:21
  76.0 14.3 %collective-permute-start.9 = (bf16[64,1024]{1,0:T(8,128)(2,1)S(1)}, bf16[64,1024]{1,0:T(8,128)(2,1)S(1)}, u32[]{:S(2)}, u32[]{:S(2)}) collective-permute-start(bf16[64,1024]{1,0:T(8,128)(2,1)S(1)} %add_convert_fusion), channel_id=1, source_target_pairs={{0,24},{8,0},{16,8},{24,16},{1,25},{9,1},{17,9},{25,17},{2,26},{10... | collective-permute-start | bytes 393224 | tf_op jit(solution)/shard_map/ppermute | solution.py:21
  85.3 11.6 %collective-permute-start.14 = (bf16[128,1024]{1,0:T(8,128)(2,1)S(1)}, bf16[128,1024]{1,0:T(8,128)(2,1)S(1)}, u32[]{:S(2)}, u32[]{:S(2)}) collective-permute-start(bf16[128,1024]{1,0:T(8,128)(2,1)S(1)} %constant_dynamic-update-slice_fusion.2.b0), channel_id=1, source_target_pairs={{0,6},{2,0},{4,2},{6,4},{1,7},{3,1},{5,3},{7,5},{8,14},{10,8},{12,... | collective-permute-start | bytes 786440 | tf_op jit(solution)/shard_map/ppermute | solution.py:21
  90.3 10.5 %collective-permute-start.10 = (bf16[128,1024]{1,0:T(8,128)(2,1)S(1)}, bf16[128,1024]{1,0:T(8,128)(2,1)S(1)}, u32[]{:S(2)}, u32[]{:S(2)}) collective-permute-start(bf16[128,1024]{1,0:T(8,128)(2,1)S(1)} %constant_dynamic-update-slice_fusion.a0), channel_id=1, source_target_pairs={{0,2},{2,4},{4,6},{6,0},{1,3},{3,5},{5,7},{7,1},{8,10},{10,12},{12... | collective-permute-start | bytes 786440 | tf_op jit(solution)/shard_map/ppermute | solution.py:21
  90.4 15.0 %collective-permute-start.17 = (bf16[128,1024]{1,0:T(8,128)(2,1)S(1)}, bf16[128,1024]{1,0:T(8,128)(2,1)S(1)}, u32[]{:S(2)}, u32[]{:S(2)}) collective-permute-start(bf16[128,1024]{1,0:T(8,128)(2,1)S(1)} %constant_dynamic-update-slice_fusion.2.b0), channel_id=1, source_target_pairs={{0,2},{2,4},{4,6},{6,0},{1,3},{3,5},{5,7},{7,1},{8,10},{10,12},{12... | collective-permute-start | bytes 786440 | tf_op jit(solution)/shard_map/ppermute | solution.py:21
  90.5 14.9 %collective-permute-start.16 = (bf16[128,1024]{1,0:T(8,128)(2,1)S(1)}, bf16[128,1024]{1,0:T(8,128)(2,1)S(1)}, u32[]{:S(2)}, u32[]{:S(2)}) collective-permute-start(bf16[128,1024]{1,0:T(8,128)(2,1)S(1)} %constant_dynamic-update-slice_fusion.a0), channel_id=1, source_target_pairs={{0,6},{2,0},{4,2},{6,4},{1,7},{3,1},{5,3},{7,5},{8,14},{10,8},{12,... | collective-permute-start | bytes 786440 | tf_op jit(solution)/shard_map/ppermute | solution.py:21
  96.9 10.5 %collective-permute-start.15 = (bf16[128,1024]{1,0:T(8,128)(2,1)S(1)}, bf16[128,1024]{1,0:T(8,128)(2,1)S(1)}, u32[]{:S(2)}, u32[]{:S(2)}) collective-permute-start(bf16[128,1024]{1,0:T(8,128)(2,1)S(1)} %collective-permute-done.14.b1), channel_id=1, source_target_pairs={{0,6},{2,0},{4,2},{6,4},{1,7},{3,1},{5,3},{7,5},{8,14},{10,8},{12,... | collective-permute-start | bytes 786440 | tf_op jit(solution)/shard_map/ppermute | solution.py:21
  100.8 7.6 %collective-permute-start.11 = (bf16[128,1024]{1,0:T(8,128)(2,1)S(1)}, bf16[128,1024]{1,0:T(8,128)(2,1)S(1)}, u32[]{:S(2)}, u32[]{:S(2)}) collective-permute-start(bf16[128,1024]{1,0:T(8,128)(2,1)S(1)} %collective-permute-done.10.a3), channel_id=1, source_target_pairs={{0,2},{2,4},{4,6},{6,0},{1,3},{3,5},{5,7},{7,1},{8,10},{10,12},{12... | collective-permute-start | bytes 786440 | tf_op jit(solution)/shard_map/ppermute | solution.py:21
  100.9 1.9 %copy-start.3 = (bf16[3,4096,128]{2,1,0:T(8,128)(2,1)S(1)}, bf16[3,4096,128]{2,1,0:T(8,128)(2,1)}, u32[]{:S(2)}) copy-start(bf16[3,4096,128]{2,1,0:T(8,128)(2,1)} %own_ref.1) | copy-start | bytes 9437188
  108.4 11.8 %copy-start.11 = (f32[1000]{0:T(1024)S(1)}, f32[1000]{0:T(1024)}, u32[]{:S(2)}) copy-start(f32[1000]{0:T(1024)} %param.13) | copy-start | bytes 12004
  108.4 15.2 %copy-start.8 = (f32[8,2,128]{2,1,0:T(2,128)S(1)}, f32[8,2,128]{2,1,0:T(2,128)}, u32[]{:S(2)}) copy-start(f32[8,2,128]{2,1,0:T(2,128)} %param.11) | copy-start | bytes 24580
  111.2 21.0 %all-to-all-start.2 = ((f32[128,2,128]{2,1,0:T(2,128)}), f32[128,2,128]{2,1,0:T(2,128)S(1)}, u32[]{:S(2)}, u32[]{:S(2)}) async-start(f32[128,2,128]{2,1,0:T(2,128)} %bitcast.17), calls=%async_computation.2 | async-start | bytes 262144 | tf_op jit(solution)/shard_map/all_to_all | solution.py:390
  132.6 0.6 copy-start.9

commit v6 on v5

--- a/solution.py
+++ b/solution.py
@@ -115,11 +115,11 @@
         for side in range(2):
             rows = slice(tm * 32 + side * 16, tm * 32 + side * 16 + 16)
             message = jnp.concatenate([part[rows] for part in parts[:2]], axis=0)
-            extra = parts[2][rows][:8]
+            extra = parts[2][rows]
             for x in range(NX):
                 place = (tm * NX + x) * 2 + side
                 out_ref[place, :32, :] = message
-                out_ref[place, 32:40, :] = extra
+                out_ref[place, 32:48, :] = extra
 
 
 def output_kernel(
@@ -143,10 +143,9 @@
             att_own_ref[...] = rows
 
     rows = jnp.concatenate(
-        [att_ref[tm * NX * 2 + side, 32:40, :].astype(F32) for tm in range(8) for side in range(2)], axis=0
-    ).astype(BF)
-    pick = reorder(128, lambda row: ((row & 15) << 3) + (row >> 4))
-    lat = dot(pick[:64, :], rows).astype(BF)
+        [att_ref[tm * NX * 2 + side, 32:48, :] for tm in range(8) for side in range(2)], axis=0
+    )
+    lat = dot(swap[:64, :], rows).astype(BF)
 
     tile = 256
     for start in range(0, own_ref.shape[2], tile):
@@ -293,7 +292,7 @@
     time_other = shift(time_project, "c", 1)
     attended = pl.pallas_call(
         space_kernel,
-        out_shape=jax.ShapeDtypeStruct((64, 40, HD), BF),
+        out_shape=jax.ShapeDtypeStruct((64, 48, HD), BF),
         grid_spec=pltpu.PrefetchScalarGridSpec(
             num_scalar_prefetch=1,
             grid=(1,),

time: 134 us -> 136 us (1.015)
  starting transfers between devices: 51.9 us -> 53.5 us
  blocking collectives: 19.2 us -> 20.7 us
    all_to_all x1, blocking collectives: 19.2 us -> 20.7 us  [body(): lax.all_to_all(attended, ('y', 'zl', 'x', 'c'), split_axis=0, concat_axis...]
where the time goes in v6:
time: 136 us; the launch traced here: 135 us
  starting transfers between devices  53.5 us (39%)
  waiting for transfers between devices  29.8 us (22%)
  blocking collectives  20.7 us (15%)
  Pallas kernels  15 us (11%)
  local copies, waits for them, and re-layouts  7.01 us (5%)
  between operations  4.5 us (3%)
  other arithmetic  3.46 us (3%)
    ppermute x18, starting transfers between devices, shift(): lax.ppermute(value, axis, [(i, (i + step) % size) for i in range(size)])  33.3 us
    all_to_all x1, blocking collectives, body(): lax.all_to_all(attended, ('y', 'zl', 'x', 'c'), split_axis=0, concat_axis...  20.7 us
    ppermute x18, waiting for transfers between devices, shift(): lax.ppermute(value, axis, [(i, (i + step) % size) for i in range(size)])  17.2 us
    all_to_all x1, starting transfers between devices, body(): lax.all_to_all(lat_rows, ('zh', 'x', 'c'), split_axis=0, concat_axis=0, t...  10.1 us
    all_to_all x1, starting transfers between devices, body(): lax.all_to_all(noise, ('y', 'zl', 'zh', 'x'), split_axis=0, concat_axis=0...  10.1 us
    all_to_all x1, waiting for transfers between devices, body(): lax.all_to_all(noise, ('y', 'zl', 'zh', 'x'), split_axis=0, concat_axis=0...  8.51 us
    all_to_all x1, waiting for transfers between devices, body(): lax.all_to_all(lat_rows, ('zh', 'x', 'c'), split_axis=0, concat_axis=0, t...  4.12 us
    unnamed x26, local copies, waits for them, and re-layouts  3.84 us
  transfers between devices with their start and end apart: 20, of which 10 were waited for; matrix products, arithmetic and copies ran while one was open for 5% of the time, Pallas kernels for 7%

profile of v6, /device:TPU:8, one launch (start us, length us, event | category | flops | bytes accessed | tf_op | source)
XLA Modules:
  0.0 135.3 jit_solution(3760640737887465357)
XLA Ops:
  0.6 0.0 copy-start
  0.7 0.1 collective-permute-start.4
  0.8 1.4 %constant_dynamic-slice_fusion.2 = (bf16[128,1024]{1,0:T(8,128)(2,1)S(1)}, bf16[128,1024]{1,0:T(8,128)(2,1)S(1)}, bf16[128,1024]{1,0:T(8,128)(2,1)S(1)}) fusion(bf16[128,4096]{1,0:T(8,128)(2,1)} %param.18, s32[]{:T(128)S(6)} %select_n.51, s32[]{:T(128)S(6)} %select_n.55, s32[]{:T(128)S(6)} %select_n.57), kind=kLoop, calls=%fused_computation.33 | loop fusion | bytes 1572876 | tf_op jit(solution)/shard_map/dynamic_slice | solution.py:285
  2.2 2.8 %collective-permute-start = (bf16[128,1024]{1,0:T(8,128)(2,1)S(1)}, bf16[128,1024]{1,0:T(8,128)(2,1)S(1)}, u32[]{:S(2)}, u32[]{:S(2)}) collective-permute-start(bf16[128,1024]{1,0:T(8,128)(2,1)S(1)} %get-tuple-element.40), channel_id=1, source_target_pairs={{0,6},{2,0},{4,2},{6,4},{1,7},{3,1},{5,3},{7,5},{8,14},{10,8},{12,... | collective-permute-start | bytes 786440 | tf_op jit(solution)/shard_map/ppermute | solution.py:21
  5.0 0.0 collective-permute-start.2
  5.0 2.3 %collective-permute-start.1 = (bf16[128,1024]{1,0:T(8,128)(2,1)S(1)}, bf16[128,1024]{1,0:T(8,128)(2,1)}, u32[]{:S(2)}, u32[]{:S(2)}) collective-permute-start(bf16[128,1024]{1,0:T(8,128)(2,1)S(1)} %get-tuple-element.41), channel_id=1, source_target_pairs={{0,4},{2,6},{4,0},{6,2},{1,5},{3,7},{5,1},{7,3},{8,12},{10,14},{12... | collective-permute-start | bytes 786440 | tf_op jit(solution)/shard_map/ppermute | solution.py:21
  7.3 0.7 convert_element_type.36
  8.0 0.7 broadcast_in_dim.16
  8.7 10.1 %all-to-all-start = ((bf16[32,16,128]{2,1,0:T(8,128)(2,1)}), bf16[32,16,128]{2,1,0:T(8,128)(2,1)S(1)}, u32[]{:S(2)}, u32[]{:S(2)}) async-start(bf16[32,16,128]{2,1,0:T(8,128)(2,1)} %broadcast_in_dim.16), calls=%async_computation | async-start | bytes 262144 | tf_op jit(solution)/shard_map/all_to_all | solution.py:266
  19.5 0.1 fusion.6
  19.5 0.0 collective-permute-done
  19.6 1.1 dynamic-slice_bitcast_fusion
  20.6 0.0 collective-permute-done.2
  20.6 0.0 collective-permute-done.1
  20.7 0.0 copy-start.4
  20.7 1.2 pad_maximum_fusion.own_ref
  21.9 0.4 collective-permute-start.3
  22.3 0.0 copy-start.2
  22.4 1.9 %copy-done.2 = bf16[3,4096,128]{2,1,0:T(8,128)(2,1)S(1)} copy-done((bf16[3,4096,128]{2,1,0:T(8,128)(2,1)S(1)}, bf16[3,4096,128]{2,1,0:T(8,128)(2,1)}, u32[]{:S(2)}) %copy-start.2) | copy-done | bytes 3145752
  24.2 1.3 fold_projection.1
  25.6 0.1 pad_add_fusion.place_ref
  25.6 4.1 %all-to-all-done = bf16[32,16,128]{2,1,0:T(8,128)(2,1)S(1)} async-done(((bf16[32,16,128]{2,1,0:T(8,128)(2,1)}), bf16[32,16,128]{2,1,0:T(8,128)(2,1)S(1)}, u32[]{:S(2)}, u32[]{:S(2)}) %all-to-all-start) | async-done | bytes 131104 | tf_op jit(solution)/shard_map/all_to_all | solution.py:266
  29.8 2.9 %space_attention.1 = bf16[64,48,128]{2,1,0:T(8,128)(2,1)S(1)} custom-call(s32[3]{0:T(128)S(1)} %pad_add_fusion.place_ref, bf16[512,128]{1,0:T(8,128)(2,1)S(1)} %bitcast.41, bf16[128,4096]{1,0:T(8,128)(2,1)S(1)} %copy-done.1, f32[1,4096]{1,0:T(1,128)S(1)} %bitcast.43, bf16[256,384]{1,0:T(8,128)(2,1)S(1)} %get-tuple-element.20.fold_ref, ...), custom_call_target="tpu_custom_call" | custom-call | tf_op jit(solution)/shard_map/space_attention/pallas_call | solution.py:293
  32.7 0.0 copy-start.5
  32.7 0.0 collective-permute-done.3.other_ref
  32.7 0.0 collective-permute-done.4.other_ref
  32.7 20.7 %all_to_all.22.att_ref = bf16[64,48,128]{2,1,0:T(8,128)(2,1)S(1)} all-to-all(bf16[64,48,128]{2,1,0:T(8,128)(2,1)S(1)} %space_attention.1), channel_id=1, replica_groups=mesh['y'=4,'zl'=2,'zh'=4,'x'=4,'c'=2] {'y','zl','x','c'}, dimensions={0} | all-to-all | bytes 1572864 | tf_op jit(solution)/shard_map/all_to_all | solution.py:307
  53.4 3.4 %space_output.1 = (bf16[192,1024]{1,0:T(8,128)(2,1)S(1)}, f32[64,1024]{1,0:T(8,128)S(1)}, bf16[256,256]{1,0:T(8,128)(2,1)S(1)}) custom-call(s32[3]{0:T(128)S(1)} %pad_add_fusion.place_ref, bf16[64,48,128]{2,1,0:T(8,128)(2,1)S(1)} %all_to_all.22.att_ref, bf16[128,4096]{1,0:T(8,128)(2,1)S(1)} %copy-done.1, f32[1,4096]{1,0:T(1,128)S(1)} %bitcast.44, ...), custom_call_target="tpu_custom_call" | custom-call | tf_op jit(solution)/shard_map/space_output/pallas_call | solution.py:310
  56.9 0.4 fusion.2
  57.4 0.9 collective-permute-start.5
  58.3 3.3 %collective-permute-start.6 = (bf16[64,1024]{1,0:T(8,128)(2,1)S(1)}, bf16[64,1024]{1,0:T(8,128)(2,1)S(1)}, u32[]{:S(2)}, u32[]{:S(2)}) collective-permute-start(bf16[64,1024]{1,0:T(8,128)(2,1)S(1)} %get-tuple-element.45), channel_id=1, source_target_pairs={{0,24},{8,0},{16,8},{24,16},{1,25},{9,1},{17,9},{25,17},{2,26},{10... | collective-permute-start | bytes 393224 | tf_op jit(solution)/shard_map/ppermute | solution.py:21
  61.6 3.2 %collective-permute-start.7 = (bf16[64,1024]{1,0:T(8,128)(2,1)S(1)}, bf16[64,1024]{1,0:T(8,128)(2,1)S(1)}, u32[]{:S(2)}, u32[]{:S(2)}) collective-permute-start(bf16[64,1024]{1,0:T(8,128)(2,1)S(1)} %get-tuple-element.44), channel_id=1, source_target_pairs={{0,16},{8,24},{16,0},{24,8},{1,17},{9,25},{17,1},{25,9},{2,18},{10... | collective-permute-start | bytes 393224 | tf_op jit(solution)/shard_map/ppermute | solution.py:21
  64.8 0.4 fusion.3
  65.2 0.1 collective-permute-start.8
  65.3 2.0 %collective-permute-done.5 = bf16[64,1024]{1,0:T(8,128)(2,1)S(1)} collective-permute-done((bf16[64,1024]{1,0:T(8,128)(2,1)S(1)}, bf16[64,1024]{1,0:T(8,128)(2,1)S(1)}, u32[]{:S(2)}, u32[]{:S(2)}) %collective-permute-start.5) | collective-permute-done | bytes 131104 | tf_op jit(solution)/shard_map/ppermute | solution.py:21
  67.4 2.7 %collective-permute-done.6 = bf16[64,1024]{1,0:T(8,128)(2,1)S(1)} collective-permute-done((bf16[64,1024]{1,0:T(8,128)(2,1)S(1)}, bf16[64,1024]{1,0:T(8,128)(2,1)S(1)}, u32[]{:S(2)}, u32[]{:S(2)}) %collective-permute-start.6) | collective-permute-done | bytes 131104 | tf_op jit(solution)/shard_map/ppermute | solution.py:21
  70.0 3.1 %collective-permute-done.7 = bf16[64,1024]{1,0:T(8,128)(2,1)S(1)} collective-permute-done((bf16[64,1024]{1,0:T(8,128)(2,1)S(1)}, bf16[64,1024]{1,0:T(8,128)(2,1)S(1)}, u32[]{:S(2)}, u32[]{:S(2)}) %collective-permute-start.7) | collective-permute-done | bytes 131104 | tf_op jit(solution)/shard_map/ppermute | solution.py:21
  73.1 0.1 add_convert_fusion
  73.2 3.3 %collective-permute-start.12 = (bf16[64,1024]{1,0:T(8,128)(2,1)S(1)}, bf16[64,1024]{1,0:T(8,128)(2,1)S(1)}, u32[]{:S(2)}, u32[]{:S(2)}) collective-permute-start(bf16[64,1024]{1,0:T(8,128)(2,1)S(1)} %add_convert_fusion), channel_id=1, source_target_pairs={{0,16},{8,24},{16,0},{24,8},{1,17},{9,25},{17,1},{25,9},{2,18},{10... | collective-permute-start | bytes 393224 | tf_op jit(solution)/shard_map/ppermute | solution.py:21
  76.4 0.9 collective-permute-start.13
  77.3 3.3 %collective-permute-start.9 = (bf16[64,1024]{1,0:T(8,128)(2,1)S(1)}, bf16[64,1024]{1,0:T(8,128)(2,1)S(1)}, u32[]{:S(2)}, u32[]{:S(2)}) collective-permute-start(bf16[64,1024]{1,0:T(8,128)(2,1)S(1)} %add_convert_fusion), channel_id=1, source_target_pairs={{0,24},{8,0},{16,8},{24,16},{1,25},{9,1},{17,9},{25,17},{2,26},{10... | collective-permute-start | bytes 393224 | tf_op jit(solution)/shard_map/ppermute | solution.py:21
  80.7 4.1 %collective-permute-done.12 = bf16[64,1024]{1,0:T(8,128)(2,1)S(1)} collective-permute-done((bf16[64,1024]{1,0:T(8,128)(2,1)S(1)}, bf16[64,1024]{1,0:T(8,128)(2,1)S(1)}, u32[]{:S(2)}, u32[]{:S(2)}) %collective-permute-start.12) | collective-permute-done | bytes 131104 | tf_op jit(solution)/shard_map/ppermute | solution.py:21
  84.8 1.0 collective-permute-done.13
  85.8 5.6 %collective-permute-start.14 = (bf16[128,1024]{1,0:T(8,128)(2,1)S(1)}, bf16[128,1024]{1,0:T(8,128)(2,1)S(1)}, u32[]{:S(2)}, u32[]{:S(2)}) collective-permute-start(bf16[128,1024]{1,0:T(8,128)(2,1)S(1)} %constant_dynamic-update-slice_fusion.2.b0), channel_id=1, source_target_pairs={{0,6},{2,0},{4,2},{6,4},{1,7},{3,1},{5,3},{7,5},{8,14},{10,8},{12,... | collective-permute-start | bytes 786440 | tf_op jit(solution)/shard_map/ppermute | solution.py:21
  91.4 0.1 collective-permute-start.10
  91.5 0.1 collective-permute-start.17
  91.6 3.3 %collective-permute-start.16 = (bf16[128,1024]{1,0:T(8,128)(2,1)S(1)}, bf16[128,1024]{1,0:T(8,128)(2,1)S(1)}, u32[]{:S(2)}, u32[]{:S(2)}) collective-permute-start(bf16[128,1024]{1,0:T(8,128)(2,1)S(1)} %constant_dynamic-update-slice_fusion.a0), channel_id=1, source_target_pairs={{0,6},{2,0},{4,2},{6,4},{1,7},{3,1},{5,3},{7,5},{8,14},{10,8},{12,... | collective-permute-start | bytes 786440 | tf_op jit(solution)/shard_map/ppermute | solution.py:21
  94.9 3.1 %collective-permute-done.14.b1 = bf16[128,1024]{1,0:T(8,128)(2,1)S(1)} collective-permute-done((bf16[128,1024]{1,0:T(8,128)(2,1)S(1)}, bf16[128,1024]{1,0:T(8,128)(2,1)S(1)}, u32[]{:S(2)}, u32[]{:S(2)}) %collective-permute-start.14) | collective-permute-done | bytes 262176 | tf_op jit(solution)/shard_map/ppermute | solution.py:21
  98.0 3.7 %collective-permute-start.15 = (bf16[128,1024]{1,0:T(8,128)(2,1)S(1)}, bf16[128,1024]{1,0:T(8,128)(2,1)S(1)}, u32[]{:S(2)}, u32[]{:S(2)}) collective-permute-start(bf16[128,1024]{1,0:T(8,128)(2,1)S(1)} %collective-permute-done.14.b1), channel_id=1, source_target_pairs={{0,6},{2,0},{4,2},{6,4},{1,7},{3,1},{5,3},{7,5},{8,14},{10,8},{12,... | collective-permute-start | bytes 786440 | tf_op jit(solution)/shard_map/ppermute | solution.py:21
  101.7 0.2 collective-permute-done.10.a3
  101.9 0.0 copy-start.3
  101.9 1.9 %copy-done.3 = bf16[3,4096,128]{2,1,0:T(8,128)(2,1)S(1)} copy-done((bf16[3,4096,128]{2,1,0:T(8,128)(2,1)S(1)}, bf16[3,4096,128]{2,1,0:T(8,128)(2,1)}, u32[]{:S(2)}) %copy-start.3) | copy-done | bytes 3145752
  103.8 2.7 %time_weights.1.held_ref = bf16[4,6,1024,128]{3,2,1,0:T(8,128)(2,1)S(1)} custom-call(s32[3]{0:T(128)S(1)} %pad_add_fusion.place_ref, bf16[3,4096,128]{2,1,0:T(8,128)(2,1)S(1)} %copy-done.3, bf16[3,4096,128]{2,1,0:T(8,128)(2,1)} %collective-permute-done.4.other_ref), custom_call_target="tpu_custom_call" | custom-call | flops 855638016 | bytes 1024 | tf_op jit(solution)/shard_map/time_weights/pallas_call | solution.py:356
  106.5 0.0 collective-permute-done.17.b3
  106.5 0.0 collective-permute-done.16.a1
  106.6 1.9 %time_projection.1 = (f32[256,768]{1,0:T(8,128)S(1)}, f32[256,128]{1,0:T(8,128)S(1)}) custom-call(s32[3]{0:T(128)S(1)} %pad_add_fusion.place_ref, bf16[128,1024]{1,0:T(8,128)(2,1)S(1)} %constant_dynamic-update-slice_fusion.a0, bf16[128,1024]{1,0:T(8,128)(2,1)S(1)} %constant_dynamic-update-slice_fusion.2.b0, ...), custom_call_target="tpu_custom_call" | custom-call | flops 1207959552 | bytes 8388608 | tf_op jit(solution)/shard_map/time_projection/pallas_call | solution.py:371
  108.5 0.0 collective-permute-done.15.b2
  108.5 1.0 collective-permute-done.11.a2
  109.5 2.7 %time_attention.1 = f32[256,128]{1,0:T(8,128)} custom-call(s32[3]{0:T(128)S(1)} %pad_add_fusion.place_ref, bf16[128,1024]{1,0:T(8,128)(2,1)S(1)} %collective-permute-done.11.a2, bf16[128,1024]{1,0:T(8,128)(2,1)S(1)} %collective-permute-done.15.b2, f32[4,1,1024]{2,1,0:T(1,128)S(1)} %bitcast.46, bf16[4,6,1024,128]{3,2,1,0:T(8,128)(2,1)S(1)} %time_weights.1.held_ref, ...), custom_call_target="tpu_custom_call" | custom-call | tf_op jit(solution)/shard_map/time_attention/pallas_call | solution.py:380
  112.2 10.1 %all-to-all-start.2 = ((f32[128,2,128]{2,1,0:T(2,128)}), f32[128,2,128]{2,1,0:T(2,128)S(1)}, u32[]{:S(2)}, u32[]{:S(2)}) async-start(f32[128,2,128]{2,1,0:T(2,128)} %bitcast.17), calls=%async_computation.2 | async-start | bytes 262144 | tf_op jit(solution)/shard_map/all_to_all | solution.py:389
  122.3 0.6 select_reduce_fusion
  125.7 8.5 %all-to-all-done.2 = f32[128,2,128]{2,1,0:T(2,128)S(1)} async-done(((f32[128,2,128]{2,1,0:T(2,128)}), f32[128,2,128]{2,1,0:T(2,128)S(1)}, u32[]{:S(2)}, u32[]{:S(2)}) %all-to-all-start.2) | async-done | bytes 131104 | tf_op jit(solution)/shard_map/all_to_all | solution.py:389
  134.3 0.4 fusion.4
  134.7 0.6 divide_add_fusion
  (33 shorter events, 0.2 us)
Async XLA Ops:
  0.6 56.3 %copy-start = (bf16[4096,128]{1,0:T(8,128)(2,1)S(1)}, bf16[4096,128]{1,0:T(8,128)(2,1)}, u32[]{:S(2)}) copy-start(bf16[4096,128]{1,0:T(8,128)(2,1)} %param.21) | copy-start | bytes 3145732
  0.6 21.6 %copy-start.10 = (f32[2,4096]{1,0:T(2,128)S(1)}, f32[2,4096]{1,0:T(2,128)}, u32[]{:S(2)}) copy-start(f32[2,4096]{1,0:T(2,128)} %param.14) | copy-start | bytes 98308
  0.7 21.7 %copy-start.1 = (bf16[128,4096]{1,0:T(8,128)(2,1)S(1)}, bf16[128,4096]{1,0:T(8,128)(2,1)}, u32[]{:S(2)}) copy-start(bf16[128,4096]{1,0:T(8,128)(2,1)} %embed_ref.5) | copy-start | bytes 3145732
  0.7 32.0 %collective-permute-start.4 = (bf16[3,4096,128]{2,1,0:T(8,128)(2,1)}, bf16[3,4096,128]{2,1,0:T(8,128)(2,1)}, u32[]{:S(2)}, u32[]{:S(2)}) collective-permute-start(bf16[3,4096,128]{2,1,0:T(8,128)(2,1)} %own_ref.1), channel_id=1, source_target_pairs={{0,1},{1,0},{2,3},{3,2},{4,5},{5,4},{6,7},{7,6},{8,9},{9,8},{10,11... | collective-permute-start | bytes 9437192 | tf_op jit(solution)/shard_map/ppermute | solution.py:21
  2.2 17.3 %collective-permute-start = (bf16[128,1024]{1,0:T(8,128)(2,1)S(1)}, bf16[128,1024]{1,0:T(8,128)(2,1)S(1)}, u32[]{:S(2)}, u32[]{:S(2)}) collective-permute-start(bf16[128,1024]{1,0:T(8,128)(2,1)S(1)} %get-tuple-element.40), channel_id=1, source_target_pairs={{0,6},{2,0},{4,2},{6,4},{1,7},{3,1},{5,3},{7,5},{8,14},{10,8},{12,... | collective-permute-start | bytes 786440 | tf_op jit(solution)/shard_map/ppermute | solution.py:21
  5.0 15.6 %collective-permute-start.2 = (bf16[128,1024]{1,0:T(8,128)(2,1)S(1)}, bf16[128,1024]{1,0:T(8,128)(2,1)}, u32[]{:S(2)}, u32[]{:S(2)}) collective-permute-start(bf16[128,1024]{1,0:T(8,128)(2,1)S(1)} %get-tuple-element.42), channel_id=1, source_target_pairs={{0,2},{2,4},{4,6},{6,0},{1,3},{3,5},{5,7},{7,1},{8,10},{10,12},{12... | collective-permute-start | bytes 786440 | tf_op jit(solution)/shard_map/ppermute | solution.py:21
  5.0 15.6 %collective-permute-start.1 = (bf16[128,1024]{1,0:T(8,128)(2,1)S(1)}, bf16[128,1024]{1,0:T(8,128)(2,1)}, u32[]{:S(2)}, u32[]{:S(2)}) collective-permute-start(bf16[128,1024]{1,0:T(8,128)(2,1)S(1)} %get-tuple-element.41), channel_id=1, source_target_pairs={{0,4},{2,6},{4,0},{6,2},{1,5},{3,7},{5,1},{7,3},{8,12},{10,14},{12... | collective-permute-start | bytes 786440 | tf_op jit(solution)/shard_map/ppermute | solution.py:21
  8.7 21.1 %all-to-all-start = ((bf16[32,16,128]{2,1,0:T(8,128)(2,1)}), bf16[32,16,128]{2,1,0:T(8,128)(2,1)S(1)}, u32[]{:S(2)}, u32[]{:S(2)}) async-start(bf16[32,16,128]{2,1,0:T(8,128)(2,1)} %broadcast_in_dim.16), calls=%async_computation | async-start | bytes 262144 | tf_op jit(solution)/shard_map/all_to_all | solution.py:266
  19.6 1.1 copy-start.7
  20.7 9.1 %copy-start.4 = (f32[4,128]{1,0:T(4,128)S(1)}, f32[4,128]{1,0:T(4,128)}, u32[]{:S(2)}) copy-start(f32[4,128]{1,0:T(4,128)} %head_gain_ref.1) | copy-start | bytes 6148
  21.9 10.8 %collective-permute-start.3 = (bf16[4,128,1024]{2,1,0:T(8,128)(2,1)S(1)}, bf16[4,128,1024]{2,1,0:T(8,128)(2,1)}, u32[]{:S(2)}, u32[]{:S(2)}) collective-permute-start(bf16[4,128,1024]{2,1,0:T(8,128)(2,1)S(1)} %pad_maximum_fusion.own_ref), channel_id=1, source_target_pairs={{0,1},{1,0},{2,3},{3,2},{4,5},{5,4},{6,7},{7,6},{8,9},{9,8},{10,11... | collective-permute-start | bytes 3145736 | tf_op jit(solution)/shard_map/ppermute | solution.py:21
  22.3 1.9 %copy-start.2 = (bf16[3,4096,128]{2,1,0:T(8,128)(2,1)S(1)}, bf16[3,4096,128]{2,1,0:T(8,128)(2,1)}, u32[]{:S(2)}) copy-start(bf16[3,4096,128]{2,1,0:T(8,128)(2,1)} %weight_ref.1) | copy-start | bytes 9437188
  32.7 24.2 %copy-start.5 = (bf16[128,4096]{1,0:T(8,128)(2,1)S(1)}, bf16[128,4096]{1,0:T(8,128)(2,1)}, u32[]{:S(2)}) copy-start(bf16[128,4096]{1,0:T(8,128)(2,1)} %param.18) | copy-start | bytes 3145732
  53.4 11.4 %copy-start.6 = (bf16[128,4096]{1,0:T(8,128)(2,1)S(1)}, bf16[128,4096]{1,0:T(8,128)(2,1)}, u32[]{:S(2)}) copy-start(bf16[128,4096]{1,0:T(8,128)(2,1)} %param.20) | copy-start | bytes 3145732
  57.4 10.0 %collective-permute-start.5 = (bf16[64,1024]{1,0:T(8,128)(2,1)S(1)}, bf16[64,1024]{1,0:T(8,128)(2,1)S(1)}, u32[]{:S(2)}, u32[]{:S(2)}) collective-permute-start(bf16[64,1024]{1,0:T(8,128)(2,1)S(1)} %get-tuple-element.43), channel_id=1, source_target_pairs={{0,8},{8,16},{16,24},{24,0},{1,9},{9,17},{17,25},{25,1},{2,10},{10... | collective-permute-start | bytes 393224 | tf_op jit(solution)/shard_map/ppermute | solution.py:21
  58.3 11.7 %collective-permute-start.6 = (bf16[64,1024]{1,0:T(8,128)(2,1)S(1)}, bf16[64,1024]{1,0:T(8,128)(2,1)S(1)}, u32[]{:S(2)}, u32[]{:S(2)}) collective-permute-start(bf16[64,1024]{1,0:T(8,128)(2,1)S(1)} %get-tuple-element.45), channel_id=1, source_target_pairs={{0,24},{8,0},{16,8},{24,16},{1,25},{9,1},{17,9},{25,17},{2,26},{10... | collective-permute-start | bytes 393224 | tf_op jit(solution)/shard_map/ppermute | solution.py:21
  61.6 11.5 %collective-permute-start.7 = (bf16[64,1024]{1,0:T(8,128)(2,1)S(1)}, bf16[64,1024]{1,0:T(8,128)(2,1)S(1)}, u32[]{:S(2)}, u32[]{:S(2)}) collective-permute-start(bf16[64,1024]{1,0:T(8,128)(2,1)S(1)} %get-tuple-element.44), channel_id=1, source_target_pairs={{0,16},{8,24},{16,0},{24,8},{1,17},{9,25},{17,1},{25,9},{2,18},{10... | collective-permute-start | bytes 393224 | tf_op jit(solution)/shard_map/ppermute | solution.py:21
  65.2 7.9 %collective-permute-start.8 = (bf16[256,128]{1,0:T(8,128)(2,1)S(1)}, bf16[256,128]{1,0:T(8,128)(2,1)S(1)}, u32[]{:S(2)}, u32[]{:S(2)}) collective-permute-start(bf16[256,128]{1,0:T(8,128)(2,1)S(1)} %pad_maximum_fusion.2), channel_id=1, source_target_pairs={{0,1},{1,0},{2,3},{3,2},{4,5},{5,4},{6,7},{7,6},{8,9},{9,8},{10,11... | collective-permute-start | bytes 196616 | tf_op jit(solution)/shard_map/ppermute | solution.py:21
  73.2 11.6 %collective-permute-start.12 = (bf16[64,1024]{1,0:T(8,128)(2,1)S(1)}, bf16[64,1024]{1,0:T(8,128)(2,1)S(1)}, u32[]{:S(2)}, u32[]{:S(2)}) collective-permute-start(bf16[64,1024]{1,0:T(8,128)(2,1)S(1)} %add_convert_fusion), channel_id=1, source_target_pairs={{0,16},{8,24},{16,0},{24,8},{1,17},{9,25},{17,1},{25,9},{2,18},{10... | collective-permute-start | bytes 393224 | tf_op jit(solution)/shard_map/ppermute | solution.py:21
  76.4 9.3 %collective-permute-start.13 = (bf16[64,1024]{1,0:T(8,128)(2,1)S(1)}, bf16[64,1024]{1,0:T(8,128)(2,1)S(1)}, u32[]{:S(2)}, u32[]{:S(2)}) collective-permute-start(bf16[64,1024]{1,0:T(8,128)(2,1)S(1)} %add_convert_fusion), channel_id=1, source_target_pairs={{0,8},{8,16},{16,24},{24,0},{1,9},{9,17},{17,25},{25,1},{2,10},{10... | collective-permute-start | bytes 393224 | tf_op jit(solution)/shard_map/ppermute | solution.py:21
  77.3 14.0 %collective-permute-start.9 = (bf16[64,1024]{1,0:T(8,128)(2,1)S(1)}, bf16[64,1024]{1,0:T(8,128)(2,1)S(1)}, u32[]{:S(2)}, u32[]{:S(2)}) collective-permute-start(bf16[64,1024]{1,0:T(8,128)(2,1)S(1)} %add_convert_fusion), channel_id=1, source_target_pairs={{0,24},{8,0},{16,8},{24,16},{1,25},{9,1},{17,9},{25,17},{2,26},{10... | collective-permute-start | bytes 393224 | tf_op jit(solution)/shard_map/ppermute | solution.py:21
  85.8 12.2 %collective-permute-start.14 = (bf16[128,1024]{1,0:T(8,128)(2,1)S(1)}, bf16[128,1024]{1,0:T(8,128)(2,1)S(1)}, u32[]{:S(2)}, u32[]{:S(2)}) collective-permute-start(bf16[128,1024]{1,0:T(8,128)(2,1)S(1)} %constant_dynamic-update-slice_fusion.2.b0), channel_id=1, source_target_pairs={{0,6},{2,0},{4,2},{6,4},{1,7},{3,1},{5,3},{7,5},{8,14},{10,8},{12,... | collective-permute-start | bytes 786440 | tf_op jit(solution)/shard_map/ppermute | solution.py:21
  91.4 10.5 %collective-permute-start.10 = (bf16[128,1024]{1,0:T(8,128)(2,1)S(1)}, bf16[128,1024]{1,0:T(8,128)(2,1)S(1)}, u32[]{:S(2)}, u32[]{:S(2)}) collective-permute-start(bf16[128,1024]{1,0:T(8,128)(2,1)S(1)} %constant_dynamic-update-slice_fusion.a0), channel_id=1, source_target_pairs={{0,2},{2,4},{4,6},{6,0},{1,3},{3,5},{5,7},{7,1},{8,10},{10,12},{12... | collective-permute-start | bytes 786440 | tf_op jit(solution)/shard_map/ppermute | solution.py:21
  91.5 15.0 %collective-permute-start.17 = (bf16[128,1024]{1,0:T(8,128)(2,1)S(1)}, bf16[128,1024]{1,0:T(8,128)(2,1)S(1)}, u32[]{:S(2)}, u32[]{:S(2)}) collective-permute-start(bf16[128,1024]{1,0:T(8,128)(2,1)S(1)} %constant_dynamic-update-slice_fusion.2.b0), channel_id=1, source_target_pairs={{0,2},{2,4},{4,6},{6,0},{1,3},{3,5},{5,7},{7,1},{8,10},{10,12},{12... | collective-permute-start | bytes 786440 | tf_op jit(solution)/shard_map/ppermute | solution.py:21
  91.6 15.0 %collective-permute-start.16 = (bf16[128,1024]{1,0:T(8,128)(2,1)S(1)}, bf16[128,1024]{1,0:T(8,128)(2,1)S(1)}, u32[]{:S(2)}, u32[]{:S(2)}) collective-permute-start(bf16[128,1024]{1,0:T(8,128)(2,1)S(1)} %constant_dynamic-update-slice_fusion.a0), channel_id=1, source_target_pairs={{0,6},{2,0},{4,2},{6,4},{1,7},{3,1},{5,3},{7,5},{8,14},{10,8},{12,... | collective-permute-start | bytes 786440 | tf_op jit(solution)/shard_map/ppermute | solution.py:21
  98.0 10.5 %collective-permute-start.15 = (bf16[128,1024]{1,0:T(8,128)(2,1)S(1)}, bf16[128,1024]{1,0:T(8,128)(2,1)S(1)}, u32[]{:S(2)}, u32[]{:S(2)}) collective-permute-start(bf16[128,1024]{1,0:T(8,128)(2,1)S(1)} %collective-permute-done.14.b1), channel_id=1, source_target_pairs={{0,6},{2,0},{4,2},{6,4},{1,7},{3,1},{5,3},{7,5},{8,14},{10,8},{12,... | collective-permute-start | bytes 786440 | tf_op jit(solution)/shard_map/ppermute | solution.py:21
  101.9 7.6 %collective-permute-start.11 = (bf16[128,1024]{1,0:T(8,128)(2,1)S(1)}, bf16[128,1024]{1,0:T(8,128)(2,1)S(1)}, u32[]{:S(2)}, u32[]{:S(2)}) collective-permute-start(bf16[128,1024]{1,0:T(8,128)(2,1)S(1)} %collective-permute-done.10.a3), channel_id=1, source_target_pairs={{0,2},{2,4},{4,6},{6,0},{1,3},{3,5},{5,7},{7,1},{8,10},{10,12},{12... | collective-permute-start | bytes 786440 | tf_op jit(solution)/shard_map/ppermute | solution.py:21
  101.9 1.9 %copy-start.3 = (bf16[3,4096,128]{2,1,0:T(8,128)(2,1)S(1)}, bf16[3,4096,128]{2,1,0:T(8,128)(2,1)}, u32[]{:S(2)}) copy-start(bf16[3,4096,128]{2,1,0:T(8,128)(2,1)} %own_ref.1) | copy-start | bytes 9437188
  109.5 12.8 %copy-start.11 = (f32[1000]{0:T(1024)S(1)}, f32[1000]{0:T(1024)}, u32[]{:S(2)}) copy-start(f32[1000]{0:T(1024)} %param.13) | copy-start | bytes 12004
  109.5 16.2 %copy-start.8 = (f32[8,2,128]{2,1,0:T(2,128)S(1)}, f32[8,2,128]{2,1,0:T(2,128)}, u32[]{:S(2)}) copy-start(f32[8,2,128]{2,1,0:T(2,128)} %param.11) | copy-start | bytes 24580
  112.2 22.0 %all-to-all-start.2 = ((f32[128,2,128]{2,1,0:T(2,128)}), f32[128,2,128]{2,1,0:T(2,128)S(1)}, u32[]{:S(2)}, u32[]{:S(2)}) async-start(f32[128,2,128]{2,1,0:T(2,128)} %bitcast.17), calls=%async_computation.2 | async-start | bytes 262144 | tf_op jit(solution)/shard_map/all_to_all | solution.py:389
  134.7 0.6 copy-start.9

commit v7 on v6

--- a/solution.py
+++ b/solution.py
@@ -95,7 +95,6 @@
     total = jnp.zeros((lat.shape[0], 128), F32)
     for start in range(0, width, chunk):
         first = dot(lat, embed_ref[:, start : start + chunk]) + temb_ref[:, start : start + chunk]
-        first = first.astype(BF).astype(F32)
         square = first * first
         for lane in range(0, chunk, 128):
             total = total + square[:, lane : lane + 128]

time: 136 us -> 136 us (level)
  transfers between devices with their start and end apart: 20 -> 20, of which waited for: 10 -> 11; matrix products, arithmetic and copies ran while one was open for 5% -> 5% of each run, Pallas kernels for 7% -> 6%
where the time goes in v7:
time: 136 us; the launch traced here: 135 us
  starting transfers between devices  53.5 us (39%)
  waiting for transfers between devices  29.9 us (22%)
  blocking collectives  20.7 us (15%)
  Pallas kernels  15 us (11%)
  local copies, waits for them, and re-layouts  7.01 us (5%)
  between operations  4.5 us (3%)
  other arithmetic  3.46 us (3%)
    ppermute x18, starting transfers between devices, shift(): lax.ppermute(value, axis, [(i, (i + step) % size) for i in range(size)])  33.3 us
    all_to_all x1, blocking collectives, body(): lax.all_to_all(attended, ('y', 'zl', 'x', 'c'), split_axis=0, concat_axis...  20.7 us
    ppermute x18, waiting for transfers between devices, shift(): lax.ppermute(value, axis, [(i, (i + step) % size) for i in range(size)])  17.2 us
    all_to_all x1, starting transfers between devices, body(): lax.all_to_all(lat_rows, ('zh', 'x', 'c'), split_axis=0, concat_axis=0, t...  10.1 us
    all_to_all x1, starting transfers between devices, body(): lax.all_to_all(noise, ('y', 'zl', 'zh', 'x'), split_axis=0, concat_axis=0...  10.1 us
    all_to_all x1, waiting for transfers between devices, body(): lax.all_to_all(noise, ('y', 'zl', 'zh', 'x'), split_axis=0, concat_axis=0...  8.51 us
    all_to_all x1, waiting for transfers between devices, body(): lax.all_to_all(lat_rows, ('zh', 'x', 'c'), split_axis=0, concat_axis=0, t...  4.12 us
    unnamed x26, local copies, waits for them, and re-layouts  3.84 us
  transfers between devices with their start and end apart: 20, of which 11 were waited for; matrix products, arithmetic and copies ran while one was open for 5% of the time, Pallas kernels for 6%

profile of v7, /device:TPU:8, one launch (start us, length us, event | category | flops | bytes accessed | tf_op | source)
XLA Modules:
  0.0 135.2 jit_solution(6345310147010340293)
XLA Ops:
  0.6 0.0 copy-start
  0.7 0.1 collective-permute-start.4
  0.8 1.4 %constant_dynamic-slice_fusion.2 = (bf16[128,1024]{1,0:T(8,128)(2,1)S(1)}, bf16[128,1024]{1,0:T(8,128)(2,1)S(1)}, bf16[128,1024]{1,0:T(8,128)(2,1)S(1)}) fusion(bf16[128,4096]{1,0:T(8,128)(2,1)} %param.18, s32[]{:T(128)S(6)} %select_n.51, s32[]{:T(128)S(6)} %select_n.55, s32[]{:T(128)S(6)} %select_n.57), kind=kLoop, calls=%fused_computation.33 | loop fusion | bytes 1572876 | tf_op jit(solution)/shard_map/dynamic_slice | solution.py:284
  2.2 2.8 %collective-permute-start = (bf16[128,1024]{1,0:T(8,128)(2,1)S(1)}, bf16[128,1024]{1,0:T(8,128)(2,1)S(1)}, u32[]{:S(2)}, u32[]{:S(2)}) collective-permute-start(bf16[128,1024]{1,0:T(8,128)(2,1)S(1)} %get-tuple-element.40), channel_id=1, source_target_pairs={{0,6},{2,0},{4,2},{6,4},{1,7},{3,1},{5,3},{7,5},{8,14},{10,8},{12,... | collective-permute-start | bytes 786440 | tf_op jit(solution)/shard_map/ppermute | solution.py:21
  5.0 0.0 collective-permute-start.2
  5.0 2.3 %collective-permute-start.1 = (bf16[128,1024]{1,0:T(8,128)(2,1)S(1)}, bf16[128,1024]{1,0:T(8,128)(2,1)}, u32[]{:S(2)}, u32[]{:S(2)}) collective-permute-start(bf16[128,1024]{1,0:T(8,128)(2,1)S(1)} %get-tuple-element.41), channel_id=1, source_target_pairs={{0,4},{2,6},{4,0},{6,2},{1,5},{3,7},{5,1},{7,3},{8,12},{10,14},{12... | collective-permute-start | bytes 786440 | tf_op jit(solution)/shard_map/ppermute | solution.py:21
  7.3 0.7 convert_element_type.36
  8.0 0.7 broadcast_in_dim.16
  8.7 10.1 %all-to-all-start = ((bf16[32,16,128]{2,1,0:T(8,128)(2,1)}), bf16[32,16,128]{2,1,0:T(8,128)(2,1)S(1)}, u32[]{:S(2)}, u32[]{:S(2)}) async-start(bf16[32,16,128]{2,1,0:T(8,128)(2,1)} %broadcast_in_dim.16), calls=%async_computation | async-start | bytes 262144 | tf_op jit(solution)/shard_map/all_to_all | solution.py:265
  19.5 0.1 fusion.6
  19.5 0.0 collective-permute-done
  19.6 1.1 dynamic-slice_bitcast_fusion
  20.6 0.0 collective-permute-done.2
  20.6 0.0 collective-permute-done.1
  20.7 0.0 copy-start.4
  20.7 1.2 pad_maximum_fusion.own_ref
  21.9 0.4 collective-permute-start.3
  22.3 0.0 copy-start.2
  22.4 1.9 %copy-done.2 = bf16[3,4096,128]{2,1,0:T(8,128)(2,1)S(1)} copy-done((bf16[3,4096,128]{2,1,0:T(8,128)(2,1)S(1)}, bf16[3,4096,128]{2,1,0:T(8,128)(2,1)}, u32[]{:S(2)}) %copy-start.2) | copy-done | bytes 3145752
  24.2 1.3 fold_projection.1
  25.6 0.1 pad_add_fusion.place_ref
  25.6 4.1 %all-to-all-done = bf16[32,16,128]{2,1,0:T(8,128)(2,1)S(1)} async-done(((bf16[32,16,128]{2,1,0:T(8,128)(2,1)}), bf16[32,16,128]{2,1,0:T(8,128)(2,1)S(1)}, u32[]{:S(2)}, u32[]{:S(2)}) %all-to-all-start) | async-done | bytes 131104 | tf_op jit(solution)/shard_map/all_to_all | solution.py:265
  29.8 2.9 %space_attention.1 = bf16[64,48,128]{2,1,0:T(8,128)(2,1)S(1)} custom-call(s32[3]{0:T(128)S(1)} %pad_add_fusion.place_ref, bf16[512,128]{1,0:T(8,128)(2,1)S(1)} %bitcast.41, bf16[128,4096]{1,0:T(8,128)(2,1)S(1)} %copy-done.1, f32[1,4096]{1,0:T(1,128)S(1)} %bitcast.43, bf16[256,384]{1,0:T(8,128)(2,1)S(1)} %get-tuple-element.20.fold_ref, ...), custom_call_target="tpu_custom_call" | custom-call | tf_op jit(solution)/shard_map/space_attention/pallas_call | solution.py:292
  32.6 0.0 copy-start.5
  32.6 0.0 collective-permute-done.3.other_ref
  32.6 20.7 %all_to_all.22.att_ref = bf16[64,48,128]{2,1,0:T(8,128)(2,1)S(1)} all-to-all(bf16[64,48,128]{2,1,0:T(8,128)(2,1)S(1)} %space_attention.1), channel_id=1, replica_groups=mesh['y'=4,'zl'=2,'zh'=4,'x'=4,'c'=2] {'y','zl','x','c'}, dimensions={0} | all-to-all | bytes 1572864 | tf_op jit(solution)/shard_map/all_to_all | solution.py:306
  53.4 3.4 %space_output.1 = (bf16[192,1024]{1,0:T(8,128)(2,1)S(1)}, f32[64,1024]{1,0:T(8,128)S(1)}, bf16[256,256]{1,0:T(8,128)(2,1)S(1)}) custom-call(s32[3]{0:T(128)S(1)} %pad_add_fusion.place_ref, bf16[64,48,128]{2,1,0:T(8,128)(2,1)S(1)} %all_to_all.22.att_ref, bf16[128,4096]{1,0:T(8,128)(2,1)S(1)} %copy-done.1, f32[1,4096]{1,0:T(1,128)S(1)} %bitcast.44, ...), custom_call_target="tpu_custom_call" | custom-call | tf_op jit(solution)/shard_map/space_output/pallas_call | solution.py:309
  56.8 0.4 fusion.2
  57.3 0.9 collective-permute-start.5
  58.2 3.3 %collective-permute-start.6 = (bf16[64,1024]{1,0:T(8,128)(2,1)S(1)}, bf16[64,1024]{1,0:T(8,128)(2,1)S(1)}, u32[]{:S(2)}, u32[]{:S(2)}) collective-permute-start(bf16[64,1024]{1,0:T(8,128)(2,1)S(1)} %get-tuple-element.45), channel_id=1, source_target_pairs={{0,24},{8,0},{16,8},{24,16},{1,25},{9,1},{17,9},{25,17},{2,26},{10... | collective-permute-start | bytes 393224 | tf_op jit(solution)/shard_map/ppermute | solution.py:21
  61.5 3.2 %collective-permute-start.7 = (bf16[64,1024]{1,0:T(8,128)(2,1)S(1)}, bf16[64,1024]{1,0:T(8,128)(2,1)S(1)}, u32[]{:S(2)}, u32[]{:S(2)}) collective-permute-start(bf16[64,1024]{1,0:T(8,128)(2,1)S(1)} %get-tuple-element.44), channel_id=1, source_target_pairs={{0,16},{8,24},{16,0},{24,8},{1,17},{9,25},{17,1},{25,9},{2,18},{10... | collective-permute-start | bytes 393224 | tf_op jit(solution)/shard_map/ppermute | solution.py:21
  64.8 0.4 fusion.3
  65.2 0.1 collective-permute-start.8
  65.3 2.0 %collective-permute-done.5 = bf16[64,1024]{1,0:T(8,128)(2,1)S(1)} collective-permute-done((bf16[64,1024]{1,0:T(8,128)(2,1)S(1)}, bf16[64,1024]{1,0:T(8,128)(2,1)S(1)}, u32[]{:S(2)}, u32[]{:S(2)}) %collective-permute-start.5) | collective-permute-done | bytes 131104 | tf_op jit(solution)/shard_map/ppermute | solution.py:21
  67.3 2.7 %collective-permute-done.6 = bf16[64,1024]{1,0:T(8,128)(2,1)S(1)} collective-permute-done((bf16[64,1024]{1,0:T(8,128)(2,1)S(1)}, bf16[64,1024]{1,0:T(8,128)(2,1)S(1)}, u32[]{:S(2)}, u32[]{:S(2)}) %collective-permute-start.6) | collective-permute-done | bytes 131104 | tf_op jit(solution)/shard_map/ppermute | solution.py:21
  70.0 3.1 %collective-permute-done.7 = bf16[64,1024]{1,0:T(8,128)(2,1)S(1)} collective-permute-done((bf16[64,1024]{1,0:T(8,128)(2,1)S(1)}, bf16[64,1024]{1,0:T(8,128)(2,1)S(1)}, u32[]{:S(2)}, u32[]{:S(2)}) %collective-permute-start.7) | collective-permute-done | bytes 131104 | tf_op jit(solution)/shard_map/ppermute | solution.py:21
  73.0 0.1 add_convert_fusion
  73.1 3.3 %collective-permute-start.12 = (bf16[64,1024]{1,0:T(8,128)(2,1)S(1)}, bf16[64,1024]{1,0:T(8,128)(2,1)S(1)}, u32[]{:S(2)}, u32[]{:S(2)}) collective-permute-start(bf16[64,1024]{1,0:T(8,128)(2,1)S(1)} %add_convert_fusion), channel_id=1, source_target_pairs={{0,16},{8,24},{16,0},{24,8},{1,17},{9,25},{17,1},{25,9},{2,18},{10... | collective-permute-start | bytes 393224 | tf_op jit(solution)/shard_map/ppermute | solution.py:21
  76.4 0.9 collective-permute-start.13
  77.3 3.3 %collective-permute-start.9 = (bf16[64,1024]{1,0:T(8,128)(2,1)S(1)}, bf16[64,1024]{1,0:T(8,128)(2,1)S(1)}, u32[]{:S(2)}, u32[]{:S(2)}) collective-permute-start(bf16[64,1024]{1,0:T(8,128)(2,1)S(1)} %add_convert_fusion), channel_id=1, source_target_pairs={{0,24},{8,0},{16,8},{24,16},{1,25},{9,1},{17,9},{25,17},{2,26},{10... | collective-permute-start | bytes 393224 | tf_op jit(solution)/shard_map/ppermute | solution.py:21
  80.6 4.1 %collective-permute-done.12 = bf16[64,1024]{1,0:T(8,128)(2,1)S(1)} collective-permute-done((bf16[64,1024]{1,0:T(8,128)(2,1)S(1)}, bf16[64,1024]{1,0:T(8,128)(2,1)S(1)}, u32[]{:S(2)}, u32[]{:S(2)}) %collective-permute-start.12) | collective-permute-done | bytes 131104 | tf_op jit(solution)/shard_map/ppermute | solution.py:21
  84.7 1.0 collective-permute-done.13
  85.7 5.6 %collective-permute-start.14 = (bf16[128,1024]{1,0:T(8,128)(2,1)S(1)}, bf16[128,1024]{1,0:T(8,128)(2,1)S(1)}, u32[]{:S(2)}, u32[]{:S(2)}) collective-permute-start(bf16[128,1024]{1,0:T(8,128)(2,1)S(1)} %constant_dynamic-update-slice_fusion.2.b0), channel_id=1, source_target_pairs={{0,6},{2,0},{4,2},{6,4},{1,7},{3,1},{5,3},{7,5},{8,14},{10,8},{12,... | collective-permute-start | bytes 786440 | tf_op jit(solution)/shard_map/ppermute | solution.py:21
  91.3 0.0 collective-permute-done.9
  91.3 0.1 collective-permute-start.10
  91.4 0.1 collective-permute-start.17
  91.5 3.3 %collective-permute-start.16 = (bf16[128,1024]{1,0:T(8,128)(2,1)S(1)}, bf16[128,1024]{1,0:T(8,128)(2,1)S(1)}, u32[]{:S(2)}, u32[]{:S(2)}) collective-permute-start(bf16[128,1024]{1,0:T(8,128)(2,1)S(1)} %constant_dynamic-update-slice_fusion.a0), channel_id=1, source_target_pairs={{0,6},{2,0},{4,2},{6,4},{1,7},{3,1},{5,3},{7,5},{8,14},{10,8},{12,... | collective-permute-start | bytes 786440 | tf_op jit(solution)/shard_map/ppermute | solution.py:21
  94.8 3.1 %collective-permute-done.14.b1 = bf16[128,1024]{1,0:T(8,128)(2,1)S(1)} collective-permute-done((bf16[128,1024]{1,0:T(8,128)(2,1)S(1)}, bf16[128,1024]{1,0:T(8,128)(2,1)S(1)}, u32[]{:S(2)}, u32[]{:S(2)}) %collective-permute-start.14) | collective-permute-done | bytes 262176 | tf_op jit(solution)/shard_map/ppermute | solution.py:21
  97.9 3.7 %collective-permute-start.15 = (bf16[128,1024]{1,0:T(8,128)(2,1)S(1)}, bf16[128,1024]{1,0:T(8,128)(2,1)S(1)}, u32[]{:S(2)}, u32[]{:S(2)}) collective-permute-start(bf16[128,1024]{1,0:T(8,128)(2,1)S(1)} %collective-permute-done.14.b1), channel_id=1, source_target_pairs={{0,6},{2,0},{4,2},{6,4},{1,7},{3,1},{5,3},{7,5},{8,14},{10,8},{12,... | collective-permute-start | bytes 786440 | tf_op jit(solution)/shard_map/ppermute | solution.py:21
  101.6 0.2 collective-permute-done.10.a3
  101.9 0.0 collective-permute-start.11
  101.9 0.0 copy-start.3
  101.9 1.9 %copy-done.3 = bf16[3,4096,128]{2,1,0:T(8,128)(2,1)S(1)} copy-done((bf16[3,4096,128]{2,1,0:T(8,128)(2,1)S(1)}, bf16[3,4096,128]{2,1,0:T(8,128)(2,1)}, u32[]{:S(2)}) %copy-start.3) | copy-done | bytes 3145752
  103.8 2.7 %time_weights.1.held_ref = bf16[4,6,1024,128]{3,2,1,0:T(8,128)(2,1)S(1)} custom-call(s32[3]{0:T(128)S(1)} %pad_add_fusion.place_ref, bf16[3,4096,128]{2,1,0:T(8,128)(2,1)S(1)} %copy-done.3, bf16[3,4096,128]{2,1,0:T(8,128)(2,1)} %collective-permute-done.4.other_ref), custom_call_target="tpu_custom_call" | custom-call | flops 855638016 | bytes 1024 | tf_op jit(solution)/shard_map/time_weights/pallas_call | solution.py:355
  106.5 0.1 collective-permute-done.17.b3
  106.5 0.0 collective-permute-done.16.a1
  106.5 1.9 %time_projection.1 = (f32[256,768]{1,0:T(8,128)S(1)}, f32[256,128]{1,0:T(8,128)S(1)}) custom-call(s32[3]{0:T(128)S(1)} %pad_add_fusion.place_ref, bf16[128,1024]{1,0:T(8,128)(2,1)S(1)} %constant_dynamic-update-slice_fusion.a0, bf16[128,1024]{1,0:T(8,128)(2,1)S(1)} %constant_dynamic-update-slice_fusion.2.b0, ...), custom_call_target="tpu_custom_call" | custom-call | flops 1207959552 | bytes 8388608 | tf_op jit(solution)/shard_map/time_projection/pallas_call | solution.py:370
  108.5 1.0 collective-permute-done.11.a2
  109.5 2.7 %time_attention.1 = f32[256,128]{1,0:T(8,128)} custom-call(s32[3]{0:T(128)S(1)} %pad_add_fusion.place_ref, bf16[128,1024]{1,0:T(8,128)(2,1)S(1)} %collective-permute-done.11.a2, bf16[128,1024]{1,0:T(8,128)(2,1)S(1)} %collective-permute-done.15.b2, f32[4,1,1024]{2,1,0:T(1,128)S(1)} %bitcast.46, bf16[4,6,1024,128]{3,2,1,0:T(8,128)(2,1)S(1)} %time_weights.1.held_ref, ...), custom_call_target="tpu_custom_call" | custom-call | tf_op jit(solution)/shard_map/time_attention/pallas_call | solution.py:379
  112.2 10.1 %all-to-all-start.2 = ((f32[128,2,128]{2,1,0:T(2,128)}), f32[128,2,128]{2,1,0:T(2,128)S(1)}, u32[]{:S(2)}, u32[]{:S(2)}) async-start(f32[128,2,128]{2,1,0:T(2,128)} %bitcast.17), calls=%async_computation.2 | async-start | bytes 262144 | tf_op jit(solution)/shard_map/all_to_all | solution.py:388
  122.3 0.6 select_reduce_fusion
  125.7 8.5 %all-to-all-done.2 = f32[128,2,128]{2,1,0:T(2,128)S(1)} async-done(((f32[128,2,128]{2,1,0:T(2,128)}), f32[128,2,128]{2,1,0:T(2,128)S(1)}, u32[]{:S(2)}, u32[]{:S(2)}) %all-to-all-start.2) | async-done | bytes 131104 | tf_op jit(solution)/shard_map/all_to_all | solution.py:388
  134.2 0.4 fusion.4
  134.6 0.6 divide_add_fusion
  (33 shorter events, 0.2 us)
Async XLA Ops:
  0.6 56.2 %copy-start = (bf16[4096,128]{1,0:T(8,128)(2,1)S(1)}, bf16[4096,128]{1,0:T(8,128)(2,1)}, u32[]{:S(2)}) copy-start(bf16[4096,128]{1,0:T(8,128)(2,1)} %param.21) | copy-start | bytes 3145732
  0.6 21.6 %copy-start.10 = (f32[2,4096]{1,0:T(2,128)S(1)}, f32[2,4096]{1,0:T(2,128)}, u32[]{:S(2)}) copy-start(f32[2,4096]{1,0:T(2,128)} %param.14) | copy-start | bytes 98308
  0.7 21.7 %copy-start.1 = (bf16[128,4096]{1,0:T(8,128)(2,1)S(1)}, bf16[128,4096]{1,0:T(8,128)(2,1)}, u32[]{:S(2)}) copy-start(bf16[128,4096]{1,0:T(8,128)(2,1)} %embed_ref.5) | copy-start | bytes 3145732
  0.7 32.0 %collective-permute-start.4 = (bf16[3,4096,128]{2,1,0:T(8,128)(2,1)}, bf16[3,4096,128]{2,1,0:T(8,128)(2,1)}, u32[]{:S(2)}, u32[]{:S(2)}) collective-permute-start(bf16[3,4096,128]{2,1,0:T(8,128)(2,1)} %own_ref.1), channel_id=1, source_target_pairs={{0,1},{1,0},{2,3},{3,2},{4,5},{5,4},{6,7},{7,6},{8,9},{9,8},{10,11... | collective-permute-start | bytes 9437192 | tf_op jit(solution)/shard_map/ppermute | solution.py:21
  2.2 17.3 %collective-permute-start = (bf16[128,1024]{1,0:T(8,128)(2,1)S(1)}, bf16[128,1024]{1,0:T(8,128)(2,1)S(1)}, u32[]{:S(2)}, u32[]{:S(2)}) collective-permute-start(bf16[128,1024]{1,0:T(8,128)(2,1)S(1)} %get-tuple-element.40), channel_id=1, source_target_pairs={{0,6},{2,0},{4,2},{6,4},{1,7},{3,1},{5,3},{7,5},{8,14},{10,8},{12,... | collective-permute-start | bytes 786440 | tf_op jit(solution)/shard_map/ppermute | solution.py:21
  5.0 15.6 %collective-permute-start.2 = (bf16[128,1024]{1,0:T(8,128)(2,1)S(1)}, bf16[128,1024]{1,0:T(8,128)(2,1)}, u32[]{:S(2)}, u32[]{:S(2)}) collective-permute-start(bf16[128,1024]{1,0:T(8,128)(2,1)S(1)} %get-tuple-element.42), channel_id=1, source_target_pairs={{0,2},{2,4},{4,6},{6,0},{1,3},{3,5},{5,7},{7,1},{8,10},{10,12},{12... | collective-permute-start | bytes 786440 | tf_op jit(solution)/shard_map/ppermute | solution.py:21
  5.0 15.6 %collective-permute-start.1 = (bf16[128,1024]{1,0:T(8,128)(2,1)S(1)}, bf16[128,1024]{1,0:T(8,128)(2,1)}, u32[]{:S(2)}, u32[]{:S(2)}) collective-permute-start(bf16[128,1024]{1,0:T(8,128)(2,1)S(1)} %get-tuple-element.41), channel_id=1, source_target_pairs={{0,4},{2,6},{4,0},{6,2},{1,5},{3,7},{5,1},{7,3},{8,12},{10,14},{12... | collective-permute-start | bytes 786440 | tf_op jit(solution)/shard_map/ppermute | solution.py:21
  8.7 21.1 %all-to-all-start = ((bf16[32,16,128]{2,1,0:T(8,128)(2,1)}), bf16[32,16,128]{2,1,0:T(8,128)(2,1)S(1)}, u32[]{:S(2)}, u32[]{:S(2)}) async-start(bf16[32,16,128]{2,1,0:T(8,128)(2,1)} %broadcast_in_dim.16), calls=%async_computation | async-start | bytes 262144 | tf_op jit(solution)/shard_map/all_to_all | solution.py:265
  19.6 1.1 copy-start.7
  20.7 9.1 %copy-start.4 = (f32[4,128]{1,0:T(4,128)S(1)}, f32[4,128]{1,0:T(4,128)}, u32[]{:S(2)}) copy-start(f32[4,128]{1,0:T(4,128)} %head_gain_ref.1) | copy-start | bytes 6148
  21.9 10.7 %collective-permute-start.3 = (bf16[4,128,1024]{2,1,0:T(8,128)(2,1)S(1)}, bf16[4,128,1024]{2,1,0:T(8,128)(2,1)}, u32[]{:S(2)}, u32[]{:S(2)}) collective-permute-start(bf16[4,128,1024]{2,1,0:T(8,128)(2,1)S(1)} %pad_maximum_fusion.own_ref), channel_id=1, source_target_pairs={{0,1},{1,0},{2,3},{3,2},{4,5},{5,4},{6,7},{7,6},{8,9},{9,8},{10,11... | collective-permute-start | bytes 3145736 | tf_op jit(solution)/shard_map/ppermute | solution.py:21
  22.3 1.9 %copy-start.2 = (bf16[3,4096,128]{2,1,0:T(8,128)(2,1)S(1)}, bf16[3,4096,128]{2,1,0:T(8,128)(2,1)}, u32[]{:S(2)}) copy-start(bf16[3,4096,128]{2,1,0:T(8,128)(2,1)} %weight_ref.1) | copy-start | bytes 9437188
  32.6 24.2 %copy-start.5 = (bf16[128,4096]{1,0:T(8,128)(2,1)S(1)}, bf16[128,4096]{1,0:T(8,128)(2,1)}, u32[]{:S(2)}) copy-start(bf16[128,4096]{1,0:T(8,128)(2,1)} %param.18) | copy-start | bytes 3145732
  53.4 11.4 %copy-start.6 = (bf16[128,4096]{1,0:T(8,128)(2,1)S(1)}, bf16[128,4096]{1,0:T(8,128)(2,1)}, u32[]{:S(2)}) copy-start(bf16[128,4096]{1,0:T(8,128)(2,1)} %param.20) | copy-start | bytes 3145732
  57.3 10.0 %collective-permute-start.5 = (bf16[64,1024]{1,0:T(8,128)(2,1)S(1)}, bf16[64,1024]{1,0:T(8,128)(2,1)S(1)}, u32[]{:S(2)}, u32[]{:S(2)}) collective-permute-start(bf16[64,1024]{1,0:T(8,128)(2,1)S(1)} %get-tuple-element.43), channel_id=1, source_target_pairs={{0,8},{8,16},{16,24},{24,0},{1,9},{9,17},{17,25},{25,1},{2,10},{10... | collective-permute-start | bytes 393224 | tf_op jit(solution)/shard_map/ppermute | solution.py:21
  58.2 11.7 %collective-permute-start.6 = (bf16[64,1024]{1,0:T(8,128)(2,1)S(1)}, bf16[64,1024]{1,0:T(8,128)(2,1)S(1)}, u32[]{:S(2)}, u32[]{:S(2)}) collective-permute-start(bf16[64,1024]{1,0:T(8,128)(2,1)S(1)} %get-tuple-element.45), channel_id=1, source_target_pairs={{0,24},{8,0},{16,8},{24,16},{1,25},{9,1},{17,9},{25,17},{2,26},{10... | collective-permute-start | bytes 393224 | tf_op jit(solution)/shard_map/ppermute | solution.py:21
  61.5 11.5 %collective-permute-start.7 = (bf16[64,1024]{1,0:T(8,128)(2,1)S(1)}, bf16[64,1024]{1,0:T(8,128)(2,1)S(1)}, u32[]{:S(2)}, u32[]{:S(2)}) collective-permute-start(bf16[64,1024]{1,0:T(8,128)(2,1)S(1)} %get-tuple-element.44), channel_id=1, source_target_pairs={{0,16},{8,24},{16,0},{24,8},{1,17},{9,25},{17,1},{25,9},{2,18},{10... | collective-permute-start | bytes 393224 | tf_op jit(solution)/shard_map/ppermute | solution.py:21
  65.2 7.9 %collective-permute-start.8 = (bf16[256,128]{1,0:T(8,128)(2,1)S(1)}, bf16[256,128]{1,0:T(8,128)(2,1)S(1)}, u32[]{:S(2)}, u32[]{:S(2)}) collective-permute-start(bf16[256,128]{1,0:T(8,128)(2,1)S(1)} %pad_maximum_fusion.2), channel_id=1, source_target_pairs={{0,1},{1,0},{2,3},{3,2},{4,5},{5,4},{6,7},{7,6},{8,9},{9,8},{10,11... | collective-permute-start | bytes 196616 | tf_op jit(solution)/shard_map/ppermute | solution.py:21
  73.1 11.6 %collective-permute-start.12 = (bf16[64,1024]{1,0:T(8,128)(2,1)S(1)}, bf16[64,1024]{1,0:T(8,128)(2,1)S(1)}, u32[]{:S(2)}, u32[]{:S(2)}) collective-permute-start(bf16[64,1024]{1,0:T(8,128)(2,1)S(1)} %add_convert_fusion), channel_id=1, source_target_pairs={{0,16},{8,24},{16,0},{24,8},{1,17},{9,25},{17,1},{25,9},{2,18},{10... | collective-permute-start | bytes 393224 | tf_op jit(solution)/shard_map/ppermute | solution.py:21
  76.4 9.3 %collective-permute-start.13 = (bf16[64,1024]{1,0:T(8,128)(2,1)S(1)}, bf16[64,1024]{1,0:T(8,128)(2,1)S(1)}, u32[]{:S(2)}, u32[]{:S(2)}) collective-permute-start(bf16[64,1024]{1,0:T(8,128)(2,1)S(1)} %add_convert_fusion), channel_id=1, source_target_pairs={{0,8},{8,16},{16,24},{24,0},{1,9},{9,17},{17,25},{25,1},{2,10},{10... | collective-permute-start | bytes 393224 | tf_op jit(solution)/shard_map/ppermute | solution.py:21
  77.3 14.0 %collective-permute-start.9 = (bf16[64,1024]{1,0:T(8,128)(2,1)S(1)}, bf16[64,1024]{1,0:T(8,128)(2,1)S(1)}, u32[]{:S(2)}, u32[]{:S(2)}) collective-permute-start(bf16[64,1024]{1,0:T(8,128)(2,1)S(1)} %add_convert_fusion), channel_id=1, source_target_pairs={{0,24},{8,0},{16,8},{24,16},{1,25},{9,1},{17,9},{25,17},{2,26},{10... | collective-permute-start | bytes 393224 | tf_op jit(solution)/shard_map/ppermute | solution.py:21
  85.7 12.2 %collective-permute-start.14 = (bf16[128,1024]{1,0:T(8,128)(2,1)S(1)}, bf16[128,1024]{1,0:T(8,128)(2,1)S(1)}, u32[]{:S(2)}, u32[]{:S(2)}) collective-permute-start(bf16[128,1024]{1,0:T(8,128)(2,1)S(1)} %constant_dynamic-update-slice_fusion.2.b0), channel_id=1, source_target_pairs={{0,6},{2,0},{4,2},{6,4},{1,7},{3,1},{5,3},{7,5},{8,14},{10,8},{12,... | collective-permute-start | bytes 786440 | tf_op jit(solution)/shard_map/ppermute | solution.py:21
  91.3 10.5 %collective-permute-start.10 = (bf16[128,1024]{1,0:T(8,128)(2,1)S(1)}, bf16[128,1024]{1,0:T(8,128)(2,1)S(1)}, u32[]{:S(2)}, u32[]{:S(2)}) collective-permute-start(bf16[128,1024]{1,0:T(8,128)(2,1)S(1)} %constant_dynamic-update-slice_fusion.a0), channel_id=1, source_target_pairs={{0,2},{2,4},{4,6},{6,0},{1,3},{3,5},{5,7},{7,1},{8,10},{10,12},{12... | collective-permute-start | bytes 786440 | tf_op jit(solution)/shard_map/ppermute | solution.py:21
  91.4 15.1 %collective-permute-start.17 = (bf16[128,1024]{1,0:T(8,128)(2,1)S(1)}, bf16[128,1024]{1,0:T(8,128)(2,1)S(1)}, u32[]{:S(2)}, u32[]{:S(2)}) collective-permute-start(bf16[128,1024]{1,0:T(8,128)(2,1)S(1)} %constant_dynamic-update-slice_fusion.2.b0), channel_id=1, source_target_pairs={{0,2},{2,4},{4,6},{6,0},{1,3},{3,5},{5,7},{7,1},{8,10},{10,12},{12... | collective-permute-start | bytes 786440 | tf_op jit(solution)/shard_map/ppermute | solution.py:21
  91.5 15.0 %collective-permute-start.16 = (bf16[128,1024]{1,0:T(8,128)(2,1)S(1)}, bf16[128,1024]{1,0:T(8,128)(2,1)S(1)}, u32[]{:S(2)}, u32[]{:S(2)}) collective-permute-start(bf16[128,1024]{1,0:T(8,128)(2,1)S(1)} %constant_dynamic-update-slice_fusion.a0), channel_id=1, source_target_pairs={{0,6},{2,0},{4,2},{6,4},{1,7},{3,1},{5,3},{7,5},{8,14},{10,8},{12,... | collective-permute-start | bytes 786440 | tf_op jit(solution)/shard_map/ppermute | solution.py:21
  97.9 10.5 %collective-permute-start.15 = (bf16[128,1024]{1,0:T(8,128)(2,1)S(1)}, bf16[128,1024]{1,0:T(8,128)(2,1)S(1)}, u32[]{:S(2)}, u32[]{:S(2)}) collective-permute-start(bf16[128,1024]{1,0:T(8,128)(2,1)S(1)} %collective-permute-done.14.b1), channel_id=1, source_target_pairs={{0,6},{2,0},{4,2},{6,4},{1,7},{3,1},{5,3},{7,5},{8,14},{10,8},{12,... | collective-permute-start | bytes 786440 | tf_op jit(solution)/shard_map/ppermute | solution.py:21
  101.9 7.6 %collective-permute-start.11 = (bf16[128,1024]{1,0:T(8,128)(2,1)S(1)}, bf16[128,1024]{1,0:T(8,128)(2,1)S(1)}, u32[]{:S(2)}, u32[]{:S(2)}) collective-permute-start(bf16[128,1024]{1,0:T(8,128)(2,1)S(1)} %collective-permute-done.10.a3), channel_id=1, source_target_pairs={{0,2},{2,4},{4,6},{6,0},{1,3},{3,5},{5,7},{7,1},{8,10},{10,12},{12... | collective-permute-start | bytes 786440 | tf_op jit(solution)/shard_map/ppermute | solution.py:21
  101.9 1.9 %copy-start.3 = (bf16[3,4096,128]{2,1,0:T(8,128)(2,1)S(1)}, bf16[3,4096,128]{2,1,0:T(8,128)(2,1)}, u32[]{:S(2)}) copy-start(bf16[3,4096,128]{2,1,0:T(8,128)(2,1)} %own_ref.1) | copy-start | bytes 9437188
  109.4 12.8 %copy-start.11 = (f32[1000]{0:T(1024)S(1)}, f32[1000]{0:T(1024)}, u32[]{:S(2)}) copy-start(f32[1000]{0:T(1024)} %param.13) | copy-start | bytes 12004
  109.4 16.2 %copy-start.8 = (f32[8,2,128]{2,1,0:T(2,128)S(1)}, f32[8,2,128]{2,1,0:T(2,128)}, u32[]{:S(2)}) copy-start(f32[8,2,128]{2,1,0:T(2,128)} %param.11) | copy-start | bytes 24580
  112.2 22.0 %all-to-all-start.2 = ((f32[128,2,128]{2,1,0:T(2,128)}), f32[128,2,128]{2,1,0:T(2,128)S(1)}, u32[]{:S(2)}, u32[]{:S(2)}) async-start(f32[128,2,128]{2,1,0:T(2,128)} %bitcast.17), calls=%async_computation.2 | async-start | bytes 262144 | tf_op jit(solution)/shard_map/all_to_all | solution.py:388
  134.6 0.6 copy-start.9
